TPU v7x, 32 devices: a whole 2x2x4 slice. The times are simulated.
32 devices in a mesh: groups: 2 (over x), section: 8 (over z, y), tensor: 2 (over core).
Axes of the slice: x: 2, y: 2, z: 4, core: 2. Of those that a mesh axis runs over, the one named last changes fastest.
Arguments:
- tokens: bfloat16 [4096, 8192], P(('groups', 'section'), 'tensor'), parts along dimension 0, may hold values from -6 to 6
- norm_gain: bfloat16 [8192], P('tensor'), may hold values from 0.099609375 to 1.8984375
- kv_weight: bfloat16 [8192, 1024], P('tensor'), may hold values from -0.0625 to 0.0625
- lengths: int32 [16, 8], P(('groups', 'section')), parts along dimension 0, may hold values from 1 to 96, 256 in all within a row
- decode_host: int32 [16, 8], P(('groups', 'section')), parts along dimension 0, may hold values from 0 to 7, as said below
- beam_counts: int32 [16, 8], P(('groups', 'section')), parts along dimension 0, may hold values from 4 to 16, as said below
- beam_query: bfloat16 [1280, 4096], P(('groups', 'section'), 'tensor'), parts along dimension 0, may hold values from -200 to 200
- beam_newkv: bfloat16 [1280, 1024], P(('groups', 'section'), 'tensor'), parts along dimension 0, may hold values from -6 to 6
Outputs:
- context: bfloat16 [1280, 4096], P(('groups', 'section'), 'tensor'), parts along dimension 0
There are 2 independent parts, one for each index of `groups`. A program takes and returns all parts, laid end to end along the dimension named above; an argument that names none is the same for every part. Nothing has to cross between parts.
Inputs may be any that keep to these rules, and one draw needn't show every extreme that they name: `lengths`: each row sums to 256; prompt i of a prefill device fills its token rows right after prompts 0 to i - 1. decode_host[s, i] is the decode device along section that holds the beams of prompt i of prefill device s. The 8 prompts of one prefill device go to different decode devices, and every decode device receives, for each i, the prompt i of exactly one prefill device. beam_counts[d, j] is the number of beams on decode device d for the prompt it receives with index j. Each row sums to 80.
All inputs are finite; a program needn't handle non-finite values.
Results may differ from a plain program's by a relative error of at most 0.012.
The roundings to bfloat16 on the way count: a program that leaves them out, or rounds other values in their place, can miss the bound.
Values may be sent and summed in bfloat16 or wider, within the bound.
No kernel may reach another device: no remote copies, remote signals or barrier semaphores. Data moves between devices by JAX's collectives and lax.ppermute only.
A program may use at most 128 MiB of HBM per device.

v0:
```python
import jax
import jax.numpy as jnp
from jax import lax
from jax.sharding import PartitionSpec as P

D = 8192
QPK = 8
HD = 128
BMAX = 16
MAXLEN = 96


def attend(query, own, cache, valid):
    blocks = query.shape[0]
    width = query.shape[1]
    groups = cache.shape[-1] // (2 * HD)
    query_heads = query.reshape(blocks, width, groups, QPK, HD)
    cache_heads = cache.reshape(blocks, cache.shape[1], groups, 2, HD)
    own_heads = own.reshape(blocks, width, groups, 2, HD)
    scale = HD ** (-0.5)
    scores = (
        jnp.einsum(
            "abgqd,atgd->abgqt",
            query_heads,
            cache_heads[:, :, :, 0],
            preferred_element_type=jnp.float32,
        )
        * scale
    )
    scores = jnp.where(valid[:, None, None, None, :], scores, -jnp.inf)
    own_score = (
        jnp.einsum(
            "abgqd,abgd->abgq",
            query_heads,
            own_heads[:, :, :, 0],
            preferred_element_type=jnp.float32,
        )
        * scale
    )
    top = jnp.maximum(jnp.max(scores, axis=-1), own_score)
    expo = jnp.exp(scores - top[..., None])
    own_expo = jnp.exp(own_score - top)
    total = jnp.sum(expo, axis=-1) + own_expo
    weights = (expo / total[..., None]).astype(jnp.bfloat16)
    own_weight = (own_expo / total).astype(jnp.bfloat16)
    mixed = jnp.einsum(
        "abgqt,atgd->abgqd", weights, cache_heads[:, :, :, 1], preferred_element_type=jnp.float32
    )
    mixed = (
        mixed
        + own_weight.astype(jnp.float32)[..., None]
        * own_heads[:, :, :, 1].astype(jnp.float32)[:, :, :, None, :]
    )
    return mixed.reshape(blocks, width, groups * QPK * HD).astype(jnp.bfloat16)


def sources_from_tags(tag_values, count):
    sections = jnp.arange(tag_values.shape[0], dtype=jnp.int32)
    wanted = jnp.arange(1, count + 1, dtype=jnp.int32)
    hits = tag_values[None, :] == wanted[:, None]
    return jnp.sum(jnp.where(hits, sections[None, :], 0), axis=1)


def per_device(
    tokens, norm_gain, kv_weight, lengths, decode_host, beam_counts, beam_query, beam_newkv
):
    tok_rows = tokens.shape[0]
    prompt_count = lengths.shape[1]
    beam_rows_dev = beam_query.shape[0]
    sections = lax.axis_size("section")
    squares = jnp.sum(jnp.square(tokens.astype(jnp.float32)), axis=1)
    total_squares = lax.psum(squares, "tensor")
    inverse = lax.rsqrt(total_squares / D + 1e-05)
    scaled = (tokens.astype(jnp.float32) * norm_gain.astype(jnp.float32)).astype(jnp.bfloat16)
    partial_value = jnp.dot(scaled, kv_weight, preferred_element_type=jnp.float32)
    own_part = lax.psum_scatter(partial_value, "tensor", scatter_dimension=1, tiled=True)
    prompt_kv = (own_part * inverse[:, None]).astype(jnp.bfloat16)
    prompt_lens = lengths[0]
    prompt_starts = jnp.cumsum(prompt_lens) - prompt_lens
    offsets = jnp.arange(MAXLEN, dtype=jnp.int32)
    row_index = jnp.clip(prompt_starts[:, None] + offsets[None, :], 0, tok_rows - 1)
    live = offsets[None, :] < prompt_lens[:, None]
    padded = prompt_kv[row_index] * live[:, :, None].astype(jnp.bfloat16)
    slot_ids = jnp.arange(prompt_count, dtype=jnp.int32)
    tags = jnp.where(live, slot_ids[:, None] + 1, 0).astype(jnp.bfloat16)
    section_ids = jnp.arange(sections, dtype=jnp.int32)
    chosen = decode_host[0][None, :] == section_ids[:, None]
    which = jnp.sum(jnp.where(chosen, slot_ids[None, :], 0), axis=1)
    present = jnp.any(chosen, axis=1)
    outgoing = padded[which] * present[:, None, None].astype(jnp.bfloat16)
    out_tags = tags[which] * present[:, None].astype(jnp.bfloat16)
    counts = beam_counts[0]
    ends = jnp.cumsum(counts)
    beam_starts = ends - counts
    beam_slots = jnp.arange(BMAX, dtype=jnp.int32)
    beam_rows = jnp.clip(beam_starts[:, None] + beam_slots[None, :], 0, beam_rows_dev - 1)
    query_pad = beam_query[beam_rows]
    own_pad = beam_newkv[beam_rows]
    beam_index = jnp.arange(beam_rows_dev, dtype=jnp.int32)
    beam_slot = jnp.sum((beam_index[:, None] >= ends[None, :]).astype(jnp.int32), axis=1)
    within = beam_index - beam_starts[beam_slot]
    received, received_tags = (
        lax.all_to_all(outgoing, "section", split_axis=0, concat_axis=0, tiled=True),
        lax.all_to_all(out_tags, "section", split_axis=0, concat_axis=0, tiled=True),
    )
    row_tag = jnp.max(received_tags.astype(jnp.float32), axis=1).astype(jnp.int32)
    from_source = sources_from_tags(row_tag, prompt_count)
    cache = received[from_source]
    valid = received_tags[from_source] > 0
    context_pad = attend(query_pad, own_pad, cache, valid)
    return context_pad[beam_slot, within]


def solution(mesh):
    placed = (
        P(("groups", "section"), "tensor"),
        P("tensor"),
        P("tensor", None),
        P(("groups", "section"), None),
        P(("groups", "section"), None),
        P(("groups", "section"), None),
        P(("groups", "section"), "tensor"),
        P(("groups", "section"), "tensor"),
    )
    return jax.shard_map(
        per_device,
        mesh=mesh,
        in_specs=placed,
        out_specs=P(("groups", "section"), "tensor"),
        check_vma=False,
    )
```

profile of v0, /device:TPU:0, one launch (start us, length us, event | category | flops | bytes accessed | tf_op | source)
XLA Modules:
  0.0 83.3 jit_solution(15237862560735438454)
XLA Ops:
  6.5 0.8 select_reduce_fusion.1
  7.4 0.8 fusion.18
  8.2 0.7 select_convert_fusion
  9.6 0.6 copy.31
  10.2 7.3 %all-to-all-start.1 = ((bf16[8,1,96]{2,1,0:T(2,128)(2,1)}), bf16[8,1,96]{2,1,0:T(2,128)(2,1)}, u32[]{:S(2)}, u32[]{:S(2)}) async-start(bf16[8,1,96]{2,1,0:T(2,128)(2,1)} %copy.31), calls=%async_computation.2 | async-start | bytes 8192 | tf_op jit(solution)/shard_map/all_to_all | solution.py:104
  17.5 0.7 convert_element_type.67
  18.2 7.3 %fusion.2 = f32[256,1024]{1,0:T(8,128)} fusion(bf16[4096,1024]{1,0:T(8,128)(2,1)} %param.10, bf16[256,4096]{1,0:T(8,128)(2,1)} %param.8, f32[4096]{0:T(1024)S(1)} %convert_element_type.67), kind=kOutput, calls=%fused_computation.12 | convolution fusion | flops 2150629376 | bytes 11550720 | tf_op jit(solution)/shard_map/dot_general | solution.py:75
  25.9 0.7 reshape.304
  26.7 0.6 copy-done.13
  28.0 0.9 %gather_fusion.5 = bf16[128,2048]{1,0:T(8,128)(2,1)S(1)} fusion(bf16[80,2048]{1,0:T(8,128)(2,1)S(1)} %copy-done, s32[1024]{0:T(1024)S(1)} %pad_clamp_fusion), kind=kCustom, calls=%fused_computation.5 | custom fusion | bytes 1049088 | tf_op jit(solution)/shard_map/gather | solution.py:97
  29.1 1.0 %gather_fusion.6 = bf16[128,512]{1,0:T(8,128)(2,1)S(1)} fusion(bf16[80,512]{1,0:T(8,128)(2,1)S(1)} %copy-done.1, s32[1024]{0:T(1024)} %copy-done.5), kind=kCustom, calls=%fused_computation.6 | custom fusion | bytes 262656 | tf_op jit(solution)/shard_map/gather | solution.py:98
  30.9 2.5 %psum.7 = f32[256]{0:T(256)S(1)} all-reduce(f32[256]{0:T(256)S(1)} %fusion.1), channel_id=1, replica_groups=mesh['groups'=2,'section'=8,'tensor'=2] {'tensor'}, use_global_device_ids=true, to_apply=%region_2.0 | all-reduce | flops 256 | bytes 2048 | tf_op jit(solution)/shard_map/psum | solution.py:72
  33.4 0.7 pad_clamp_fusion.3
  34.0 0.7 convert_reduce_fusion
  34.8 0.7 fusion.19
  36.0 1.1 %multiply_convert_fusion = bf16[256,512]{1,0:T(8,128)(2,1)S(1)} fusion(f32[256,512]{1,0:T(8,128)} %reduce-scatter.2.cloned.1.call-done, f32[256]{0:T(256)S(1)} %add_rsqrt_fusion), kind=kLoop, calls=%fused_computation.25 | loop fusion | flops 262144 | bytes 787456 | tf_op jit(solution)/shard_map/convert_element_type | solution.py:77
  37.1 2.7 %gather_fusion = bf16[768,512]{1,0:T(8,128)(2,1)S(1)} fusion(bf16[256,512]{1,0:T(8,128)(2,1)S(1)} %multiply_convert_fusion, s32[1024]{0:T(1024)S(1)} %pad_clamp_fusion.3), kind=kCustom, calls=%fused_computation | custom fusion | bytes 1575936 | tf_op jit(solution)/shard_map/gather | solution.py:83
  40.0 0.7 gather_fusion.1
  40.7 1.0 %broadcast_multiply_fusion = bf16[8,96,512]{2,1,0:T(8,128)(2,1)} fusion(bf16[8,96,512]{2,1,0:T(8,128)(2,1)S(1)} %gather_fusion.1, bf16[8]{0:T(256)(128)(2,1)S(1)} %copy-done.8), kind=kLoop, calls=%fused_computation.28 | loop fusion | flops 393216 | bytes 1572880 | tf_op jit(solution)/shard_map/mul | solution.py:90
  41.8 6.0 %all-to-all-start = ((bf16[8,96,512]{2,1,0:T(8,128)(2,1)}), bf16[8,96,512]{2,1,0:T(8,128)(2,1)S(1)}, u32[]{:S(2)}, u32[]{:S(2)}) async-start(bf16[8,96,512]{2,1,0:T(8,128)(2,1)} %broadcast_multiply_fusion), calls=%async_computation.1 | async-start | bytes 1572864 | tf_op jit(solution)/shard_map/all_to_all | solution.py:103
  47.7 0.7 fusion.31
  48.5 5.0 %fusion.28 = s32[80]{0:T(128)S(1)} fusion(s32[80]{0:T(128)S(1)} %convert_reduce_fusion, s32[]{:T(128)} %bitcast.28, s32[]{:T(128)} %bitcast.29, s32[]{:T(128)} %bitcast.30, s32[]{:T(128)} %bitcast.31, s32[]{:T(128)} %bitcast.32, s32[]{:T(128)} %bitcast.34, s32[]{:T(128)} %bitcast.33, s32[]{:T(128)} %bitcast.27), kind=kLoop, calls=%fused_computation.81 | loop fusion | flops 2080 | bytes 672 | tf_op jit(solution)/shard_map/concatenate | solution.py:111
  53.5 0.7 copy.66
  54.2 0.8 reduce_max.23
  55.2 0.6 gather_fusion.4
  55.8 12.4 %all-to-all-done = bf16[8,96,512]{2,1,0:T(8,128)(2,1)S(1)} async-done(((bf16[8,96,512]{2,1,0:T(8,128)(2,1)}), bf16[8,96,512]{2,1,0:T(8,128)(2,1)S(1)}, u32[]{:S(2)}, u32[]{:S(2)}) %all-to-all-start) | async-done | bytes 786464 | tf_op jit(solution)/shard_map/all_to_all | solution.py:103
  68.2 0.6 gather_fusion.3
  69.0 1.1 %fusion.29 = (bf16[8,96,2,1,128]{4,3,2,1,0:T(2,128)(2,1)S(1)}, bf16[8,96,2,1,128]{4,3,2,1,0:T(2,128)(2,1)S(1)}) fusion(bf16[8,96,2,2,128]{4,3,2,1,0:T(2,128)(2,1)S(1)} %reshape.295), kind=kLoop, calls=%fused_computation.84 | loop fusion | bytes 1572864 | tf_op jit(solution)/shard_map/slice | solution.py:47
  70.1 0.6 fusion.32
  70.7 0.7 fusion.9
  71.4 1.1 %fusion.8 = bf16[8,16,2,8,128]{4,1,3,2,0:T(8,128)(2,1)S(1)} fusion(f32[8,16,2,128]{3,1,2,0:T(8,128)S(1)} %fusion.14, f32[8,16,2,8]{1,3,2,0:T(8,128)S(1)} %get-tuple-element.8, f32[8,16,2,8,96]{4,1,3,2,0:T(8,128)S(1)} %get-tuple-element.20, f32[8,16,2,8]{1,3,2,0:T(8,128)S(1)} %get-tuple-element.7, f32[8,16,2,8]{1,3,2,0:T(8,128)S(1)} %fusion.15, ...), kind=kOutput, calls=%fused_computation.19 | convolution fusion | flops 51707904 | bytes 1859584 | tf_op jit(solution)/shard_map/abgqt,atgd->abgqd/dot_general | solution.py:46
  72.9 3.5 %gather_fusion.7 = bf16[80,2048]{1,0:T(8,128)(2,1)} fusion(bf16[8,16,2048]{2,1,0:T(8,128)(2,1)S(1)} %convert_element_type.78, s32[80]{0:T(128)S(1)} %fusion.28), kind=kCustom, calls=%fused_computation.7 | custom fusion | bytes 656000 | tf_op jit(solution)/shard_map/gather | solution.py:111
  (65 shorter events, 4.3 us)
Async XLA Ops:
  6.5 21.5 %copy-start = (bf16[80,2048]{1,0:T(8,128)(2,1)S(1)}, bf16[80,2048]{1,0:T(8,128)(2,1)}, u32[]{:S(2)}) copy-start(bf16[80,2048]{1,0:T(8,128)(2,1)} %param.14) | copy-start | bytes 983044
  6.5 1.6 %copy-start.10 = (s32[8]{0:T(128)}, s32[8]{0:T(128)S(1)}, u32[]{:S(2)}) copy-start(s32[8]{0:T(128)S(1)} %iota_add_fusion) | copy-start | bytes 100
  8.2 10.0 %copy-start.6 = (s32[1024]{0:T(1024)}, s32[1024]{0:T(1024)S(1)}, u32[]{:S(2)}) copy-start(s32[1024]{0:T(1024)S(1)} %pad_clamp_fusion.2) | copy-start | bytes 12292
  8.2 10.0 %copy-start.7 = (bf16[8]{0:T(256)(128)(2,1)}, bf16[8]{0:T(256)(128)(2,1)S(1)}, u32[]{:S(2)}) copy-start(bf16[8]{0:T(256)(128)(2,1)S(1)} %convert_element_type.71) | copy-start | bytes 52
  10.2 31.6 %all-to-all-start.1 = ((bf16[8,1,96]{2,1,0:T(2,128)(2,1)}), bf16[8,1,96]{2,1,0:T(2,128)(2,1)}, u32[]{:S(2)}, u32[]{:S(2)}) async-start(bf16[8,1,96]{2,1,0:T(2,128)(2,1)} %copy.31), calls=%async_computation.2 | async-start | bytes 8192 | tf_op jit(solution)/shard_map/all_to_all | solution.py:104
  17.4 18.5 %reduce-scatter.2.cloned.1.call-start = ((), (), s32[]{:S(2)}) async-start(), calls=%async_computation.3 | async-start | bytes 1572864 | tf_op jit(solution)/shard_map/reduce_scatter | solution.py:76
  18.2 7.4 %copy-start.9 = (s32[1,8]{1,0:T(1,128)S(1)}, s32[1,8]{1,0:T(1,128)}, u32[]{:S(2)}) copy-start(s32[1,8]{1,0:T(1,128)} %param.11) | copy-start | bytes 100
  18.2 8.3 %copy-start.12 = (s32[1,8]{1,0:T(1,128)S(1)}, s32[1,8]{1,0:T(1,128)}, u32[]{:S(2)}) copy-start(s32[1,8]{1,0:T(1,128)} %param.13) | copy-start | bytes 100
  25.6 3.5 %copy-start.1 = (bf16[80,512]{1,0:T(8,128)(2,1)S(1)}, bf16[80,512]{1,0:T(8,128)(2,1)}, u32[]{:S(2)}) copy-start(bf16[80,512]{1,0:T(8,128)(2,1)} %param.15) | copy-start | bytes 245764
  25.6 4.8 %copy-start.2 = (bf16[256,4096]{1,0:T(8,128)(2,1)S(1)}, bf16[256,4096]{1,0:T(8,128)(2,1)}, u32[]{:S(2)}) copy-start(bf16[256,4096]{1,0:T(8,128)(2,1)} %param.8) | copy-start | bytes 6291460
  26.7 0.6 copy-start.13
  27.3 0.5 copy-start.3
  28.0 1.0 %copy-start.5 = (s32[1024]{0:T(1024)}, s32[1024]{0:T(1024)S(1)}, u32[]{:S(2)}) copy-start(s32[1024]{0:T(1024)S(1)} %pad_clamp_fusion) | copy-start | bytes 12292
  37.1 3.6 %copy-start.8 = (bf16[8]{0:T(256)(128)(2,1)S(1)}, bf16[8]{0:T(256)(128)(2,1)}, u32[]{:S(2)}) copy-start(bf16[8]{0:T(256)(128)(2,1)} %copy-done.7) | copy-start | bytes 52
  39.8 7.9 %copy-start.4 = (s32[8]{0:T(128)S(1)}, s32[8]{0:T(128)}, u32[]{:S(2)}) copy-start(s32[8]{0:T(128)} %copy-done.3) | copy-start | bytes 100
  39.8 15.2 %copy-start.11 = (s32[8]{0:T(128)S(1)}, s32[8]{0:T(128)}, u32[]{:S(2)}) copy-start(s32[8]{0:T(128)} %copy-done.10) | copy-start | bytes 100
  41.8 26.4 %all-to-all-start = ((bf16[8,96,512]{2,1,0:T(8,128)(2,1)}), bf16[8,96,512]{2,1,0:T(8,128)(2,1)S(1)}, u32[]{:S(2)}, u32[]{:S(2)}) async-start(bf16[8,96,512]{2,1,0:T(8,128)(2,1)} %broadcast_multiply_fusion), calls=%async_computation.1 | async-start | bytes 1572864 | tf_op jit(solution)/shard_map/all_to_all | solution.py:103
Sparse Core Ops, SparseCore 0:
  25.7 9.8 reduce-scatter.1
where the time goes:
time: 83.8 us; the launch traced here: 83.3 us
  local copies, waits for them, and re-layouts  16.6 us (20%)
  other arithmetic  15.4 us (18%)
  between operations  13.7 us (16%)
  starting transfers between devices  13.3 us (16%)
  waiting for transfers between devices  12.4 us (15%)
  matrix products  9.43 us (11%)
  blocking collectives  2.46 us (3%)
    all_to_all x1, waiting for transfers between devices, per_device(): lax.all_to_all(outgoing, 'section', split_axis=0, concat_axis=0, tiled=True)  12.4 us
    dot_general x1, matrix products, per_device(): jnp.dot(scaled, kv_weight, preferred_element_type=jnp.float32)  7.35 us
    all_to_all x1, starting transfers between devices, per_device(): lax.all_to_all(out_tags, 'section', split_axis=0, concat_axis=0, tiled=True)  7.28 us
    all_to_all x1, starting transfers between devices, per_device(): lax.all_to_all(outgoing, 'section', split_axis=0, concat_axis=0, tiled=True)  5.96 us
    concatenate x1, other arithmetic, per_device(): return context_pad[beam_slot, within]  5.01 us
    gather x1, local copies, waits for them, and re-layouts, per_device(): return context_pad[beam_slot, within]  3.54 us
    gather x1, local copies, waits for them, and re-layouts, per_device(): padded = prompt_kv[row_index] * live[:, :, None].astype(jnp.bfloat16)  2.68 us
    psum x1, blocking collectives, per_device(): total_squares = lax.psum(squares, 'tensor')  2.46 us
  transfers between devices with their start and end apart: 3, of which 1 were waited for; matrix products, arithmetic and copies ran while one was open for 34% of the time, Pallas kernels for 0%

commit v1 on v0

v1 whole, which is shorter than its diff:
```python
import functools

import jax
import jax.numpy as jnp
from jax import lax
from jax.experimental import pallas as pl
from jax.experimental.pallas import tpu as pltpu
from jax.sharding import PartitionSpec as P

D = 8192
QPK = 8
HD = 128
BMAX = 16
MAXLEN = 96
META = 16
PACK = 8
STEP = 512
VMEM_LIMIT = 48 * 1024 * 1024


def project_kernel(half, tok_ref, gain_ref, w_ref, out_ref, *, with_squares):
    first = pl.program_id(0) == 0
    width = w_ref.shape[1]
    tok = tok_ref[...].astype(jnp.float32)
    scaled = (tok * gain_ref[...].astype(jnp.float32)).astype(jnp.bfloat16)
    part = jnp.dot(scaled, w_ref[...], preferred_element_type=jnp.float32)
    if with_squares:
        sq = tok * tok
        lanes = sq[:, :HD]
        for c in range(HD, sq.shape[1], HD):
            lanes = lanes + sq[:, c : c + HD]

    @pl.when(first)
    def _():
        out_ref[:, :width] = part
        if with_squares:
            out_ref[:, width:] = lanes

    @pl.when(jnp.logical_not(first))
    def _():
        out_ref[:, :width] += part
        if with_squares:
            out_ref[:, width:] += lanes


def project(half, tokens, gain, weight, with_squares):
    rows, depth = tokens.shape
    width = weight.shape[1] // 2
    out_width = width + (HD if with_squares else 0)
    return pl.pallas_call(
        functools.partial(project_kernel, with_squares=with_squares),
        out_shape=jax.ShapeDtypeStruct((rows, out_width), jnp.float32),
        grid_spec=pltpu.PrefetchScalarGridSpec(
            num_scalar_prefetch=1,
            grid=(depth // STEP,),
            in_specs=[
                pl.BlockSpec((rows, STEP), lambda k, half: (0, k)),
                pl.BlockSpec((1, STEP), lambda k, half: (0, k)),
                pl.BlockSpec((STEP, width), lambda k, half: (k, half[0])),
            ],
            out_specs=pl.BlockSpec((rows, out_width), lambda k, half: (0, 0)),
        ),
        compiler_params=pltpu.CompilerParams(vmem_limit_bytes=VMEM_LIMIT),
        cost_estimate=pl.CostEstimate(
            flops=2 * rows * depth * width,
            bytes_accessed=2 * depth * (rows + width) + 4 * rows * out_width,
            transcendentals=0,
        ),
        name="project",
    )(half, tokens, gain, weight)


def pack_kernel(keep_ref, recv_ref, sq_ref, len_ref, host_ref, out_ref):
    rows, width = keep_ref.shape
    prompts = len_ref.shape[1]
    squares = jnp.sum(recv_ref[:, width:] + sq_ref[...], axis=1, keepdims=True)
    inverse = lax.rsqrt(squares / D + 1e-05)
    kv = ((keep_ref[...] + recv_ref[:, :width]) * inverse).astype(jnp.bfloat16)
    lane = lax.broadcasted_iota(jnp.int32, (META, HD), 1)
    row_at = lax.broadcasted_iota(jnp.int32, (MAXLEN, rows), 1)
    row_at = row_at - lax.broadcasted_iota(jnp.int32, (MAXLEN, rows), 0)

    def place(chunk, start):
        picks = []
        for i in range(PACK):
            picks.append((row_at == start).astype(jnp.float32).astype(jnp.bfloat16))
            start = start + len_ref[0, chunk * PACK + i]
        blocks = jnp.dot(
            jnp.concatenate(picks, axis=0), kv, preferred_element_type=jnp.float32
        ).astype(jnp.bfloat16)
        for i in range(PACK):
            slot = chunk * PACK + i
            dest = host_ref[0, slot]
            for g in range(width // HD):
                out_ref[dest, g * MAXLEN : (g + 1) * MAXLEN, :] = blocks[
                    i * MAXLEN : (i + 1) * MAXLEN, g * HD : (g + 1) * HD
                ]
            meta = jnp.where(lane == 0, slot, jnp.where(lane == 1, len_ref[0, slot], 0))
            out_ref[dest, width // HD * MAXLEN :, :] = meta.astype(jnp.float32).astype(jnp.bfloat16)
        return start

    if prompts == PACK:
        place(0, 0)
    else:
        lax.fori_loop(0, prompts // PACK, place, jnp.int32(0))


def pack(keep, recv, send, lengths, decode_host, sections):
    rows, width = keep.shape
    height = width // HD * MAXLEN + META
    smem = pl.BlockSpec(memory_space=pltpu.SMEM)
    return pl.pallas_call(
        pack_kernel,
        out_shape=jax.ShapeDtypeStruct((sections, height, HD), jnp.bfloat16),
        grid=(1,),
        in_specs=[
            pl.BlockSpec((rows, width), lambda i: (0, 0)),
            pl.BlockSpec((rows, width + HD), lambda i: (0, 0)),
            pl.BlockSpec((rows, HD), lambda i: (0, width // HD)),
            smem,
            smem,
        ],
        out_specs=pl.BlockSpec((sections, height, HD), lambda i: (0, 0, 0)),
        compiler_params=pltpu.CompilerParams(vmem_limit_bytes=VMEM_LIMIT),
        name="pack",
    )(keep, recv, send, lengths, decode_host)


def attend_kernel(got_ref, query_ref, own_ref, count_ref, out_ref, q_ref, own32_ref, o_ref, src_ref, len_ref):
    sections = got_ref.shape[0]
    beams = query_ref.shape[0]
    heads = query_ref.shape[1] // HD
    groups = heads // QPK
    base = 2 * groups * MAXLEN
    scale = HD ** (-0.5)
    tail = jnp.zeros((BMAX, HD), jnp.float32)
    for h in range(heads):
        q_ref[h, :beams, :] = query_ref[:, h * HD : (h + 1) * HD].astype(jnp.float32)
        q_ref[h, beams:, :] = tail
    for g in range(2 * groups):
        own32_ref[g, :beams, :] = own_ref[:, g * HD : (g + 1) * HD].astype(jnp.float32)
        own32_ref[g, beams:, :] = tail
    for s in range(sections):
        meta = got_ref[s, base : base + META, :].astype(jnp.float32)
        slot = meta[0, 0].astype(jnp.int32)
        src_ref[slot] = s
        len_ref[slot] = meta[0, 1].astype(jnp.int32)
    lane = lax.broadcasted_iota(jnp.int32, (QPK * BMAX, MAXLEN), 1)

    def prompt(j, start):
        source = src_ref[j]
        live = lane < len_ref[j]
        at = pl.ds(start, BMAX)
        for g in range(groups):
            keys = got_ref[source, 2 * g * MAXLEN : (2 * g + 1) * MAXLEN, :]
            values = got_ref[source, (2 * g + 1) * MAXLEN : (2 * g + 2) * MAXLEN, :]
            q3 = q_ref[g * QPK : (g + 1) * QPK, at, :]
            own_key = own32_ref[2 * g, at, :]
            own_value = own32_ref[2 * g + 1, at, :]
            own_score = jnp.sum(q3 * own_key[None], axis=2, keepdims=True) * scale
            own_score = own_score.reshape(QPK * BMAX, 1)
            q2 = q3.reshape(QPK * BMAX, HD).astype(jnp.bfloat16)
            scores = lax.dot_general(
                q2, keys, (((1,), (1,)), ((), ())), preferred_element_type=jnp.float32
            )
            scores = jnp.where(live, scores * scale, -jnp.inf)
            top = jnp.maximum(jnp.max(scores, axis=1, keepdims=True), own_score)
            expo = jnp.exp(scores - top)
            own_expo = jnp.exp(own_score - top)
            total = jnp.sum(expo, axis=1, keepdims=True) + own_expo
            weights = (expo / total).astype(jnp.bfloat16)
            own_weight = (own_expo / total).astype(jnp.bfloat16).astype(jnp.float32)
            mixed = jnp.dot(weights, values, preferred_element_type=jnp.float32)
            mixed = mixed.reshape(QPK, BMAX, HD)
            mixed = mixed + own_weight.reshape(QPK, BMAX, 1) * own_value[None]
            o_ref[g * QPK : (g + 1) * QPK, at, :] = mixed
        return start + count_ref[0, j]

    if sections <= 8:
        start = 0
        for j in range(sections):
            start = prompt(j, start)
    else:
        lax.fori_loop(0, sections, prompt, jnp.int32(0))
    for h in range(heads):
        out_ref[:, h * HD : (h + 1) * HD] = o_ref[h, :beams, :].astype(jnp.bfloat16)


def attend(got, query, own, counts):
    sections, height, _ = got.shape
    beams, width = query.shape
    heads = width // HD
    return pl.pallas_call(
        attend_kernel,
        out_shape=jax.ShapeDtypeStruct((beams, width), jnp.bfloat16),
        in_specs=[
            pl.BlockSpec(memory_space=pltpu.VMEM),
            pl.BlockSpec(memory_space=pltpu.VMEM),
            pl.BlockSpec(memory_space=pltpu.VMEM),
            pl.BlockSpec(memory_space=pltpu.SMEM),
        ],
        out_specs=pl.BlockSpec(memory_space=pltpu.VMEM),
        scratch_shapes=[
            pltpu.VMEM((heads, beams + BMAX, HD), jnp.float32),
            pltpu.VMEM((own.shape[1] // HD, beams + BMAX, HD), jnp.float32),
            pltpu.VMEM((heads, beams + BMAX, HD), jnp.float32),
            pltpu.SMEM((sections,), jnp.int32),
            pltpu.SMEM((sections,), jnp.int32),
        ],
        compiler_params=pltpu.CompilerParams(vmem_limit_bytes=VMEM_LIMIT),
        name="attend",
    )(got, query, own, counts)


def per_device(tokens, norm_gain, kv_weight, lengths, decode_host, beam_counts, beam_query, beam_newkv):
    sections = lax.axis_size("section")
    mine = lax.axis_index("tensor").astype(jnp.int32).reshape(1)
    gain = norm_gain.reshape(1, -1)
    send = project(1 - mine, tokens, gain, kv_weight, True)
    recv = lax.ppermute(send, "tensor", [(0, 1), (1, 0)])
    keep = project(mine, tokens, gain, kv_weight, False)
    outgoing = pack(keep, recv, send, lengths, decode_host, sections)
    got = lax.all_to_all(outgoing, "section", split_axis=0, concat_axis=0, tiled=True)
    return attend(got, beam_query, beam_newkv, beam_counts)


def solution(mesh):
    rows = ("groups", "section")
    placed = (
        P(rows, "tensor"),
        P("tensor"),
        P("tensor", None),
        P(rows, None),
        P(rows, None),
        P(rows, None),
        P(rows, "tensor"),
        P(rows, "tensor"),
    )
    return jax.shard_map(
        per_device,
        mesh=mesh,
        in_specs=placed,
        out_specs=P(rows, "tensor"),
        check_vma=False,
    )
```

time: 83.8 us -> 52.2 us (0.62)
  blocking collectives: 2.46 us -> 28.9 us
  Pallas kernels: 0 us -> 19.9 us
  other arithmetic: 15.4 us -> 0 us
  local copies, waits for them, and re-layouts: 16.6 us -> 2.32 us
  between operations: 13.7 us -> 0.09 us
  starting transfers between devices: 13.3 us -> 0.52 us
  waiting for transfers between devices: 12.4 us -> 0.01 us
  matrix products: 9.43 us -> 0 us
    all_to_all x0 -> x1, blocking collectives: none -> 28.9 us  [per_device(): lax.all_to_all(outgoing, 'section', split_axis=0, concat_axis=0, tiled=True)]
    pallas_call x0 -> x4, Pallas kernels: none -> 19.9 us  [the longest x2 12.6 us: project(): pl.pallas_call(functools.partial(project_kernel, with_squares=with_square...]
    all_to_all x2 -> x0, starting transfers between devices: 13.2 us -> none  [the longest x1 7.28 us: per_device(): lax.all_to_all(out_tags, 'section', split_axis=0, concat_axis=0, tiled=True)]
    all_to_all x2 -> x0, waiting for transfers between devices: 12.4 us -> none  [the longest x1 12.4 us: per_device(): lax.all_to_all(outgoing, 'section', split_axis=0, concat_axis=0, tiled=True)]
    gather x9 -> x0, local copies, waits for them, and re-layouts: 11.2 us -> none  [the longest x1 3.54 us: per_device(): return context_pad[beam_slot, within]]
    dot_general x4 -> x0, matrix products: 9.43 us -> none  [the longest x1 7.35 us: per_device(): jnp.dot(scaled, kv_weight, preferred_element_type=jnp.float32)]
    concatenate x1 -> x0, other arithmetic: 5.01 us -> none  [per_device(): return context_pad[beam_slot, within]]
    convert_element_type x6 -> x0, other arithmetic: 3.32 us -> none  [the longest x1 1.14 us: per_device(): prompt_kv = (own_part * inverse[:, None]).astype(jnp.bfloat16)]
  transfers between devices with their start and end apart: 3 -> 1, of which waited for: 1 -> 0; matrix products, arithmetic and copies ran while one was open for 34% -> 0% of each run, Pallas kernels for 0% -> 12%
where the time goes in v1:
time: 52.2 us; the launch traced here: 51.8 us
  blocking collectives  28.9 us (55%)
  Pallas kernels  19.9 us (38%)
  local copies, waits for them, and re-layouts  2.32 us (4%)
    all_to_all x1, blocking collectives, per_device(): lax.all_to_all(outgoing, 'section', split_axis=0, concat_axis=0, tiled=True)  28.9 us
    pallas_call x2, Pallas kernels, project(): pl.pallas_call(functools.partial(project_kernel, with_squares=with_square...  12.6 us
    pallas_call x1, Pallas kernels, attend(): pl.pallas_call(attend_kernel, out_shape=jax.ShapeDtypeStruct((beams, widt...  6.32 us
    unnamed x14, local copies, waits for them, and re-layouts  1.62 us
  transfers between devices with their start and end apart: 1, of which 0 were waited for; matrix products, arithmetic and copies ran while one was open for 0% of the time, Pallas kernels for 12%

profile of v1, /device:TPU:0, one launch (start us, length us, event | category | flops | bytes accessed | tf_op | source)
XLA Modules:
  0.0 51.8 jit_solution(8961826735695939680)
XLA Ops:
  0.0 0.7 %reshape.7.gain_ref = bf16[1,4096]{1,0:T(2,128)(2,1)S(1)} reshape(bf16[4096]{0:T(1024)(128)(2,1)} %param.9) | data formatting | bytes 16384 | tf_op jit(solution)/shard_map/reshape | solution.py:218
  0.7 0.0 copy-start
  0.7 1.6 %copy-done = bf16[256,4096]{1,0:T(8,128)(2,1)S(1)} copy-done((bf16[256,4096]{1,0:T(8,128)(2,1)S(1)}, bf16[256,4096]{1,0:T(8,128)(2,1)}, u32[]{:S(2)}) %copy-start) | copy-done | bytes 2097176
  2.3 0.0 copy-start.1
  2.3 0.0 copy-start.4
  2.3 0.0 copy-start.5
  2.3 6.4 %project.3.sq_ref = f32[256,640]{1,0:T(8,128)S(1)} custom-call(s32[1]{0:T(128)S(6)} %sub.3.half, bf16[256,4096]{1,0:T(8,128)(2,1)S(1)} %copy-done, bf16[1,4096]{1,0:T(2,128)(2,1)S(1)} %reshape.7.gain_ref, bf16[4096,1024]{1,0:T(8,128)(2,1)} %w_ref.3), custom_call_target="tpu_custom_call" | custom-call | flops 1073741824 | bytes 6946816 | tf_op jit(solution)/shard_map/project/pallas_call | solution.py:50
  8.8 0.0 copy-start.2
  8.8 0.0 copy-start.3
  8.8 0.0 copy-start.6
  8.8 0.5 collective-permute-start
  9.3 0.0 copy-done.1
  9.3 6.2 %project.2.keep_ref = f32[256,512]{1,0:T(8,128)S(1)} custom-call(s32[1]{0:T(128)} %bitcast.half, bf16[256,4096]{1,0:T(8,128)(2,1)S(1)} %copy-done.1, bf16[1,4096]{1,0:T(2,128)(2,1)S(1)} %reshape.7.gain_ref, bf16[4096,1024]{1,0:T(8,128)(2,1)} %w_ref.3), custom_call_target="tpu_custom_call" | custom-call | flops 1073741824 | bytes 6815744 | tf_op jit(solution)/shard_map/project/pallas_call | solution.py:50
  15.5 0.0 collective-permute-done.recv_ref
  15.5 0.0 copy-done.4
  15.5 0.0 copy-done.5
  15.5 1.0 %pack.1 = bf16[8,400,128]{2,1,0:T(8,128)(2,1)S(1)} custom-call(f32[256,512]{1,0:T(8,128)S(1)} %project.2.keep_ref, f32[256,640]{1,0:T(8,128)S(1)} %collective-permute-done.recv_ref, f32[256,640]{1,0:T(8,128)S(1)} %project.3.sq_ref, s32[1,8]{1,0:T(1,128)S(1)} %copy-done.4, s32[1,8]{1,0:T(1,128)S(1)} %copy-done.5), custom_call_target="tpu_custom_call" | custom-call | tf_op jit(solution)/shard_map/pack/pallas_call | solution.py:112
  16.5 28.9 %all_to_all.5.got_ref = bf16[8,400,128]{2,1,0:T(8,128)(2,1)S(1)} all-to-all(bf16[8,400,128]{2,1,0:T(8,128)(2,1)S(1)} %pack.1), channel_id=1, replica_groups=mesh['groups'=2,'section'=8,'tensor'=2] {'section'}, dimensions={0} | all-to-all | bytes 1638400 | tf_op jit(solution)/shard_map/all_to_all | solution.py:223
  45.4 0.0 copy-done.2
  45.4 0.0 copy-done.3
  45.4 0.0 copy-done.6
  45.4 6.3 %attend.1 = bf16[80,2048]{1,0:T(8,128)(2,1)} custom-call(bf16[8,400,128]{2,1,0:T(8,128)(2,1)S(1)} %all_to_all.5.got_ref, bf16[80,2048]{1,0:T(8,128)(2,1)S(1)} %copy-done.2, bf16[80,512]{1,0:T(8,128)(2,1)S(1)} %copy-done.3, s32[1,8]{1,0:T(1,128)S(1)} %copy-done.6), custom_call_target="tpu_custom_call" | custom-call | tf_op jit(solution)/shard_map/attend/pallas_call | solution.py:193
Async XLA Ops:
  0.7 1.6 %copy-start = (bf16[256,4096]{1,0:T(8,128)(2,1)S(1)}, bf16[256,4096]{1,0:T(8,128)(2,1)}, u32[]{:S(2)}) copy-start(bf16[256,4096]{1,0:T(8,128)(2,1)} %tok_ref.3) | copy-start | bytes 6291460
  2.3 7.0 %copy-start.1 = (bf16[256,4096]{1,0:T(8,128)(2,1)S(1)}, bf16[256,4096]{1,0:T(8,128)(2,1)}, u32[]{:S(2)}) copy-start(bf16[256,4096]{1,0:T(8,128)(2,1)} %tok_ref.3) | copy-start | bytes 6291460
  2.3 13.2 %copy-start.4 = (s32[1,8]{1,0:T(1,128)S(1)}, s32[1,8]{1,0:T(1,128)}, u32[]{:S(2)}) copy-start(s32[1,8]{1,0:T(1,128)} %len_ref.1) | copy-start | bytes 100
  2.3 13.2 %copy-start.5 = (s32[1,8]{1,0:T(1,128)S(1)}, s32[1,8]{1,0:T(1,128)}, u32[]{:S(2)}) copy-start(s32[1,8]{1,0:T(1,128)} %host_ref.1) | copy-start | bytes 100
  8.8 36.7 %copy-start.2 = (bf16[80,2048]{1,0:T(8,128)(2,1)S(1)}, bf16[80,2048]{1,0:T(8,128)(2,1)}, u32[]{:S(2)}) copy-start(bf16[80,2048]{1,0:T(8,128)(2,1)} %query_ref.1) | copy-start | bytes 983044
  8.8 36.7 %copy-start.3 = (bf16[80,512]{1,0:T(8,128)(2,1)S(1)}, bf16[80,512]{1,0:T(8,128)(2,1)}, u32[]{:S(2)}) copy-start(bf16[80,512]{1,0:T(8,128)(2,1)} %own_ref.1) | copy-start | bytes 245764
  8.8 36.6 %copy-start.6 = (s32[1,8]{1,0:T(1,128)S(1)}, s32[1,8]{1,0:T(1,128)}, u32[]{:S(2)}) copy-start(s32[1,8]{1,0:T(1,128)} %count_ref.1) | copy-start | bytes 100
  8.8 6.7 %collective-permute-start = (f32[256,640]{1,0:T(8,128)S(1)}, f32[256,640]{1,0:T(8,128)S(1)}, u32[]{:S(2)}, u32[]{:S(2)}) collective-permute-start(f32[256,640]{1,0:T(8,128)S(1)} %project.3.sq_ref), channel_id=1, source_target_pairs={{0,1},{1,0},{2,3},{3,2},{4,5},{5,4},{6,7},{7,6},{8,9},{9,8},{10,11... | collective-permute-start | bytes 1966088 | tf_op jit(solution)/shard_map/ppermute | solution.py:220

commit v2 on v0

v2 whole, which is shorter than its diff:
```python
import functools

import jax
import jax.numpy as jnp
from jax import lax
from jax.experimental import pallas as pl
from jax.experimental.pallas import tpu as pltpu
from jax.sharding import PartitionSpec as P

D = 8192
QPK = 8
HD = 128
BMAX = 16
MAXLEN = 96
META = 16
STEP = 512
GROUP = 8
VMEM_LIMIT = 44 * 1024 * 1024

VMEM = pl.BlockSpec(memory_space=pltpu.VMEM)
SMEM = pl.BlockSpec(memory_space=pltpu.SMEM)
HBM = pl.BlockSpec(memory_space=pltpu.HBM)


def weight_copy(w_ref, w_buf, sem, half, c):
    width = w_buf.shape[2]
    columns = pl.ds(pl.multiple_of(half * width, width), width)
    return pltpu.make_async_copy(w_ref.at[pl.ds(c * STEP, STEP), columns], w_buf.at[c], sem.at[c])


def project_send_kernel(half_ref, tok_ref, gain_ref, w_ref, out_ref, scaled_ref, tok_buf, w_buf, tok_sem, w_sem):
    half = half_ref[0]
    steps = w_buf.shape[0]
    width = w_buf.shape[2]

    def token_copy(c):
        return pltpu.make_async_copy(tok_ref.at[:, pl.ds(c * STEP, STEP)], tok_buf.at[c], tok_sem.at[c])

    for c in range(steps):
        token_copy(c).start()
        weight_copy(w_ref, w_buf, w_sem, half, c).start()
    gain = gain_ref[...].astype(jnp.float32)
    for c in range(steps):
        token_copy(c).wait()
        for b in range(STEP // HD):
            at = c * (STEP // HD) + b
            tok = tok_buf[c, :, b * HD : (b + 1) * HD].astype(jnp.float32)
            scaled_ref[:, at * HD : (at + 1) * HD] = (tok * gain[at : at + 1, :]).astype(jnp.bfloat16)
            if at == 0:
                out_ref[:, width:] = tok * tok
            else:
                out_ref[:, width:] += tok * tok
        weight_copy(w_ref, w_buf, w_sem, half, c).wait()
        part = jnp.dot(
            scaled_ref[:, c * STEP : (c + 1) * STEP], w_buf[c], preferred_element_type=jnp.float32
        )
        if c == 0:
            out_ref[:, :width] = part
        else:
            out_ref[:, :width] += part


def project_keep_kernel(half_ref, scaled_ref, w_ref, out_ref, w_buf, w_sem):
    half = half_ref[0]
    steps = w_buf.shape[0]
    for c in range(steps):
        weight_copy(w_ref, w_buf, w_sem, half, c).start()
    for c in range(steps):
        weight_copy(w_ref, w_buf, w_sem, half, c).wait()
        part = jnp.dot(
            scaled_ref[:, c * STEP : (c + 1) * STEP], w_buf[c], preferred_element_type=jnp.float32
        )
        if c == 0:
            out_ref[...] = part
        else:
            out_ref[...] += part


def project_cost(rows, depth, width):
    return pl.CostEstimate(
        flops=2 * rows * depth * width,
        bytes_accessed=2 * depth * (rows + width) + 4 * rows * width,
        transcendentals=0,
    )


def project_send(half, tokens, gain, weight):
    rows, depth = tokens.shape
    width = weight.shape[1] // 2
    steps = depth // STEP
    return pl.pallas_call(
        project_send_kernel,
        out_shape=(
            jax.ShapeDtypeStruct((rows, width + HD), jnp.float32),
            jax.ShapeDtypeStruct((rows, depth), jnp.bfloat16),
        ),
        in_specs=[SMEM, HBM, VMEM, HBM],
        out_specs=(VMEM, VMEM),
        scratch_shapes=[
            pltpu.VMEM((steps, rows, STEP), jnp.bfloat16),
            pltpu.VMEM((steps, STEP, width), jnp.bfloat16),
            pltpu.SemaphoreType.DMA((steps,)),
            pltpu.SemaphoreType.DMA((steps,)),
        ],
        compiler_params=pltpu.CompilerParams(vmem_limit_bytes=VMEM_LIMIT),
        cost_estimate=project_cost(rows, depth, width),
        name="project_send",
    )(half, tokens, gain, weight)


def project_keep(half, scaled, weight):
    rows, depth = scaled.shape
    width = weight.shape[1] // 2
    steps = depth // STEP
    return pl.pallas_call(
        project_keep_kernel,
        out_shape=jax.ShapeDtypeStruct((rows, width), jnp.float32),
        in_specs=[SMEM, VMEM, HBM],
        out_specs=VMEM,
        scratch_shapes=[
            pltpu.VMEM((steps, STEP, width), jnp.bfloat16),
            pltpu.SemaphoreType.DMA((steps,)),
        ],
        compiler_params=pltpu.CompilerParams(vmem_limit_bytes=VMEM_LIMIT),
        cost_estimate=project_cost(rows, depth, width),
        name="project_keep",
    )(half, scaled, weight)


def pack_kernel(me_ref, keep_ref, recv_ref, send_ref, len_ref, host_ref, *refs):
    outs, slot_ref, start_ref = refs[:-2], refs[-2], refs[-1]
    rows, width = keep_ref.shape
    prompts = len_ref.shape[1]
    me = me_ref[0]
    start = 0
    for i in range(prompts):
        turn = host_ref[0, i] ^ me
        slot_ref[turn] = i
        start_ref[turn] = start
        start = start + len_ref[0, i]
    squares = jnp.sum(recv_ref[:, width:] + send_ref[:, width:], axis=1, keepdims=True)
    inverse = lax.rsqrt(squares / D + 1e-05)
    kv = ((keep_ref[...] + recv_ref[:, :width]) * inverse).astype(jnp.bfloat16)
    lane = lax.broadcasted_iota(jnp.int32, (META, HD), 1)
    row_at = lax.broadcasted_iota(jnp.int32, (MAXLEN, rows), 1)
    row_at = row_at - lax.broadcasted_iota(jnp.int32, (MAXLEN, rows), 0)
    for base in range(0, prompts, GROUP):
        turns = range(base, min(base + GROUP, prompts))
        picks = [(row_at == start_ref[k]).astype(jnp.float32).astype(jnp.bfloat16) for k in turns]
        blocks = jnp.dot(
            jnp.concatenate(picks, axis=0), kv, preferred_element_type=jnp.float32
        ).astype(jnp.bfloat16)
        for k in turns:
            at = (k - base) * MAXLEN
            for g in range(width // HD):
                outs[k][g * MAXLEN : (g + 1) * MAXLEN, :] = blocks[
                    at : at + MAXLEN, g * HD : (g + 1) * HD
                ]
            slot = slot_ref[k]
            meta = jnp.where(lane == 0, slot, jnp.where(lane == 1, len_ref[0, slot], 0))
            outs[k][width // HD * MAXLEN :, :] = meta.astype(jnp.float32).astype(jnp.bfloat16)


def pack(me, keep, recv, send, lengths, decode_host, sections):
    width = keep.shape[1]
    height = width // HD * MAXLEN + META
    return pl.pallas_call(
        pack_kernel,
        out_shape=[jax.ShapeDtypeStruct((height, HD), jnp.bfloat16)] * sections,
        in_specs=[SMEM, VMEM, VMEM, VMEM, SMEM, SMEM],
        out_specs=[VMEM] * sections,
        scratch_shapes=[pltpu.SMEM((sections,), jnp.int32), pltpu.SMEM((sections,), jnp.int32)],
        compiler_params=pltpu.CompilerParams(vmem_limit_bytes=VMEM_LIMIT),
        name="pack",
    )(me, keep, recv, send, lengths, decode_host)


def attend_blocks(blocks, count_ref, q_ref, score_ref, value_ref, acc_ref):
    groups = q_ref.shape[0] // QPK
    scale = HD ** (-0.5)
    flat = QPK * BMAX
    lane = lax.broadcasted_iota(jnp.int32, (flat, MAXLEN), 1)
    beam = lax.broadcasted_iota(jnp.int32, (QPK, BMAX, HD), 1)
    work = []
    for block in blocks:
        meta = block[2 * groups * MAXLEN :, :].astype(jnp.float32)
        slot = meta[0, 0].astype(jnp.int32)
        length = meta[0, 1].astype(jnp.int32)
        start = 0
        for i in range(count_ref.shape[1]):
            start = start + jnp.where(i < slot, count_ref[0, i], 0)
        for g in range(groups):
            work.append((block, g, length, pl.ds(start, BMAX), count_ref[0, slot]))
    scores = []
    for block, g, length, at, count in work:
        q = q_ref[g * QPK : (g + 1) * QPK, at, :].reshape(flat, HD).astype(jnp.bfloat16)
        keys = block[2 * g * MAXLEN : (2 * g + 1) * MAXLEN, :]
        raw = lax.dot_general(q, keys, (((1,), (1,)), ((), ())), preferred_element_type=jnp.float32)
        scores.append(jnp.where(lane < length, raw * scale, -jnp.inf))
    tops, owns = [], []
    for (block, g, length, at, count), score in zip(work, scores):
        own = score_ref[g * QPK : (g + 1) * QPK, at, :].reshape(flat, HD)[:, :1]
        owns.append(own)
        tops.append(jnp.maximum(jnp.max(score, axis=1, keepdims=True), own))
    expos = [jnp.exp(score - top) for score, top in zip(scores, tops)]
    own_expos = [jnp.exp(own - top) for own, top in zip(owns, tops)]
    totals = [jnp.sum(e, axis=1, keepdims=True) + o for e, o in zip(expos, own_expos)]
    weights = [(e / t).astype(jnp.bfloat16) for e, t in zip(expos, totals)]
    own_weights = [(o / t).astype(jnp.bfloat16).astype(jnp.float32) for o, t in zip(own_expos, totals)]
    mixes = []
    for (block, g, length, at, count), weight in zip(work, weights):
        values = block[(2 * g + 1) * MAXLEN : (2 * g + 2) * MAXLEN, :]
        mixes.append(jnp.dot(weight, values, preferred_element_type=jnp.float32))
    for (block, g, length, at, count), mix, own in zip(work, mixes, own_weights):
        own = own.reshape(QPK, BMAX, 1) * value_ref[g, at, :][None]
        heads = slice(g * QPK, (g + 1) * QPK)
        acc_ref[heads, at, :] = jnp.where(
            beam < count, mix.reshape(QPK, BMAX, HD) + own, acc_ref[heads, at, :]
        )


def first_kernel(query_ref, own_ref, count_ref, block_ref, q_ref, score_ref, value_ref, acc_ref):
    beams = query_ref.shape[0]
    heads = query_ref.shape[1] // HD
    scale = HD ** (-0.5)
    tail = jnp.zeros((BMAX, HD), jnp.float32)
    for g in range(heads // QPK):
        key = own_ref[:, 2 * g * HD : (2 * g + 1) * HD].astype(jnp.float32)
        value_ref[g, :beams, :] = own_ref[:, (2 * g + 1) * HD : (2 * g + 2) * HD].astype(jnp.float32)
        value_ref[g, beams:, :] = tail
        for h in range(g * QPK, (g + 1) * QPK):
            q = query_ref[:, h * HD : (h + 1) * HD].astype(jnp.float32)
            q_ref[h, :beams, :] = q
            q_ref[h, beams:, :] = tail
            score = jnp.sum(q * key, axis=1, keepdims=True) * scale
            score_ref[h, :beams, :] = jnp.broadcast_to(score, (beams, HD))
            score_ref[h, beams:, :] = tail
    acc_ref[...] = jnp.zeros_like(acc_ref)
    attend_blocks([block_ref], count_ref, q_ref, score_ref, value_ref, acc_ref)


def attend_first(query, own, counts, block):
    beams, width = query.shape
    heads = width // HD
    tall = jax.ShapeDtypeStruct((heads, beams + BMAX, HD), jnp.float32)
    return pl.pallas_call(
        first_kernel,
        out_shape=(tall, tall, jax.ShapeDtypeStruct((heads // QPK, beams + BMAX, HD), jnp.float32), tall),
        in_specs=[VMEM, VMEM, SMEM, VMEM],
        out_specs=(VMEM,) * 4,
        compiler_params=pltpu.CompilerParams(vmem_limit_bytes=VMEM_LIMIT),
        cost_estimate=pl.CostEstimate(flops=1 << 24, bytes_accessed=4 << 20, transcendentals=0),
        name="attend_first",
    )(query, own, counts, block)


def later_kernel(count_ref, q_ref, score_ref, value_ref, acc_in, *refs, n_blocks, last):
    blocks, rest = refs[:n_blocks], refs[n_blocks:]
    acc_ref = rest[0]
    for base in range(0, n_blocks, GROUP // 2):
        attend_blocks(blocks[base : base + GROUP // 2], count_ref, q_ref, score_ref, value_ref, acc_ref)
    if last:
        out_ref = rest[1]
        beams = out_ref.shape[0]
        for h in range(acc_ref.shape[0]):
            out_ref[:, h * HD : (h + 1) * HD] = acc_ref[h, :beams, :].astype(jnp.bfloat16)


def attend_later(counts, q, score, value, acc, blocks, out_shape):
    last = out_shape is not None
    shapes = [jax.ShapeDtypeStruct(acc.shape, acc.dtype)]
    if last:
        shapes.append(out_shape)
    return pl.pallas_call(
        functools.partial(later_kernel, n_blocks=len(blocks), last=last),
        out_shape=shapes,
        in_specs=[SMEM] + [VMEM] * (4 + len(blocks)),
        out_specs=[VMEM] * len(shapes),
        input_output_aliases={4: 0},
        compiler_params=pltpu.CompilerParams(vmem_limit_bytes=VMEM_LIMIT),
        cost_estimate=pl.CostEstimate(flops=1 << 24, bytes_accessed=4 << 20, transcendentals=0),
        name="attend_last" if last else "attend_more",
    )(counts, q, score, value, acc, *blocks)


def per_device(tokens, norm_gain, kv_weight, lengths, decode_host, beam_counts, beam_query, beam_newkv):
    sections = lax.axis_size("section")
    mine = lax.axis_index("tensor").astype(jnp.int32).reshape(1)
    me = lax.axis_index("section").astype(jnp.int32).reshape(1)
    gain = norm_gain.reshape(-1, HD)
    send, scaled = project_send(1 - mine, tokens, gain, kv_weight)
    recv = lax.ppermute(send, "tensor", [(0, 1), (1, 0)])
    keep = project_keep(mine, scaled, kv_weight)
    blocks = pack(me, keep, recv, send, lengths, decode_host, sections)
    got = {}
    for k in range(1, sections):
        got[k] = lax.ppermute(blocks[k], "section", [(s, s ^ k) for s in range(sections)])
    q, score, value, acc = attend_first(beam_query, beam_newkv, beam_counts, blocks[0])
    cut = sections // 2
    early = [got[k] for k in range(sections - 1, cut, -1)]
    late = [got[k] for k in range(cut, 0, -1)]
    (acc,) = attend_later(beam_counts, q, score, value, acc, early, None)
    out_shape = jax.ShapeDtypeStruct(beam_query.shape, jnp.bfloat16)
    return attend_later(beam_counts, q, score, value, acc, late, out_shape)[1]


def solution(mesh):
    rows = ("groups", "section")
    placed = (
        P(rows, "tensor"),
        P("tensor"),
        P("tensor", None),
        P(rows, None),
        P(rows, None),
        P(rows, None),
        P(rows, "tensor"),
        P(rows, "tensor"),
    )
    return jax.shard_map(
        per_device,
        mesh=mesh,
        in_specs=placed,
        out_specs=P(rows, "tensor"),
        check_vma=False,
    )
```

time: 83.8 us -> 38.1 us (0.45)
  other arithmetic: 15.4 us -> 0 us
  local copies, waits for them, and re-layouts: 16.6 us -> 2.31 us
  between operations: 13.7 us -> 0.08 us
  Pallas kernels: 0 us -> 13.4 us
  waiting for transfers between devices: 12.4 us -> 2.15 us
  matrix products: 9.43 us -> 0 us
  starting transfers between devices: 13.3 us -> 20 us
  blocking collectives: 2.46 us -> 0 us
    ppermute x0 -> x8, starting transfers between devices: none -> 20 us  [the longest x7 19.5 us: per_device(): lax.ppermute(blocks[k], 'section', [(s, s ^ k) for s in range(sections)])]
    pallas_call x0 -> x6, Pallas kernels: none -> 13.4 us  [the longest x2 4.3 us: attend_later(): pl.pallas_call(functools.partial(later_kernel, n_blocks=len(blocks), last...]
    all_to_all x2 -> x0, starting transfers between devices: 13.2 us -> none  [the longest x1 7.28 us: per_device(): lax.all_to_all(out_tags, 'section', split_axis=0, concat_axis=0, tiled=True)]
    all_to_all x2 -> x0, waiting for transfers between devices: 12.4 us -> none  [the longest x1 12.4 us: per_device(): lax.all_to_all(outgoing, 'section', split_axis=0, concat_axis=0, tiled=True)]
    gather x9 -> x0, local copies, waits for them, and re-layouts: 11.2 us -> none  [the longest x1 3.54 us: per_device(): return context_pad[beam_slot, within]]
    dot_general x4 -> x0, matrix products: 9.43 us -> none  [the longest x1 7.35 us: per_device(): jnp.dot(scaled, kv_weight, preferred_element_type=jnp.float32)]
    concatenate x1 -> x0, other arithmetic: 5.01 us -> none  [per_device(): return context_pad[beam_slot, within]]
    convert_element_type x6 -> x0, other arithmetic: 3.32 us -> none  [the longest x1 1.14 us: per_device(): prompt_kv = (own_part * inverse[:, None]).astype(jnp.bfloat16)]
  transfers between devices with their start and end apart: 3 -> 8, of which waited for: 1 -> 3; matrix products, arithmetic and copies ran while one was open for 34% -> 0% of each run, Pallas kernels for 0% -> 15%
where the time goes in v2:
time: 38.1 us; the launch traced here: 37.9 us
  starting transfers between devices  20 us (52%)
  Pallas kernels  13.4 us (35%)
  local copies, waits for them, and re-layouts  2.31 us (6%)
  waiting for transfers between devices  2.15 us (6%)
    ppermute x7, starting transfers between devices, per_device(): lax.ppermute(blocks[k], 'section', [(s, s ^ k) for s in range(sections)])  19.5 us
    pallas_call x2, Pallas kernels, attend_later(): pl.pallas_call(functools.partial(later_kernel, n_blocks=len(blocks), last...  4.3 us
    pallas_call x1, Pallas kernels, project_send(): pl.pallas_call(project_send_kernel, out_shape=(jax.ShapeDtypeStruct((rows...  3.88 us
    pallas_call x1, Pallas kernels, project_keep(): pl.pallas_call(project_keep_kernel, out_shape=jax.ShapeDtypeStruct((rows,...  2.78 us
    unnamed x14, local copies, waits for them, and re-layouts  2.31 us
    ppermute x7, waiting for transfers between devices, per_device(): lax.ppermute(blocks[k], 'section', [(s, s ^ k) for s in range(sections)])  2.15 us
    pallas_call x1, Pallas kernels, attend_first(): pl.pallas_call(first_kernel, out_shape=(tall, tall, jax.ShapeDtypeStruct(...  1.37 us
    pallas_call x1, Pallas kernels, pack(): pl.pallas_call(pack_kernel, out_shape=[jax.ShapeDtypeStruct((height, HD),...  1.02 us
  transfers between devices with their start and end apart: 8, of which 3 were waited for; matrix products, arithmetic and copies ran while one was open for 0% of the time, Pallas kernels for 15%

profile of v2, /device:TPU:0, one launch (start us, length us, event | category | flops | bytes accessed | tf_op | source)
XLA Modules:
  0.0 37.9 jit_solution(12999330717116355090)
XLA Ops:
  0.0 0.0 copy-start
  0.0 1.6 %copy-done = bf16[256,4096]{1,0:T(8,128)(2,1)S(1)} copy-done((bf16[256,4096]{1,0:T(8,128)(2,1)S(1)}, bf16[256,4096]{1,0:T(8,128)(2,1)}, u32[]{:S(2)}) %copy-start) | copy-done | bytes 2097176
  1.6 0.0 copy-start.3
  1.6 0.7 %copy-done.3 = bf16[4096]{0:T(1024)(128)(2,1)S(1)} copy-done((bf16[4096]{0:T(1024)(128)(2,1)S(1)}, bf16[4096]{0:T(1024)(128)(2,1)}, u32[]{:S(2)}) %copy-start.3) | copy-done | bytes 8216
  2.3 3.9 %project_send.1 = (f32[256,640]{1,0:T(8,128)S(1)}, bf16[256,4096]{1,0:T(8,128)(2,1)S(1)}) custom-call(s32[1]{0:T(128)S(6)} %sub.3.half_ref, bf16[256,4096]{1,0:T(8,128)(2,1)S(1)} %copy-done, bf16[32,128]{1,0:T(8,128)(2,1)S(1)} %bitcast.3, bf16[4096,1024]{1,0:T(8,128)(2,1)} %w_ref.3), custom_call_target="tpu_custom_call" | custom-call | flops 1073741824 | bytes 6815744 | tf_op jit(solution)/shard_map/project_send/pallas_call | solution.py:91
  6.2 0.5 %collective-permute-start = (f32[256,640]{1,0:T(8,128)S(1)}, f32[256,640]{1,0:T(8,128)S(1)}, u32[]{:S(2)}, u32[]{:S(2)}) collective-permute-start(f32[256,640]{1,0:T(8,128)S(1)} %get-tuple-element.21.send_ref), channel_id=1, source_target_pairs={{0,1},{1,0},{2,3},{3,2},{4,5},{5,4},{6,7},{7,6},{8,9},{9,8},{10,11... | collective-permute-start | bytes 1966088 | tf_op jit(solution)/shard_map/ppermute | solution.py:292
  6.7 0.0 copy-start.4
  6.7 2.8 %project_keep.1.keep_ref = f32[256,512]{1,0:T(8,128)S(1)} custom-call(s32[1]{0:T(128)} %bitcast.1.half_ref, bf16[256,4096]{1,0:T(8,128)(2,1)S(1)} %get-tuple-element.20.scaled_ref, bf16[4096,1024]{1,0:T(8,128)(2,1)} %w_ref.3), custom_call_target="tpu_custom_call" | custom-call | flops 1073741824 | bytes 6815744 | tf_op jit(solution)/shard_map/project_keep/pallas_call | solution.py:115
  9.5 0.0 collective-permute-done.recv_ref
  9.5 0.0 copy-done.5
  9.5 0.0 copy-done.6
  9.5 1.0 %pack.1 = (bf16[400,128]{1,0:T(8,128)(2,1)S(1)}, bf16[400,128]{1,0:T(8,128)(2,1)S(1)}, bf16[400,128]{1,0:T(8,128)(2,1)S(1)}, bf16[400,128]{1,0:T(8,128)(2,1)S(1)...) custom-call(s32[1]{0:T(128)} %bitcast.me_ref, ...), custom_call_target="tpu_custom_call" | custom-call | tf_op jit(solution)/shard_map/pack/pallas_call | solution.py:167
  10.6 5.7 %collective-permute-start.1 = (bf16[400,128]{1,0:T(8,128)(2,1)S(1)}, bf16[400,128]{1,0:T(8,128)(2,1)S(1)}, u32[]{:S(2)}, u32[]{:S(2)}) collective-permute-start(bf16[400,128]{1,0:T(8,128)(2,1)S(1)} %get-tuple-element.27), channel_id=1, source_target_pairs={{0,14},{2,12},{4,10},{6,8},{8,6},{10,4},{12,2},{14,0},{1,15},{3,13... | collective-permute-start | bytes 307208 | tf_op jit(solution)/shard_map/ppermute | solution.py:297
  16.2 0.2 collective-permute-start.2
  16.5 0.7 %collective-permute-start.3 = (bf16[400,128]{1,0:T(8,128)(2,1)S(1)}, bf16[400,128]{1,0:T(8,128)(2,1)S(1)}, u32[]{:S(2)}, u32[]{:S(2)}) collective-permute-start(bf16[400,128]{1,0:T(8,128)(2,1)S(1)} %get-tuple-element.29), channel_id=1, source_target_pairs={{0,10},{2,8},{4,14},{6,12},{8,2},{10,0},{12,6},{14,4},{1,11},{3,9}... | collective-permute-start | bytes 307208 | tf_op jit(solution)/shard_map/ppermute | solution.py:297
  17.2 2.0 %collective-permute-start.4 = (bf16[400,128]{1,0:T(8,128)(2,1)S(1)}, bf16[400,128]{1,0:T(8,128)(2,1)S(1)}, u32[]{:S(2)}, u32[]{:S(2)}) collective-permute-start(bf16[400,128]{1,0:T(8,128)(2,1)S(1)} %get-tuple-element.30), channel_id=1, source_target_pairs={{0,8},{2,10},{4,12},{6,14},{8,0},{10,2},{12,4},{14,6},{1,9},{3,11}... | collective-permute-start | bytes 307208 | tf_op jit(solution)/shard_map/ppermute | solution.py:297
  19.2 2.3 %collective-permute-start.5 = (bf16[400,128]{1,0:T(8,128)(2,1)S(1)}, bf16[400,128]{1,0:T(8,128)(2,1)S(1)}, u32[]{:S(2)}, u32[]{:S(2)}) collective-permute-start(bf16[400,128]{1,0:T(8,128)(2,1)S(1)} %get-tuple-element.31), channel_id=1, source_target_pairs={{0,6},{2,4},{4,2},{6,0},{8,14},{10,12},{12,10},{14,8},{1,7},{3,5},... | collective-permute-start | bytes 307208 | tf_op jit(solution)/shard_map/ppermute | solution.py:297
  21.5 0.0 collective-permute-done.1.refs_0_
  21.5 7.0 %collective-permute-start.6 = (bf16[400,128]{1,0:T(8,128)(2,1)S(1)}, bf16[400,128]{1,0:T(8,128)(2,1)S(1)}, u32[]{:S(2)}, u32[]{:S(2)}) collective-permute-start(bf16[400,128]{1,0:T(8,128)(2,1)S(1)} %get-tuple-element.32), channel_id=1, source_target_pairs={{0,4},{2,6},{4,0},{6,2},{8,12},{10,14},{12,8},{14,10},{1,5},{3,7},... | collective-permute-start | bytes 307208 | tf_op jit(solution)/shard_map/ppermute | solution.py:297
  28.6 0.0 collective-permute-done.2.refs_1_
  28.6 1.5 %collective-permute-start.7 = (bf16[400,128]{1,0:T(8,128)(2,1)S(1)}, bf16[400,128]{1,0:T(8,128)(2,1)S(1)}, u32[]{:S(2)}, u32[]{:S(2)}) collective-permute-start(bf16[400,128]{1,0:T(8,128)(2,1)S(1)} %get-tuple-element.33), channel_id=1, source_target_pairs={{0,2},{2,0},{4,6},{6,4},{8,10},{10,8},{12,14},{14,12},{1,3},{3,1},... | collective-permute-start | bytes 307208 | tf_op jit(solution)/shard_map/ppermute | solution.py:297
  30.0 0.0 copy-done.1
  30.0 0.0 copy-done.2
  30.1 0.0 copy-done.4
  30.1 1.4 %attend_first.1 = (f32[16,96,128]{2,1,0:T(8,128)S(1)}, f32[16,96,128]{2,1,0:T(8,128)S(1)}, f32[2,96,128]{2,1,0:T(8,128)S(1)}, f32[16,96,128]{2,1,0:T(8,128)S(1)}) custom-call(bf16[80,2048]{1,0:T(8,128)(2,1)S(1)} %copy-done.1, bf16[80,512]{1,0:T(8,128)(2,1)S(1)} %copy-done.2, s32[1,8]{1,0:T(1,128)S(1)} %copy-done.4, ...), custom_call_target="tpu_custom_call" | custom-call | flops 16777216 | bytes 4194304 | tf_op jit(solution)/shard_map/attend_first/pallas_call | solution.py:246
  31.4 1.1 %collective-permute-done.3.refs_2_ = bf16[400,128]{1,0:T(8,128)(2,1)S(1)} collective-permute-done((bf16[400,128]{1,0:T(8,128)(2,1)S(1)}, bf16[400,128]{1,0:T(8,128)(2,1)S(1)}, u32[]{:S(2)}, u32[]{:S(2)}) %collective-permute-start.3) | collective-permute-done | bytes 102432 | tf_op jit(solution)/shard_map/ppermute | solution.py:297
  32.5 1.7 %attend_more.1.acc_in = f32[16,96,128]{2,1,0:T(8,128)S(1)} custom-call(s32[1,8]{1,0:T(1,128)S(1)} %copy-done.4, f32[16,96,128]{2,1,0:T(8,128)S(1)} %get-tuple-element.23.q_ref, f32[16,96,128]{2,1,0:T(8,128)S(1)} %get-tuple-element.24.score_ref, f32[2,96,128]{2,1,0:T(8,128)S(1)} %get-tuple-element.25.value_ref, ...), custom_call_target="tpu_custom_call", output_to_operand_aliasing={{}: (4, {})} | custom-call | flops 16777216 | bytes 4194304 | tf_op jit(solution)/shard_map/attend_more/pallas_call | solution.py:274
  34.2 0.1 collective-permute-done.4.refs_0_
  34.4 0.0 collective-permute-done.5.refs_1_
  34.4 0.9 %collective-permute-done.6.refs_2_ = bf16[400,128]{1,0:T(8,128)(2,1)S(1)} collective-permute-done((bf16[400,128]{1,0:T(8,128)(2,1)S(1)}, bf16[400,128]{1,0:T(8,128)(2,1)S(1)}, u32[]{:S(2)}, u32[]{:S(2)}) %collective-permute-start.6) | collective-permute-done | bytes 102432 | tf_op jit(solution)/shard_map/ppermute | solution.py:297
  35.2 0.0 collective-permute-done.7.refs_3_
  35.3 2.6 %attend_last.1 = (f32[16,96,128]{2,1,0:T(8,128)S(1)}, bf16[80,2048]{1,0:T(8,128)(2,1)}) custom-call(s32[1,8]{1,0:T(1,128)S(1)} %copy-done.4, f32[16,96,128]{2,1,0:T(8,128)S(1)} %get-tuple-element.23.q_ref, f32[16,96,128]{2,1,0:T(8,128)S(1)} %get-tuple-element.24.score_ref, ...), custom_call_target="tpu_custom_call", output_to_operand_aliasing={{0}: (4, {})} | custom-call | flops 16777216 | bytes 4194304 | tf_op jit(solution)/shard_map/attend_last/pallas_call | solution.py:274
  (4 shorter events, 0.0 us)
Async XLA Ops:
  0.0 1.6 %copy-start = (bf16[256,4096]{1,0:T(8,128)(2,1)S(1)}, bf16[256,4096]{1,0:T(8,128)(2,1)}, u32[]{:S(2)}) copy-start(bf16[256,4096]{1,0:T(8,128)(2,1)} %tok_ref.1) | copy-start | bytes 6291460
  1.6 0.7 %copy-start.3 = (bf16[4096]{0:T(1024)(128)(2,1)S(1)}, bf16[4096]{0:T(1024)(128)(2,1)}, u32[]{:S(2)}) copy-start(bf16[4096]{0:T(1024)(128)(2,1)} %param.9) | copy-start | bytes 24580
  6.2 3.3 %collective-permute-start = (f32[256,640]{1,0:T(8,128)S(1)}, f32[256,640]{1,0:T(8,128)S(1)}, u32[]{:S(2)}, u32[]{:S(2)}) collective-permute-start(f32[256,640]{1,0:T(8,128)S(1)} %get-tuple-element.21.send_ref), channel_id=1, source_target_pairs={{0,1},{1,0},{2,3},{3,2},{4,5},{5,4},{6,7},{7,6},{8,9},{9,8},{10,11... | collective-permute-start | bytes 1966088 | tf_op jit(solution)/shard_map/ppermute | solution.py:292
  6.7 2.8 %copy-start.5 = (s32[1,8]{1,0:T(1,128)S(1)}, s32[1,8]{1,0:T(1,128)}, u32[]{:S(2)}) copy-start(s32[1,8]{1,0:T(1,128)} %len_ref.1) | copy-start | bytes 100
  6.7 2.8 %copy-start.6 = (s32[1,8]{1,0:T(1,128)S(1)}, s32[1,8]{1,0:T(1,128)}, u32[]{:S(2)}) copy-start(s32[1,8]{1,0:T(1,128)} %host_ref.1) | copy-start | bytes 100
  6.7 23.3 %copy-start.1 = (bf16[80,2048]{1,0:T(8,128)(2,1)S(1)}, bf16[80,2048]{1,0:T(8,128)(2,1)}, u32[]{:S(2)}) copy-start(bf16[80,2048]{1,0:T(8,128)(2,1)} %query_ref.1) | copy-start | bytes 983044
  6.7 23.3 %copy-start.2 = (bf16[80,512]{1,0:T(8,128)(2,1)S(1)}, bf16[80,512]{1,0:T(8,128)(2,1)}, u32[]{:S(2)}) copy-start(bf16[80,512]{1,0:T(8,128)(2,1)} %own_ref.1) | copy-start | bytes 245764
  6.7 23.3 %copy-start.4 = (s32[1,8]{1,0:T(1,128)S(1)}, s32[1,8]{1,0:T(1,128)}, u32[]{:S(2)}) copy-start(s32[1,8]{1,0:T(1,128)} %count_ref.5) | copy-start | bytes 100
  10.6 11.0 %collective-permute-start.1 = (bf16[400,128]{1,0:T(8,128)(2,1)S(1)}, bf16[400,128]{1,0:T(8,128)(2,1)S(1)}, u32[]{:S(2)}, u32[]{:S(2)}) collective-permute-start(bf16[400,128]{1,0:T(8,128)(2,1)S(1)} %get-tuple-element.27), channel_id=1, source_target_pairs={{0,14},{2,12},{4,10},{6,8},{8,6},{10,4},{12,2},{14,0},{1,15},{3,13... | collective-permute-start | bytes 307208 | tf_op jit(solution)/shard_map/ppermute | solution.py:297
  16.2 12.3 %collective-permute-start.2 = (bf16[400,128]{1,0:T(8,128)(2,1)S(1)}, bf16[400,128]{1,0:T(8,128)(2,1)S(1)}, u32[]{:S(2)}, u32[]{:S(2)}) collective-permute-start(bf16[400,128]{1,0:T(8,128)(2,1)S(1)} %get-tuple-element.28), channel_id=1, source_target_pairs={{0,12},{2,14},{4,8},{6,10},{8,4},{10,6},{12,0},{14,2},{1,13},{3,15... | collective-permute-start | bytes 307208 | tf_op jit(solution)/shard_map/ppermute | solution.py:297
  16.5 16.1 %collective-permute-start.3 = (bf16[400,128]{1,0:T(8,128)(2,1)S(1)}, bf16[400,128]{1,0:T(8,128)(2,1)S(1)}, u32[]{:S(2)}, u32[]{:S(2)}) collective-permute-start(bf16[400,128]{1,0:T(8,128)(2,1)S(1)} %get-tuple-element.29), channel_id=1, source_target_pairs={{0,10},{2,8},{4,14},{6,12},{8,2},{10,0},{12,6},{14,4},{1,11},{3,9}... | collective-permute-start | bytes 307208 | tf_op jit(solution)/shard_map/ppermute | solution.py:297
  17.2 17.2 %collective-permute-start.4 = (bf16[400,128]{1,0:T(8,128)(2,1)S(1)}, bf16[400,128]{1,0:T(8,128)(2,1)S(1)}, u32[]{:S(2)}, u32[]{:S(2)}) collective-permute-start(bf16[400,128]{1,0:T(8,128)(2,1)S(1)} %get-tuple-element.30), channel_id=1, source_target_pairs={{0,8},{2,10},{4,12},{6,14},{8,0},{10,2},{12,4},{14,6},{1,9},{3,11}... | collective-permute-start | bytes 307208 | tf_op jit(solution)/shard_map/ppermute | solution.py:297
  19.2 15.1 %collective-permute-start.5 = (bf16[400,128]{1,0:T(8,128)(2,1)S(1)}, bf16[400,128]{1,0:T(8,128)(2,1)S(1)}, u32[]{:S(2)}, u32[]{:S(2)}) collective-permute-start(bf16[400,128]{1,0:T(8,128)(2,1)S(1)} %get-tuple-element.31), channel_id=1, source_target_pairs={{0,6},{2,4},{4,2},{6,0},{8,14},{10,12},{12,10},{14,8},{1,7},{3,5},... | collective-permute-start | bytes 307208 | tf_op jit(solution)/shard_map/ppermute | solution.py:297
  21.5 13.7 %collective-permute-start.6 = (bf16[400,128]{1,0:T(8,128)(2,1)S(1)}, bf16[400,128]{1,0:T(8,128)(2,1)S(1)}, u32[]{:S(2)}, u32[]{:S(2)}) collective-permute-start(bf16[400,128]{1,0:T(8,128)(2,1)S(1)} %get-tuple-element.32), channel_id=1, source_target_pairs={{0,4},{2,6},{4,0},{6,2},{8,12},{10,14},{12,8},{14,10},{1,5},{3,7},... | collective-permute-start | bytes 307208 | tf_op jit(solution)/shard_map/ppermute | solution.py:297
  28.6 6.7 %collective-permute-start.7 = (bf16[400,128]{1,0:T(8,128)(2,1)S(1)}, bf16[400,128]{1,0:T(8,128)(2,1)S(1)}, u32[]{:S(2)}, u32[]{:S(2)}) collective-permute-start(bf16[400,128]{1,0:T(8,128)(2,1)S(1)} %get-tuple-element.33), channel_id=1, source_target_pairs={{0,2},{2,0},{4,6},{6,4},{8,10},{10,8},{12,14},{14,12},{1,3},{3,1},... | collective-permute-start | bytes 307208 | tf_op jit(solution)/shard_map/ppermute | solution.py:297

commit v3 on v2

--- a/solution.py
+++ b/solution.py
@@ -16,6 +16,7 @@
 STEP = 512
 GROUP = 8
 VMEM_LIMIT = 44 * 1024 * 1024
+PROJECT_LIMIT = 52800000
 
 VMEM = pl.BlockSpec(memory_space=pltpu.VMEM)
 SMEM = pl.BlockSpec(memory_space=pltpu.SMEM)
@@ -32,25 +33,33 @@
     half = half_ref[0]
     steps = w_buf.shape[0]
     width = w_buf.shape[2]
+    blocks = STEP // HD
 
     def token_copy(c):
         return pltpu.make_async_copy(tok_ref.at[:, pl.ds(c * STEP, STEP)], tok_buf.at[c], tok_sem.at[c])
+
+    def scale(c):
+        token_copy(c).wait()
+        squares = None
+        for b in range(blocks):
+            at = c * blocks + b
+            tok = tok_buf[c, :, b * HD : (b + 1) * HD].astype(jnp.float32)
+            scaled_ref[:, at * HD : (at + 1) * HD] = (tok * gain[at : at + 1, :]).astype(jnp.bfloat16)
+            squares = tok * tok if squares is None else squares + tok * tok
+        if c == 0:
+            out_ref[:, width:] = squares
+        else:
+            out_ref[:, width:] += squares
 
     for c in range(steps):
         token_copy(c).start()
         weight_copy(w_ref, w_buf, w_sem, half, c).start()
     gain = gain_ref[...].astype(jnp.float32)
+    scale(0)
     for c in range(steps):
-        token_copy(c).wait()
-        for b in range(STEP // HD):
-            at = c * (STEP // HD) + b
-            tok = tok_buf[c, :, b * HD : (b + 1) * HD].astype(jnp.float32)
-            scaled_ref[:, at * HD : (at + 1) * HD] = (tok * gain[at : at + 1, :]).astype(jnp.bfloat16)
-            if at == 0:
-                out_ref[:, width:] = tok * tok
-            else:
-                out_ref[:, width:] += tok * tok
         weight_copy(w_ref, w_buf, w_sem, half, c).wait()
+        if c + 1 < steps:
+            scale(c + 1)
         part = jnp.dot(
             scaled_ref[:, c * STEP : (c + 1) * STEP], w_buf[c], preferred_element_type=jnp.float32
         )
@@ -102,7 +111,7 @@
             pltpu.SemaphoreType.DMA((steps,)),
             pltpu.SemaphoreType.DMA((steps,)),
         ],
-        compiler_params=pltpu.CompilerParams(vmem_limit_bytes=VMEM_LIMIT),
+        compiler_params=pltpu.CompilerParams(vmem_limit_bytes=PROJECT_LIMIT),
         cost_estimate=project_cost(rows, depth, width),
         name="project_send",
     )(half, tokens, gain, weight)
@@ -297,8 +306,11 @@
         got[k] = lax.ppermute(blocks[k], "section", [(s, s ^ k) for s in range(sections)])
     q, score, value, acc = attend_first(beam_query, beam_newkv, beam_counts, blocks[0])
     cut = sections // 2
-    early = [got[k] for k in range(sections - 1, cut, -1)]
-    late = [got[k] for k in range(cut, 0, -1)]
+    near = [k for k in range(1, cut)]
+    order = [sections - 1] + [k for pair in zip(range(sections - 2, cut, -1), near) for k in pair]
+    order = order + [near[-1], cut]
+    early = [got[k] for k in order[:-2]]
+    late = [got[k] for k in order[-2:]]
     (acc,) = attend_later(beam_counts, q, score, value, acc, early, None)
     out_shape = jax.ShapeDtypeStruct(beam_query.shape, jnp.bfloat16)
     return attend_later(beam_counts, q, score, value, acc, late, out_shape)[1]

time: 38.1 us -> 35.1 us (0.921)
  local copies, waits for them, and re-layouts: 2.31 us -> 0.72 us
  waiting for transfers between devices: 2.15 us -> 0.89 us
  starting transfers between devices: 20 us -> 19.6 us
    unnamed x14 -> x12, local copies, waits for them, and re-layouts: 2.31 us -> 0.72 us
    ppermute x7, waiting for transfers between devices: 2.15 us -> 0.89 us  [per_device(): lax.ppermute(blocks[k], 'section', [(s, s ^ k) for s in range(sections)])]
  transfers between devices with their start and end apart: 8 -> 8, of which waited for: 3 -> 1; matrix products, arithmetic and copies ran while one was open for 0% -> 0% of each run, Pallas kernels for 15% -> 19%
where the time goes in v3:
time: 35.1 us; the launch traced here: 34.9 us
  starting transfers between devices  19.6 us (56%)
  Pallas kernels  13.5 us (38%)
  waiting for transfers between devices  0.89 us (3%)
  local copies, waits for them, and re-layouts  0.72 us (2%)
    ppermute x7, starting transfers between devices, per_device(): lax.ppermute(blocks[k], 'section', [(s, s ^ k) for s in range(sections)])  19.1 us
    pallas_call x2, Pallas kernels, attend_later(): pl.pallas_call(functools.partial(later_kernel, n_blocks=len(blocks), last...  4.57 us
    pallas_call x1, Pallas kernels, project_send(): pl.pallas_call(project_send_kernel, out_shape=(jax.ShapeDtypeStruct((rows...  3.79 us
    pallas_call x1, Pallas kernels, project_keep(): pl.pallas_call(project_keep_kernel, out_shape=jax.ShapeDtypeStruct((rows,...  2.78 us
    pallas_call x1, Pallas kernels, attend_first(): pl.pallas_call(first_kernel, out_shape=(tall, tall, jax.ShapeDtypeStruct(...  1.37 us
    pallas_call x1, Pallas kernels, pack(): pl.pallas_call(pack_kernel, out_shape=[jax.ShapeDtypeStruct((height, HD),...  1.02 us
    ppermute x7, waiting for transfers between devices, per_device(): lax.ppermute(blocks[k], 'section', [(s, s ^ k) for s in range(sections)])  0.89 us
    unnamed x12, local copies, waits for them, and re-layouts  0.72 us
  transfers between devices with their start and end apart: 8, of which 1 were waited for; matrix products, arithmetic and copies ran while one was open for 0% of the time, Pallas kernels for 19%

profile of v3, /device:TPU:0, one launch (start us, length us, event | category | flops | bytes accessed | tf_op | source)
XLA Modules:
  0.0 34.9 jit_solution(2193068138806203697)
XLA Ops:
  0.0 0.0 copy-start.2
  0.0 0.7 %copy-done.2 = bf16[4096]{0:T(1024)(128)(2,1)S(1)} copy-done((bf16[4096]{0:T(1024)(128)(2,1)S(1)}, bf16[4096]{0:T(1024)(128)(2,1)}, u32[]{:S(2)}) %copy-start.2) | copy-done | bytes 8216
  0.7 3.8 %project_send.1 = (f32[256,640]{1,0:T(8,128)S(1)}, bf16[256,4096]{1,0:T(8,128)(2,1)S(1)}) custom-call(s32[1]{0:T(128)S(6)} %sub.3.half_ref, bf16[256,4096]{1,0:T(8,128)(2,1)} %tok_ref.1, bf16[32,128]{1,0:T(8,128)(2,1)S(1)} %bitcast.3, bf16[4096,1024]{1,0:T(8,128)(2,1)} %w_ref.3), custom_call_target="tpu_custom_call" | custom-call | flops 1073741824 | bytes 6815744 | tf_op jit(solution)/shard_map/project_send/pallas_call | solution.py:100
  4.5 0.5 %collective-permute-start = (f32[256,640]{1,0:T(8,128)S(1)}, f32[256,640]{1,0:T(8,128)S(1)}, u32[]{:S(2)}, u32[]{:S(2)}) collective-permute-start(f32[256,640]{1,0:T(8,128)S(1)} %get-tuple-element.21.send_ref), channel_id=1, source_target_pairs={{0,1},{1,0},{2,3},{3,2},{4,5},{5,4},{6,7},{7,6},{8,9},{9,8},{10,11... | collective-permute-start | bytes 1966088 | tf_op jit(solution)/shard_map/ppermute | solution.py:301
  5.0 0.0 copy-start.4
  5.0 0.0 copy-start.5
  5.0 0.0 copy-start.3
  5.0 2.8 %project_keep.1.keep_ref = f32[256,512]{1,0:T(8,128)S(1)} custom-call(s32[1]{0:T(128)} %bitcast.1.half_ref, bf16[256,4096]{1,0:T(8,128)(2,1)S(1)} %get-tuple-element.20.scaled_ref, bf16[4096,1024]{1,0:T(8,128)(2,1)} %w_ref.3), custom_call_target="tpu_custom_call" | custom-call | flops 1073741824 | bytes 6815744 | tf_op jit(solution)/shard_map/project_keep/pallas_call | solution.py:124
  7.8 0.0 collective-permute-done.recv_ref
  7.8 0.0 copy-done.4
  7.9 0.0 copy-done.5
  7.9 1.0 %pack.1 = (bf16[400,128]{1,0:T(8,128)(2,1)S(1)}, bf16[400,128]{1,0:T(8,128)(2,1)S(1)}, bf16[400,128]{1,0:T(8,128)(2,1)S(1)}, bf16[400,128]{1,0:T(8,128)(2,1)S(1)...) custom-call(s32[1]{0:T(128)} %bitcast.me_ref, ...), custom_call_target="tpu_custom_call" | custom-call | tf_op jit(solution)/shard_map/pack/pallas_call | solution.py:176
  8.9 5.7 %collective-permute-start.1 = (bf16[400,128]{1,0:T(8,128)(2,1)S(1)}, bf16[400,128]{1,0:T(8,128)(2,1)S(1)}, u32[]{:S(2)}, u32[]{:S(2)}) collective-permute-start(bf16[400,128]{1,0:T(8,128)(2,1)S(1)} %get-tuple-element.27), channel_id=1, source_target_pairs={{0,14},{2,12},{4,10},{6,8},{8,6},{10,4},{12,2},{14,0},{1,15},{3,13... | collective-permute-start | bytes 307208 | tf_op jit(solution)/shard_map/ppermute | solution.py:306
  14.6 0.2 collective-permute-start.2
  14.8 0.4 %collective-permute-start.3 = (bf16[400,128]{1,0:T(8,128)(2,1)S(1)}, bf16[400,128]{1,0:T(8,128)(2,1)S(1)}, u32[]{:S(2)}, u32[]{:S(2)}) collective-permute-start(bf16[400,128]{1,0:T(8,128)(2,1)S(1)} %get-tuple-element.29), channel_id=1, source_target_pairs={{0,2},{2,0},{4,6},{6,4},{8,10},{10,8},{12,14},{14,12},{1,3},{3,1},... | collective-permute-start | bytes 307208 | tf_op jit(solution)/shard_map/ppermute | solution.py:306
  15.2 1.8 %collective-permute-start.4 = (bf16[400,128]{1,0:T(8,128)(2,1)S(1)}, bf16[400,128]{1,0:T(8,128)(2,1)S(1)}, u32[]{:S(2)}, u32[]{:S(2)}) collective-permute-start(bf16[400,128]{1,0:T(8,128)(2,1)S(1)} %get-tuple-element.30), channel_id=1, source_target_pairs={{0,10},{2,8},{4,14},{6,12},{8,2},{10,0},{12,6},{14,4},{1,11},{3,9}... | collective-permute-start | bytes 307208 | tf_op jit(solution)/shard_map/ppermute | solution.py:306
  17.0 3.4 %collective-permute-start.5 = (bf16[400,128]{1,0:T(8,128)(2,1)S(1)}, bf16[400,128]{1,0:T(8,128)(2,1)S(1)}, u32[]{:S(2)}, u32[]{:S(2)}) collective-permute-start(bf16[400,128]{1,0:T(8,128)(2,1)S(1)} %get-tuple-element.31), channel_id=1, source_target_pairs={{0,4},{2,6},{4,0},{6,2},{8,12},{10,14},{12,8},{14,10},{1,5},{3,7},... | collective-permute-start | bytes 307208 | tf_op jit(solution)/shard_map/ppermute | solution.py:306
  20.4 0.0 collective-permute-done.1.refs_0_
  20.4 5.2 %collective-permute-start.6 = (bf16[400,128]{1,0:T(8,128)(2,1)S(1)}, bf16[400,128]{1,0:T(8,128)(2,1)S(1)}, u32[]{:S(2)}, u32[]{:S(2)}) collective-permute-start(bf16[400,128]{1,0:T(8,128)(2,1)S(1)} %get-tuple-element.32), channel_id=1, source_target_pairs={{0,6},{2,4},{4,2},{6,0},{8,14},{10,12},{12,10},{14,8},{1,7},{3,5},... | collective-permute-start | bytes 307208 | tf_op jit(solution)/shard_map/ppermute | solution.py:306
  25.6 0.0 collective-permute-done.2.refs_1_
  25.6 2.4 %collective-permute-start.7 = (bf16[400,128]{1,0:T(8,128)(2,1)S(1)}, bf16[400,128]{1,0:T(8,128)(2,1)S(1)}, u32[]{:S(2)}, u32[]{:S(2)}) collective-permute-start(bf16[400,128]{1,0:T(8,128)(2,1)S(1)} %get-tuple-element.33), channel_id=1, source_target_pairs={{0,8},{2,10},{4,12},{6,14},{8,0},{10,2},{12,4},{14,6},{1,9},{3,11}... | collective-permute-start | bytes 307208 | tf_op jit(solution)/shard_map/ppermute | solution.py:306
  28.0 0.0 copy-done
  28.0 0.0 copy-done.1
  28.0 0.0 copy-done.3
  28.0 1.4 %attend_first.1 = (f32[16,96,128]{2,1,0:T(8,128)S(1)}, f32[16,96,128]{2,1,0:T(8,128)S(1)}, f32[2,96,128]{2,1,0:T(8,128)S(1)}, f32[16,96,128]{2,1,0:T(8,128)S(1)}) custom-call(bf16[80,2048]{1,0:T(8,128)(2,1)S(1)} %copy-done, bf16[80,512]{1,0:T(8,128)(2,1)S(1)} %copy-done.1, s32[1,8]{1,0:T(1,128)S(1)} %copy-done.3, ...), custom_call_target="tpu_custom_call" | custom-call | flops 16777216 | bytes 4194304 | tf_op jit(solution)/shard_map/attend_first/pallas_call | solution.py:255
  29.4 0.0 collective-permute-done.3.refs_2_
  29.4 0.0 collective-permute-done.4.refs_3_
  29.4 0.0 collective-permute-done.5.refs_4_
  29.4 2.3 %attend_more.1.acc_in = f32[16,96,128]{2,1,0:T(8,128)S(1)} custom-call(s32[1,8]{1,0:T(1,128)S(1)} %copy-done.3, f32[16,96,128]{2,1,0:T(8,128)S(1)} %get-tuple-element.23.q_ref, f32[16,96,128]{2,1,0:T(8,128)S(1)} %get-tuple-element.24.score_ref, f32[2,96,128]{2,1,0:T(8,128)S(1)} %get-tuple-element.25.value_ref, ...), custom_call_target="tpu_custom_call", output_to_operand_aliasing={{}: (4, {})} | custom-call | flops 16777216 | bytes 4194304 | tf_op jit(solution)/shard_map/attend_more/pallas_call | solution.py:283
  31.8 0.0 collective-permute-done.6.refs_0_
  31.8 0.9 %collective-permute-done.7.refs_1_ = bf16[400,128]{1,0:T(8,128)(2,1)S(1)} collective-permute-done((bf16[400,128]{1,0:T(8,128)(2,1)S(1)}, bf16[400,128]{1,0:T(8,128)(2,1)S(1)}, u32[]{:S(2)}, u32[]{:S(2)}) %collective-permute-start.7) | collective-permute-done | bytes 102432 | tf_op jit(solution)/shard_map/ppermute | solution.py:306
  32.6 2.2 %attend_last.1 = (f32[16,96,128]{2,1,0:T(8,128)S(1)}, bf16[80,2048]{1,0:T(8,128)(2,1)}) custom-call(s32[1,8]{1,0:T(1,128)S(1)} %copy-done.3, f32[16,96,128]{2,1,0:T(8,128)S(1)} %get-tuple-element.23.q_ref, f32[16,96,128]{2,1,0:T(8,128)S(1)} %get-tuple-element.24.score_ref, ...), custom_call_target="tpu_custom_call", output_to_operand_aliasing={{0}: (4, {})} | custom-call | flops 16777216 | bytes 4194304 | tf_op jit(solution)/shard_map/attend_last/pallas_call | solution.py:283
  (2 shorter events, 0.0 us)
Async XLA Ops:
  0.0 0.7 %copy-start.2 = (bf16[4096]{0:T(1024)(128)(2,1)S(1)}, bf16[4096]{0:T(1024)(128)(2,1)}, u32[]{:S(2)}) copy-start(bf16[4096]{0:T(1024)(128)(2,1)} %param.9) | copy-start | bytes 24580
  4.5 3.3 %collective-permute-start = (f32[256,640]{1,0:T(8,128)S(1)}, f32[256,640]{1,0:T(8,128)S(1)}, u32[]{:S(2)}, u32[]{:S(2)}) collective-permute-start(f32[256,640]{1,0:T(8,128)S(1)} %get-tuple-element.21.send_ref), channel_id=1, source_target_pairs={{0,1},{1,0},{2,3},{3,2},{4,5},{5,4},{6,7},{7,6},{8,9},{9,8},{10,11... | collective-permute-start | bytes 1966088 | tf_op jit(solution)/shard_map/ppermute | solution.py:301
  5.0 2.8 %copy-start.4 = (s32[1,8]{1,0:T(1,128)S(1)}, s32[1,8]{1,0:T(1,128)}, u32[]{:S(2)}) copy-start(s32[1,8]{1,0:T(1,128)} %len_ref.1) | copy-start | bytes 100
  5.0 2.8 %copy-start.5 = (s32[1,8]{1,0:T(1,128)S(1)}, s32[1,8]{1,0:T(1,128)}, u32[]{:S(2)}) copy-start(s32[1,8]{1,0:T(1,128)} %host_ref.1) | copy-start | bytes 100
  5.0 23.0 %copy-start = (bf16[80,2048]{1,0:T(8,128)(2,1)S(1)}, bf16[80,2048]{1,0:T(8,128)(2,1)}, u32[]{:S(2)}) copy-start(bf16[80,2048]{1,0:T(8,128)(2,1)} %query_ref.1) | copy-start | bytes 983044
  5.0 23.0 %copy-start.1 = (bf16[80,512]{1,0:T(8,128)(2,1)S(1)}, bf16[80,512]{1,0:T(8,128)(2,1)}, u32[]{:S(2)}) copy-start(bf16[80,512]{1,0:T(8,128)(2,1)} %own_ref.1) | copy-start | bytes 245764
  5.0 23.0 %copy-start.3 = (s32[1,8]{1,0:T(1,128)S(1)}, s32[1,8]{1,0:T(1,128)}, u32[]{:S(2)}) copy-start(s32[1,8]{1,0:T(1,128)} %count_ref.5) | copy-start | bytes 100
  8.9 11.5 %collective-permute-start.1 = (bf16[400,128]{1,0:T(8,128)(2,1)S(1)}, bf16[400,128]{1,0:T(8,128)(2,1)S(1)}, u32[]{:S(2)}, u32[]{:S(2)}) collective-permute-start(bf16[400,128]{1,0:T(8,128)(2,1)S(1)} %get-tuple-element.27), channel_id=1, source_target_pairs={{0,14},{2,12},{4,10},{6,8},{8,6},{10,4},{12,2},{14,0},{1,15},{3,13... | collective-permute-start | bytes 307208 | tf_op jit(solution)/shard_map/ppermute | solution.py:306
  14.6 11.1 %collective-permute-start.2 = (bf16[400,128]{1,0:T(8,128)(2,1)S(1)}, bf16[400,128]{1,0:T(8,128)(2,1)S(1)}, u32[]{:S(2)}, u32[]{:S(2)}) collective-permute-start(bf16[400,128]{1,0:T(8,128)(2,1)S(1)} %get-tuple-element.28), channel_id=1, source_target_pairs={{0,12},{2,14},{4,8},{6,10},{8,4},{10,6},{12,0},{14,2},{1,13},{3,15... | collective-permute-start | bytes 307208 | tf_op jit(solution)/shard_map/ppermute | solution.py:306
  14.8 14.6 %collective-permute-start.3 = (bf16[400,128]{1,0:T(8,128)(2,1)S(1)}, bf16[400,128]{1,0:T(8,128)(2,1)S(1)}, u32[]{:S(2)}, u32[]{:S(2)}) collective-permute-start(bf16[400,128]{1,0:T(8,128)(2,1)S(1)} %get-tuple-element.29), channel_id=1, source_target_pairs={{0,2},{2,0},{4,6},{6,4},{8,10},{10,8},{12,14},{14,12},{1,3},{3,1},... | collective-permute-start | bytes 307208 | tf_op jit(solution)/shard_map/ppermute | solution.py:306
  15.2 14.2 %collective-permute-start.4 = (bf16[400,128]{1,0:T(8,128)(2,1)S(1)}, bf16[400,128]{1,0:T(8,128)(2,1)S(1)}, u32[]{:S(2)}, u32[]{:S(2)}) collective-permute-start(bf16[400,128]{1,0:T(8,128)(2,1)S(1)} %get-tuple-element.30), channel_id=1, source_target_pairs={{0,10},{2,8},{4,14},{6,12},{8,2},{10,0},{12,6},{14,4},{1,11},{3,9}... | collective-permute-start | bytes 307208 | tf_op jit(solution)/shard_map/ppermute | solution.py:306
  17.0 12.4 %collective-permute-start.5 = (bf16[400,128]{1,0:T(8,128)(2,1)S(1)}, bf16[400,128]{1,0:T(8,128)(2,1)S(1)}, u32[]{:S(2)}, u32[]{:S(2)}) collective-permute-start(bf16[400,128]{1,0:T(8,128)(2,1)S(1)} %get-tuple-element.31), channel_id=1, source_target_pairs={{0,4},{2,6},{4,0},{6,2},{8,12},{10,14},{12,8},{14,10},{1,5},{3,7},... | collective-permute-start | bytes 307208 | tf_op jit(solution)/shard_map/ppermute | solution.py:306
  20.4 11.4 %collective-permute-start.6 = (bf16[400,128]{1,0:T(8,128)(2,1)S(1)}, bf16[400,128]{1,0:T(8,128)(2,1)S(1)}, u32[]{:S(2)}, u32[]{:S(2)}) collective-permute-start(bf16[400,128]{1,0:T(8,128)(2,1)S(1)} %get-tuple-element.32), channel_id=1, source_target_pairs={{0,6},{2,4},{4,2},{6,0},{8,14},{10,12},{12,10},{14,8},{1,7},{3,5},... | collective-permute-start | bytes 307208 | tf_op jit(solution)/shard_map/ppermute | solution.py:306
  25.6 7.0 %collective-permute-start.7 = (bf16[400,128]{1,0:T(8,128)(2,1)S(1)}, bf16[400,128]{1,0:T(8,128)(2,1)S(1)}, u32[]{:S(2)}, u32[]{:S(2)}) collective-permute-start(bf16[400,128]{1,0:T(8,128)(2,1)S(1)} %get-tuple-element.33), channel_id=1, source_target_pairs={{0,8},{2,10},{4,12},{6,14},{8,0},{10,2},{12,4},{14,6},{1,9},{3,11}... | collective-permute-start | bytes 307208 | tf_op jit(solution)/shard_map/ppermute | solution.py:306

commit v4 on v3

--- a/solution.py
+++ b/solution.py
@@ -12,9 +12,10 @@
 HD = 128
 BMAX = 16
 MAXLEN = 96
-META = 16
+META = 8
 STEP = 512
 GROUP = 8
+ORDER = (7, 3, 6, 2, 5, 1, 4)
 VMEM_LIMIT = 44 * 1024 * 1024
 PROJECT_LIMIT = 52800000
 
@@ -136,52 +137,73 @@
     )(half, scaled, weight)
 
 
-def pack_kernel(me_ref, keep_ref, recv_ref, send_ref, len_ref, host_ref, *refs):
-    outs, slot_ref, start_ref = refs[:-2], refs[-2], refs[-1]
-    rows, width = keep_ref.shape
-    prompts = len_ref.shape[1]
-    me = me_ref[0]
+def pack_blocks(turns, kv, me, len_ref, host_ref, outs, slot_ref, start_ref):
+    rows, width = kv.shape
     start = 0
-    for i in range(prompts):
+    for i in range(len_ref.shape[1]):
         turn = host_ref[0, i] ^ me
         slot_ref[turn] = i
         start_ref[turn] = start
         start = start + len_ref[0, i]
+    lane = lax.broadcasted_iota(jnp.int32, (META, HD), 1)
+    row_at = lax.broadcasted_iota(jnp.int32, (MAXLEN, rows), 1)
+    row_at = row_at - lax.broadcasted_iota(jnp.int32, (MAXLEN, rows), 0)
+    for base in range(0, len(turns), GROUP):
+        part = turns[base : base + GROUP]
+        picks = [(row_at == start_ref[k]).astype(jnp.float32).astype(jnp.bfloat16) for k in part]
+        blocks = jnp.dot(
+            jnp.concatenate(picks, axis=0), kv, preferred_element_type=jnp.float32
+        ).astype(jnp.bfloat16)
+        for i, k in enumerate(part):
+            out = outs[base + i]
+            for g in range(width // HD):
+                out[g * MAXLEN : (g + 1) * MAXLEN, :] = blocks[
+                    i * MAXLEN : (i + 1) * MAXLEN, g * HD : (g + 1) * HD
+                ]
+            slot = slot_ref[k]
+            meta = jnp.where(lane == 0, slot, jnp.where(lane == 1, len_ref[0, slot], 0))
+            out[width // HD * MAXLEN :, :] = meta.astype(jnp.float32).astype(jnp.bfloat16)
+
+
+def pack_first_kernel(me_ref, keep_ref, recv_ref, send_ref, len_ref, host_ref, kv_ref, *refs, turns):
+    width = keep_ref.shape[1]
     squares = jnp.sum(recv_ref[:, width:] + send_ref[:, width:], axis=1, keepdims=True)
     inverse = lax.rsqrt(squares / D + 1e-05)
     kv = ((keep_ref[...] + recv_ref[:, :width]) * inverse).astype(jnp.bfloat16)
-    lane = lax.broadcasted_iota(jnp.int32, (META, HD), 1)
-    row_at = lax.broadcasted_iota(jnp.int32, (MAXLEN, rows), 1)
-    row_at = row_at - lax.broadcasted_iota(jnp.int32, (MAXLEN, rows), 0)
-    for base in range(0, prompts, GROUP):
-        turns = range(base, min(base + GROUP, prompts))
-        picks = [(row_at == start_ref[k]).astype(jnp.float32).astype(jnp.bfloat16) for k in turns]
-        blocks = jnp.dot(
-            jnp.concatenate(picks, axis=0), kv, preferred_element_type=jnp.float32
-        ).astype(jnp.bfloat16)
-        for k in turns:
-            at = (k - base) * MAXLEN
-            for g in range(width // HD):
-                outs[k][g * MAXLEN : (g + 1) * MAXLEN, :] = blocks[
-                    at : at + MAXLEN, g * HD : (g + 1) * HD
-                ]
-            slot = slot_ref[k]
-            meta = jnp.where(lane == 0, slot, jnp.where(lane == 1, len_ref[0, slot], 0))
-            outs[k][width // HD * MAXLEN :, :] = meta.astype(jnp.float32).astype(jnp.bfloat16)
-
-
-def pack(me, keep, recv, send, lengths, decode_host, sections):
-    width = keep.shape[1]
-    height = width // HD * MAXLEN + META
-    return pl.pallas_call(
-        pack_kernel,
-        out_shape=[jax.ShapeDtypeStruct((height, HD), jnp.bfloat16)] * sections,
+    kv_ref[...] = kv
+    pack_blocks(turns, kv, me_ref[0], len_ref, host_ref, refs[:-2], refs[-2], refs[-1])
+
+
+def pack_rest_kernel(me_ref, kv_ref, len_ref, host_ref, *refs, turns):
+    pack_blocks(turns, kv_ref[...], me_ref[0], len_ref, host_ref, refs[:-2], refs[-2], refs[-1])
+
+
+def pack(me, keep, recv, send, lengths, decode_host, sections, turns):
+    rows, width = keep.shape
+    block = jax.ShapeDtypeStruct((width // HD * MAXLEN + META, HD), jnp.bfloat16)
+    scratch = [pltpu.SMEM((sections,), jnp.int32), pltpu.SMEM((sections,), jnp.int32)]
+    params = pltpu.CompilerParams(vmem_limit_bytes=VMEM_LIMIT)
+    kv, *front = pl.pallas_call(
+        functools.partial(pack_first_kernel, turns=turns),
+        out_shape=[jax.ShapeDtypeStruct((rows, width), jnp.bfloat16)] + [block] * len(turns),
         in_specs=[SMEM, VMEM, VMEM, VMEM, SMEM, SMEM],
-        out_specs=[VMEM] * sections,
-        scratch_shapes=[pltpu.SMEM((sections,), jnp.int32), pltpu.SMEM((sections,), jnp.int32)],
-        compiler_params=pltpu.CompilerParams(vmem_limit_bytes=VMEM_LIMIT),
-        name="pack",
+        out_specs=[VMEM] * (1 + len(turns)),
+        scratch_shapes=scratch,
+        compiler_params=params,
+        name="pack_first",
     )(me, keep, recv, send, lengths, decode_host)
+    others = [k for k in range(sections) if k not in turns]
+    rest = pl.pallas_call(
+        functools.partial(pack_rest_kernel, turns=others),
+        out_shape=[block] * len(others),
+        in_specs=[SMEM, VMEM, SMEM, SMEM],
+        out_specs=[VMEM] * len(others),
+        scratch_shapes=scratch,
+        compiler_params=params,
+        cost_estimate=pl.CostEstimate(flops=1 << 24, bytes_accessed=4 << 20, transcendentals=0),
+        name="pack_rest",
+    )(me, kv, lengths, decode_host)
+    return dict(zip(list(turns) + others, list(front) + list(rest)))
 
 
 def attend_blocks(blocks, count_ref, q_ref, score_ref, value_ref, acc_ref):
@@ -300,18 +322,16 @@
     send, scaled = project_send(1 - mine, tokens, gain, kv_weight)
     recv = lax.ppermute(send, "tensor", [(0, 1), (1, 0)])
     keep = project_keep(mine, scaled, kv_weight)
-    blocks = pack(me, keep, recv, send, lengths, decode_host, sections)
+    front = (sections - 1, sections - 2)
+    blocks = pack(me, keep, recv, send, lengths, decode_host, sections, front)
     got = {}
     for k in range(1, sections):
         got[k] = lax.ppermute(blocks[k], "section", [(s, s ^ k) for s in range(sections)])
     q, score, value, acc = attend_first(beam_query, beam_newkv, beam_counts, blocks[0])
-    cut = sections // 2
-    near = [k for k in range(1, cut)]
-    order = [sections - 1] + [k for pair in zip(range(sections - 2, cut, -1), near) for k in pair]
-    order = order + [near[-1], cut]
-    early = [got[k] for k in order[:-2]]
-    late = [got[k] for k in order[-2:]]
-    (acc,) = attend_later(beam_counts, q, score, value, acc, early, None)
+    order = ORDER if sections == len(ORDER) + 1 else tuple(range(sections - 1, 0, -1))
+    for part in (order[:3], order[3:-1]):
+        (acc,) = attend_later(beam_counts, q, score, value, acc, [got[k] for k in part], None)
+    late = [got[order[-1]]]
     out_shape = jax.ShapeDtypeStruct(beam_query.shape, jnp.bfloat16)
     return attend_later(beam_counts, q, score, value, acc, late, out_shape)[1]
 

time: 35.1 us -> 34.3 us (0.977)
  starting transfers between devices: 19.6 us -> 15.7 us
  waiting for transfers between devices: 0.89 us -> 2.52 us
  Pallas kernels: 13.5 us -> 15 us
    ppermute x7, starting transfers between devices: 19.1 us -> 15.2 us  [per_device(): lax.ppermute(blocks[k], 'section', [(s, s ^ k) for s in range(sections)])]
    ppermute x7, waiting for transfers between devices: 0.89 us -> 2.52 us  [per_device(): lax.ppermute(blocks[k], 'section', [(s, s ^ k) for s in range(sections)])]
    pallas_call x2 -> x3, Pallas kernels: 4.57 us -> 5.32 us  [attend_later(): pl.pallas_call(functools.partial(later_kernel, n_blocks=len(blocks), last...]
    pallas_call x1 -> x2, Pallas kernels: 1.02 us -> 1.73 us  [the longest x1 0.87 us: pack(): pl.pallas_call(functools.partial(pack_first_kernel, turns=turns), out_sha...]
  transfers between devices with their start and end apart: 8 -> 8, of which waited for: 1 -> 3; matrix products, arithmetic and copies ran while one was open for 0% -> 0% of each run, Pallas kernels for 19% -> 25%
where the time goes in v4:
time: 34.3 us; the launch traced here: 34 us
  starting transfers between devices  15.7 us (46%)
  Pallas kernels  15 us (44%)
  waiting for transfers between devices  2.52 us (7%)
  local copies, waits for them, and re-layouts  0.72 us (2%)
    ppermute x7, starting transfers between devices, per_device(): lax.ppermute(blocks[k], 'section', [(s, s ^ k) for s in range(sections)])  15.2 us
    pallas_call x3, Pallas kernels, attend_later(): pl.pallas_call(functools.partial(later_kernel, n_blocks=len(blocks), last...  5.32 us
    pallas_call x1, Pallas kernels, project_send(): pl.pallas_call(project_send_kernel, out_shape=(jax.ShapeDtypeStruct((rows...  3.79 us
    pallas_call x1, Pallas kernels, project_keep(): pl.pallas_call(project_keep_kernel, out_shape=jax.ShapeDtypeStruct((rows,...  2.76 us
    ppermute x7, waiting for transfers between devices, per_device(): lax.ppermute(blocks[k], 'section', [(s, s ^ k) for s in range(sections)])  2.52 us
    pallas_call x1, Pallas kernels, attend_first(): pl.pallas_call(first_kernel, out_shape=(tall, tall, jax.ShapeDtypeStruct(...  1.38 us
    pallas_call x1, Pallas kernels, pack(): pl.pallas_call(functools.partial(pack_first_kernel, turns=turns), out_sha...  0.87 us
    pallas_call x1, Pallas kernels, pack(): pl.pallas_call(functools.partial(pack_rest_kernel, turns=others), out_sha...  0.86 us
  transfers between devices with their start and end apart: 8, of which 3 were waited for; matrix products, arithmetic and copies ran while one was open for 0% of the time, Pallas kernels for 25%

profile of v4, /device:TPU:0, one launch (start us, length us, event | category | flops | bytes accessed | tf_op | source)
XLA Modules:
  0.0 34.0 jit_solution(8335712221273468439)
XLA Ops:
  0.0 0.7 %copy-done.2 = bf16[4096]{0:T(1024)(128)(2,1)S(1)} copy-done((bf16[4096]{0:T(1024)(128)(2,1)S(1)}, bf16[4096]{0:T(1024)(128)(2,1)}, u32[]{:S(2)}) %copy-start.2) | copy-done | bytes 8216
  0.7 3.8 %project_send.1 = (f32[256,640]{1,0:T(8,128)S(1)}, bf16[256,4096]{1,0:T(8,128)(2,1)S(1)}) custom-call(s32[1]{0:T(128)S(6)} %sub.3.half_ref, bf16[256,4096]{1,0:T(8,128)(2,1)} %tok_ref.1, bf16[32,128]{1,0:T(8,128)(2,1)S(1)} %bitcast.3, bf16[4096,1024]{1,0:T(8,128)(2,1)} %w_ref.3), custom_call_target="tpu_custom_call" | custom-call | flops 1073741824 | bytes 6815744 | tf_op jit(solution)/shard_map/project_send/pallas_call | solution.py:101
  4.5 0.5 %collective-permute-start = (f32[256,640]{1,0:T(8,128)S(1)}, f32[256,640]{1,0:T(8,128)S(1)}, u32[]{:S(2)}, u32[]{:S(2)}) collective-permute-start(f32[256,640]{1,0:T(8,128)S(1)} %get-tuple-element.22.send_ref), channel_id=1, source_target_pairs={{0,1},{1,0},{2,3},{3,2},{4,5},{5,4},{6,7},{7,6},{8,9},{9,8},{10,11... | collective-permute-start | bytes 1966088 | tf_op jit(solution)/shard_map/ppermute | solution.py:323
  5.0 2.8 %project_keep.1.keep_ref = f32[256,512]{1,0:T(8,128)S(1)} custom-call(s32[1]{0:T(128)} %bitcast.1.half_ref, bf16[256,4096]{1,0:T(8,128)(2,1)S(1)} %get-tuple-element.21.scaled_ref, bf16[4096,1024]{1,0:T(8,128)(2,1)} %w_ref.3), custom_call_target="tpu_custom_call" | custom-call | flops 1073741824 | bytes 6815744 | tf_op jit(solution)/shard_map/project_keep/pallas_call | solution.py:125
  7.8 0.0 copy-start
  7.8 0.0 copy-start.1
  7.8 0.0 copy-start.3
  7.8 0.0 collective-permute-done.recv_ref
  7.8 0.0 copy-done.4
  7.8 0.0 copy-done.5
  7.9 0.9 %pack_first.1 = (bf16[256,512]{1,0:T(8,128)(2,1)S(1)}, bf16[392,128]{1,0:T(8,128)(2,1)S(1)}, bf16[392,128]{1,0:T(8,128)(2,1)S(1)}) custom-call(s32[1]{0:T(128)} %bitcast.me_ref, f32[256,512]{1,0:T(8,128)S(1)} %project_keep.1.keep_ref, f32[256,640]{1,0:T(8,128)S(1)} %collective-permute-done.recv_ref, f32[256,640]{1,0:T(8,128)S(1)} %get-tuple-element.22.send_ref, ...), custom_call_target="tpu_custom_call" | custom-call | tf_op jit(solution)/shard_map/pack_first/pallas_call | solution.py:186
  8.7 5.6 %collective-permute-start.1 = (bf16[392,128]{1,0:T(8,128)(2,1)S(1)}, bf16[392,128]{1,0:T(8,128)(2,1)S(1)}, u32[]{:S(2)}, u32[]{:S(2)}) collective-permute-start(bf16[392,128]{1,0:T(8,128)(2,1)S(1)} %get-tuple-element.29), channel_id=1, source_target_pairs={{0,14},{2,12},{4,10},{6,8},{8,6},{10,4},{12,2},{14,0},{1,15},{3,13... | collective-permute-start | bytes 301064 | tf_op jit(solution)/shard_map/ppermute | solution.py:329
  14.4 0.2 collective-permute-start.3
  14.6 0.9 %pack_rest.1 = (bf16[392,128]{1,0:T(8,128)(2,1)S(1)}, bf16[392,128]{1,0:T(8,128)(2,1)S(1)}, bf16[392,128]{1,0:T(8,128)(2,1)S(1)}, bf16[392,128]{1,0:T(8,128)(2,1...) custom-call(s32[1]{0:T(128)} %bitcast.me_ref, bf16[256,512]{1,0:T(8,128)(2,1)S(1)} %get-tuple-element.23.kv_ref, ...), custom_call_target="tpu_custom_call" | custom-call | flops 16777216 | bytes 4194304 | tf_op jit(solution)/shard_map/pack_rest/pallas_call | solution.py:196
  15.5 0.1 collective-permute-start.2
  15.5 1.9 %collective-permute-start.4 = (bf16[392,128]{1,0:T(8,128)(2,1)S(1)}, bf16[392,128]{1,0:T(8,128)(2,1)S(1)}, u32[]{:S(2)}, u32[]{:S(2)}) collective-permute-start(bf16[392,128]{1,0:T(8,128)(2,1)S(1)} %get-tuple-element.32), channel_id=1, source_target_pairs={{0,4},{2,6},{4,0},{6,2},{8,12},{10,14},{12,8},{14,10},{1,5},{3,7},... | collective-permute-start | bytes 301064 | tf_op jit(solution)/shard_map/ppermute | solution.py:329
  17.4 3.2 %collective-permute-start.5 = (bf16[392,128]{1,0:T(8,128)(2,1)S(1)}, bf16[392,128]{1,0:T(8,128)(2,1)S(1)}, u32[]{:S(2)}, u32[]{:S(2)}) collective-permute-start(bf16[392,128]{1,0:T(8,128)(2,1)S(1)} %get-tuple-element.33), channel_id=1, source_target_pairs={{0,10},{2,8},{4,14},{6,12},{8,2},{10,0},{12,6},{14,4},{1,11},{3,9}... | collective-permute-start | bytes 301064 | tf_op jit(solution)/shard_map/ppermute | solution.py:329
  20.6 0.0 collective-permute-done.1.refs_0_
  20.6 0.6 %collective-permute-start.6 = (bf16[392,128]{1,0:T(8,128)(2,1)S(1)}, bf16[392,128]{1,0:T(8,128)(2,1)S(1)}, u32[]{:S(2)}, u32[]{:S(2)}) collective-permute-start(bf16[392,128]{1,0:T(8,128)(2,1)S(1)} %get-tuple-element.34), channel_id=1, source_target_pairs={{0,2},{2,0},{4,6},{6,4},{8,10},{10,8},{12,14},{14,12},{1,3},{3,1},... | collective-permute-start | bytes 301064 | tf_op jit(solution)/shard_map/ppermute | solution.py:329
  21.2 0.7 %collective-permute-done.3.refs_2_ = bf16[392,128]{1,0:T(8,128)(2,1)S(1)} collective-permute-done((bf16[392,128]{1,0:T(8,128)(2,1)S(1)}, bf16[392,128]{1,0:T(8,128)(2,1)S(1)}, u32[]{:S(2)}, u32[]{:S(2)}) %collective-permute-start.3) | collective-permute-done | bytes 100384 | tf_op jit(solution)/shard_map/ppermute | solution.py:329
  21.9 3.6 %collective-permute-start.7 = (bf16[392,128]{1,0:T(8,128)(2,1)S(1)}, bf16[392,128]{1,0:T(8,128)(2,1)S(1)}, u32[]{:S(2)}, u32[]{:S(2)}) collective-permute-start(bf16[392,128]{1,0:T(8,128)(2,1)S(1)} %get-tuple-element.35), channel_id=1, source_target_pairs={{0,8},{2,10},{4,12},{6,14},{8,0},{10,2},{12,4},{14,6},{1,9},{3,11}... | collective-permute-start | bytes 301064 | tf_op jit(solution)/shard_map/ppermute | solution.py:329
  25.4 0.0 copy-done
  25.4 0.0 copy-done.1
  25.5 1.4 %attend_first.1 = (f32[16,96,128]{2,1,0:T(8,128)S(1)}, f32[16,96,128]{2,1,0:T(8,128)S(1)}, f32[2,96,128]{2,1,0:T(8,128)S(1)}, f32[16,96,128]{2,1,0:T(8,128)S(1)}) custom-call(bf16[80,2048]{1,0:T(8,128)(2,1)S(1)} %copy-done, bf16[80,512]{1,0:T(8,128)(2,1)S(1)} %copy-done.1, s32[1,8]{1,0:T(1,128)S(1)} %copy-done.3, ...), custom_call_target="tpu_custom_call" | custom-call | flops 16777216 | bytes 4194304 | tf_op jit(solution)/shard_map/attend_first/pallas_call | solution.py:277
  26.8 0.0 collective-permute-done.2.refs_1_
  26.8 1.7 %attend_more.2.acc_in = f32[16,96,128]{2,1,0:T(8,128)S(1)} custom-call(s32[1,8]{1,0:T(1,128)S(1)} %copy-done.3, f32[16,96,128]{2,1,0:T(8,128)S(1)} %get-tuple-element.25.q_ref, f32[16,96,128]{2,1,0:T(8,128)S(1)} %get-tuple-element.26.score_ref, f32[2,96,128]{2,1,0:T(8,128)S(1)} %get-tuple-element.27.value_ref, ...), custom_call_target="tpu_custom_call", output_to_operand_aliasing={{}: (4, {})} | custom-call | flops 16777216 | bytes 4194304 | tf_op jit(solution)/shard_map/attend_more/pallas_call | solution.py:305
  28.5 0.0 collective-permute-done.4.refs_0_
  28.5 1.7 %collective-permute-done.5.refs_1_ = bf16[392,128]{1,0:T(8,128)(2,1)S(1)} collective-permute-done((bf16[392,128]{1,0:T(8,128)(2,1)S(1)}, bf16[392,128]{1,0:T(8,128)(2,1)S(1)}, u32[]{:S(2)}, u32[]{:S(2)}) %collective-permute-start.5) | collective-permute-done | bytes 100384 | tf_op jit(solution)/shard_map/ppermute | solution.py:329
  30.3 0.0 collective-permute-done.6.refs_2_
  30.3 1.7 %attend_more.3.acc_in = f32[16,96,128]{2,1,0:T(8,128)S(1)} custom-call(s32[1,8]{1,0:T(1,128)S(1)} %copy-done.3, f32[16,96,128]{2,1,0:T(8,128)S(1)} %get-tuple-element.25.q_ref, f32[16,96,128]{2,1,0:T(8,128)S(1)} %get-tuple-element.26.score_ref, f32[2,96,128]{2,1,0:T(8,128)S(1)} %get-tuple-element.27.value_ref, ...), custom_call_target="tpu_custom_call", output_to_operand_aliasing={{}: (4, {})} | custom-call | flops 16777216 | bytes 4194304 | tf_op jit(solution)/shard_map/attend_more/pallas_call | solution.py:305
  31.9 0.1 collective-permute-done.7.refs_0_
  32.1 2.0 %attend_last.1 = (f32[16,96,128]{2,1,0:T(8,128)S(1)}, bf16[80,2048]{1,0:T(8,128)(2,1)}) custom-call(s32[1,8]{1,0:T(1,128)S(1)} %copy-done.3, f32[16,96,128]{2,1,0:T(8,128)S(1)} %get-tuple-element.25.q_ref, f32[16,96,128]{2,1,0:T(8,128)S(1)} %get-tuple-element.26.score_ref, ...), custom_call_target="tpu_custom_call", output_to_operand_aliasing={{0}: (4, {})} | custom-call | flops 16777216 | bytes 4194304 | tf_op jit(solution)/shard_map/attend_last/pallas_call | solution.py:305
  (4 shorter events, 0.0 us)
Async XLA Ops:
  0.0 0.7 %copy-start.2 = (bf16[4096]{0:T(1024)(128)(2,1)S(1)}, bf16[4096]{0:T(1024)(128)(2,1)}, u32[]{:S(2)}) copy-start(bf16[4096]{0:T(1024)(128)(2,1)} %param.9) | copy-start | bytes 24580
  4.5 3.3 %collective-permute-start = (f32[256,640]{1,0:T(8,128)S(1)}, f32[256,640]{1,0:T(8,128)S(1)}, u32[]{:S(2)}, u32[]{:S(2)}) collective-permute-start(f32[256,640]{1,0:T(8,128)S(1)} %get-tuple-element.22.send_ref), channel_id=1, source_target_pairs={{0,1},{1,0},{2,3},{3,2},{4,5},{5,4},{6,7},{7,6},{8,9},{9,8},{10,11... | collective-permute-start | bytes 1966088 | tf_op jit(solution)/shard_map/ppermute | solution.py:323
  5.0 2.8 %copy-start.4 = (s32[1,8]{1,0:T(1,128)S(1)}, s32[1,8]{1,0:T(1,128)}, u32[]{:S(2)}) copy-start(s32[1,8]{1,0:T(1,128)} %len_ref.3) | copy-start | bytes 100
  5.0 2.8 %copy-start.5 = (s32[1,8]{1,0:T(1,128)S(1)}, s32[1,8]{1,0:T(1,128)}, u32[]{:S(2)}) copy-start(s32[1,8]{1,0:T(1,128)} %host_ref.3) | copy-start | bytes 100
  7.8 17.7 %copy-start = (bf16[80,2048]{1,0:T(8,128)(2,1)S(1)}, bf16[80,2048]{1,0:T(8,128)(2,1)}, u32[]{:S(2)}) copy-start(bf16[80,2048]{1,0:T(8,128)(2,1)} %query_ref.1) | copy-start | bytes 983044
  7.8 17.7 %copy-start.1 = (bf16[80,512]{1,0:T(8,128)(2,1)S(1)}, bf16[80,512]{1,0:T(8,128)(2,1)}, u32[]{:S(2)}) copy-start(bf16[80,512]{1,0:T(8,128)(2,1)} %own_ref.1) | copy-start | bytes 245764
  7.8 17.6 %copy-start.3 = (s32[1,8]{1,0:T(1,128)S(1)}, s32[1,8]{1,0:T(1,128)}, u32[]{:S(2)}) copy-start(s32[1,8]{1,0:T(1,128)} %count_ref.7) | copy-start | bytes 100
  8.7 11.9 %collective-permute-start.1 = (bf16[392,128]{1,0:T(8,128)(2,1)S(1)}, bf16[392,128]{1,0:T(8,128)(2,1)S(1)}, u32[]{:S(2)}, u32[]{:S(2)}) collective-permute-start(bf16[392,128]{1,0:T(8,128)(2,1)S(1)} %get-tuple-element.29), channel_id=1, source_target_pairs={{0,14},{2,12},{4,10},{6,8},{8,6},{10,4},{12,2},{14,0},{1,15},{3,13... | collective-permute-start | bytes 301064 | tf_op jit(solution)/shard_map/ppermute | solution.py:329
  14.4 7.5 %collective-permute-start.3 = (bf16[392,128]{1,0:T(8,128)(2,1)S(1)}, bf16[392,128]{1,0:T(8,128)(2,1)S(1)}, u32[]{:S(2)}, u32[]{:S(2)}) collective-permute-start(bf16[392,128]{1,0:T(8,128)(2,1)S(1)} %get-tuple-element.31), channel_id=1, source_target_pairs={{0,12},{2,14},{4,8},{6,10},{8,4},{10,6},{12,0},{14,2},{1,13},{3,15... | collective-permute-start | bytes 301064 | tf_op jit(solution)/shard_map/ppermute | solution.py:329
  15.5 11.4 %collective-permute-start.2 = (bf16[392,128]{1,0:T(8,128)(2,1)S(1)}, bf16[392,128]{1,0:T(8,128)(2,1)S(1)}, u32[]{:S(2)}, u32[]{:S(2)}) collective-permute-start(bf16[392,128]{1,0:T(8,128)(2,1)S(1)} %get-tuple-element.30), channel_id=1, source_target_pairs={{0,6},{2,4},{4,2},{6,0},{8,14},{10,12},{12,10},{14,8},{1,7},{3,5},... | collective-permute-start | bytes 301064 | tf_op jit(solution)/shard_map/ppermute | solution.py:329
  15.5 13.0 %collective-permute-start.4 = (bf16[392,128]{1,0:T(8,128)(2,1)S(1)}, bf16[392,128]{1,0:T(8,128)(2,1)S(1)}, u32[]{:S(2)}, u32[]{:S(2)}) collective-permute-start(bf16[392,128]{1,0:T(8,128)(2,1)S(1)} %get-tuple-element.32), channel_id=1, source_target_pairs={{0,4},{2,6},{4,0},{6,2},{8,12},{10,14},{12,8},{14,10},{1,5},{3,7},... | collective-permute-start | bytes 301064 | tf_op jit(solution)/shard_map/ppermute | solution.py:329
  17.4 12.9 %collective-permute-start.5 = (bf16[392,128]{1,0:T(8,128)(2,1)S(1)}, bf16[392,128]{1,0:T(8,128)(2,1)S(1)}, u32[]{:S(2)}, u32[]{:S(2)}) collective-permute-start(bf16[392,128]{1,0:T(8,128)(2,1)S(1)} %get-tuple-element.33), channel_id=1, source_target_pairs={{0,10},{2,8},{4,14},{6,12},{8,2},{10,0},{12,6},{14,4},{1,11},{3,9}... | collective-permute-start | bytes 301064 | tf_op jit(solution)/shard_map/ppermute | solution.py:329
  20.6 9.7 %collective-permute-start.6 = (bf16[392,128]{1,0:T(8,128)(2,1)S(1)}, bf16[392,128]{1,0:T(8,128)(2,1)S(1)}, u32[]{:S(2)}, u32[]{:S(2)}) collective-permute-start(bf16[392,128]{1,0:T(8,128)(2,1)S(1)} %get-tuple-element.34), channel_id=1, source_target_pairs={{0,2},{2,0},{4,6},{6,4},{8,10},{10,8},{12,14},{14,12},{1,3},{3,1},... | collective-permute-start | bytes 301064 | tf_op jit(solution)/shard_map/ppermute | solution.py:329
  21.9 10.2 %collective-permute-start.7 = (bf16[392,128]{1,0:T(8,128)(2,1)S(1)}, bf16[392,128]{1,0:T(8,128)(2,1)S(1)}, u32[]{:S(2)}, u32[]{:S(2)}) collective-permute-start(bf16[392,128]{1,0:T(8,128)(2,1)S(1)} %get-tuple-element.35), channel_id=1, source_target_pairs={{0,8},{2,10},{4,12},{6,14},{8,0},{10,2},{12,4},{14,6},{1,9},{3,11}... | collective-permute-start | bytes 301064 | tf_op jit(solution)/shard_map/ppermute | solution.py:329

commit v5 on v4

--- a/solution.py
+++ b/solution.py
@@ -13,7 +13,7 @@
 BMAX = 16
 MAXLEN = 96
 META = 8
-STEP = 512
+STEP = 1024
 GROUP = 8
 ORDER = (7, 3, 6, 2, 5, 1, 4)
 VMEM_LIMIT = 44 * 1024 * 1024
@@ -27,59 +27,56 @@
 def weight_copy(w_ref, w_buf, sem, half, c):
     width = w_buf.shape[2]
     columns = pl.ds(pl.multiple_of(half * width, width), width)
-    return pltpu.make_async_copy(w_ref.at[pl.ds(c * STEP, STEP), columns], w_buf.at[c], sem.at[c])
-
-
-def project_send_kernel(half_ref, tok_ref, gain_ref, w_ref, out_ref, scaled_ref, tok_buf, w_buf, tok_sem, w_sem):
+    rows = pl.ds(pl.multiple_of(c * STEP, STEP), STEP)
+    return pltpu.make_async_copy(w_ref.at[rows, columns], w_buf.at[c], sem.at[c])
+
+
+def project_send_kernel(half_ref, tok_ref, gain_hbm, w_ref, out_ref, scaled_ref, gain_buf, gain_ref, tok_buf, w_buf, gain_sem, tok_sem, w_sem):
     half = half_ref[0]
     steps = w_buf.shape[0]
     width = w_buf.shape[2]
     blocks = STEP // HD
 
     def token_copy(c):
-        return pltpu.make_async_copy(tok_ref.at[:, pl.ds(c * STEP, STEP)], tok_buf.at[c], tok_sem.at[c])
-
-    def scale(c):
-        token_copy(c).wait()
-        squares = None
-        for b in range(blocks):
-            at = c * blocks + b
-            tok = tok_buf[c, :, b * HD : (b + 1) * HD].astype(jnp.float32)
-            scaled_ref[:, at * HD : (at + 1) * HD] = (tok * gain[at : at + 1, :]).astype(jnp.bfloat16)
-            squares = tok * tok if squares is None else squares + tok * tok
-        if c == 0:
-            out_ref[:, width:] = squares
-        else:
-            out_ref[:, width:] += squares
-
-    for c in range(steps):
+        columns = pl.ds(pl.multiple_of(c * STEP, STEP), STEP)
+        return pltpu.make_async_copy(tok_ref.at[:, columns], tok_buf.at[c], tok_sem.at[c])
+
+    def begin(c, _):
         token_copy(c).start()
         weight_copy(w_ref, w_buf, w_sem, half, c).start()
-    gain = gain_ref[...].astype(jnp.float32)
-    scale(0)
-    for c in range(steps):
+        return _
+
+    def step(c, _):
+        token_copy(c).wait()
+        squares = out_ref[:, width:]
+        for b in range(blocks):
+            tok = tok_buf[c, :, b * HD : (b + 1) * HD].astype(jnp.float32)
+            scale = gain_ref[pl.ds(c * blocks + b, 1), :]
+            scaled_ref[c, :, b * HD : (b + 1) * HD] = (tok * scale).astype(jnp.bfloat16)
+            squares = squares + tok * tok
+        out_ref[:, width:] = squares
         weight_copy(w_ref, w_buf, w_sem, half, c).wait()
-        if c + 1 < steps:
-            scale(c + 1)
-        part = jnp.dot(
-            scaled_ref[:, c * STEP : (c + 1) * STEP], w_buf[c], preferred_element_type=jnp.float32
-        )
-        if c == 0:
-            out_ref[:, :width] = part
-        else:
-            out_ref[:, :width] += part
+        out_ref[:, :width] += jnp.dot(scaled_ref[c], w_buf[c], preferred_element_type=jnp.float32)
+        return _
+
+    gain_copy = pltpu.make_async_copy(gain_hbm, gain_buf, gain_sem.at[0])
+    gain_copy.start()
+    out_ref[...] = jnp.zeros_like(out_ref)
+    lax.fori_loop(0, steps, begin, 0)
+    gain_copy.wait()
+    gain_ref[...] = gain_buf[...].astype(jnp.float32)
+    lax.fori_loop(0, steps, step, 0)
 
 
 def project_keep_kernel(half_ref, scaled_ref, w_ref, out_ref, w_buf, w_sem):
     half = half_ref[0]
     steps = w_buf.shape[0]
+
     for c in range(steps):
         weight_copy(w_ref, w_buf, w_sem, half, c).start()
     for c in range(steps):
         weight_copy(w_ref, w_buf, w_sem, half, c).wait()
-        part = jnp.dot(
-            scaled_ref[:, c * STEP : (c + 1) * STEP], w_buf[c], preferred_element_type=jnp.float32
-        )
+        part = jnp.dot(scaled_ref[c], w_buf[c], preferred_element_type=jnp.float32)
         if c == 0:
             out_ref[...] = part
         else:
@@ -102,13 +99,16 @@
         project_send_kernel,
         out_shape=(
             jax.ShapeDtypeStruct((rows, width + HD), jnp.float32),
-            jax.ShapeDtypeStruct((rows, depth), jnp.bfloat16),
+            jax.ShapeDtypeStruct((steps, rows, STEP), jnp.bfloat16),
         ),
-        in_specs=[SMEM, HBM, VMEM, HBM],
+        in_specs=[SMEM, HBM, HBM, HBM],
         out_specs=(VMEM, VMEM),
         scratch_shapes=[
+            pltpu.VMEM(gain.shape, jnp.bfloat16),
+            pltpu.VMEM(gain.shape, jnp.float32),
             pltpu.VMEM((steps, rows, STEP), jnp.bfloat16),
             pltpu.VMEM((steps, STEP, width), jnp.bfloat16),
+            pltpu.SemaphoreType.DMA((1,)),
             pltpu.SemaphoreType.DMA((steps,)),
             pltpu.SemaphoreType.DMA((steps,)),
         ],
@@ -119,9 +119,9 @@
 
 
 def project_keep(half, scaled, weight):
-    rows, depth = scaled.shape
+    steps, rows, _ = scaled.shape
+    depth = steps * STEP
     width = weight.shape[1] // 2
-    steps = depth // STEP
     return pl.pallas_call(
         project_keep_kernel,
         out_shape=jax.ShapeDtypeStruct((rows, width), jnp.float32),
@@ -318,7 +318,7 @@
     sections = lax.axis_size("section")
     mine = lax.axis_index("tensor").astype(jnp.int32).reshape(1)
     me = lax.axis_index("section").astype(jnp.int32).reshape(1)
-    gain = norm_gain.reshape(-1, HD)
+    gain = pltpu.with_memory_space_constraint(norm_gain.reshape(-1, HD), pltpu.HBM)
     send, scaled = project_send(1 - mine, tokens, gain, kv_weight)
     recv = lax.ppermute(send, "tensor", [(0, 1), (1, 0)])
     keep = project_keep(mine, scaled, kv_weight)

time: 34.3 us -> 33.7 us (0.983)
  local copies, waits for them, and re-layouts: 0.72 us -> 0.03 us
    unnamed x12 -> x10, local copies, waits for them, and re-layouts: 0.72 us -> 0.03 us
where the time goes in v5:
time: 33.7 us; the launch traced here: 33.4 us
  starting transfers between devices  15.7 us (47%)
  Pallas kernels  15.1 us (45%)
  waiting for transfers between devices  2.51 us (7%)
    ppermute x7, starting transfers between devices, per_device(): lax.ppermute(blocks[k], 'section', [(s, s ^ k) for s in range(sections)])  15.2 us
    pallas_call x3, Pallas kernels, attend_later(): pl.pallas_call(functools.partial(later_kernel, n_blocks=len(blocks), last...  5.33 us
    pallas_call x1, Pallas kernels, project_send(): pl.pallas_call(project_send_kernel, out_shape=(jax.ShapeDtypeStruct((rows...  3.96 us
    pallas_call x1, Pallas kernels, project_keep(): pl.pallas_call(project_keep_kernel, out_shape=jax.ShapeDtypeStruct((rows,...  2.69 us
    ppermute x7, waiting for transfers between devices, per_device(): lax.ppermute(blocks[k], 'section', [(s, s ^ k) for s in range(sections)])  2.51 us
    pallas_call x1, Pallas kernels, attend_first(): pl.pallas_call(first_kernel, out_shape=(tall, tall, jax.ShapeDtypeStruct(...  1.38 us
    pallas_call x1, Pallas kernels, pack(): pl.pallas_call(functools.partial(pack_first_kernel, turns=turns), out_sha...  0.87 us
    pallas_call x1, Pallas kernels, pack(): pl.pallas_call(functools.partial(pack_rest_kernel, turns=others), out_sha...  0.85 us
  transfers between devices with their start and end apart: 8, of which 3 were waited for; matrix products, arithmetic and copies ran while one was open for 0% of the time, Pallas kernels for 25%

profile of v5, /device:TPU:0, one launch (start us, length us, event | category | flops | bytes accessed | tf_op | source)
XLA Modules:
  0.0 33.4 jit_solution(16975371976964161367)
XLA Ops:
  0.0 4.0 %project_send.1 = (f32[256,640]{1,0:T(8,128)S(1)}, bf16[4,256,1024]{2,1,0:T(8,128)(2,1)S(1)}) custom-call(s32[1]{0:T(128)S(6)} %sub.3.half_ref, bf16[256,4096]{1,0:T(8,128)(2,1)} %tok_ref.1, bf16[32,128]{1,0:T(8,128)(2,1)} %bitcast.3, bf16[4096,1024]{1,0:T(8,128)(2,1)} %w_ref.3), custom_call_target="tpu_custom_call" | custom-call | flops 1073741824 | bytes 6815744 | tf_op jit(solution)/shard_map/project_send/pallas_call | solution.py:98
  4.0 0.5 %collective-permute-start = (f32[256,640]{1,0:T(8,128)S(1)}, f32[256,640]{1,0:T(8,128)S(1)}, u32[]{:S(2)}, u32[]{:S(2)}) collective-permute-start(f32[256,640]{1,0:T(8,128)S(1)} %get-tuple-element.22.send_ref), channel_id=1, source_target_pairs={{0,1},{1,0},{2,3},{3,2},{4,5},{5,4},{6,7},{7,6},{8,9},{9,8},{10,11... | collective-permute-start | bytes 1966088 | tf_op jit(solution)/shard_map/ppermute | solution.py:323
  4.5 2.7 %project_keep.1.keep_ref = f32[256,512]{1,0:T(8,128)S(1)} custom-call(s32[1]{0:T(128)} %bitcast.1.half_ref, bf16[4,256,1024]{2,1,0:T(8,128)(2,1)S(1)} %get-tuple-element.21.scaled_ref, bf16[4096,1024]{1,0:T(8,128)(2,1)} %w_ref.3), custom_call_target="tpu_custom_call" | custom-call | flops 1073741824 | bytes 6815744 | tf_op jit(solution)/shard_map/project_keep/pallas_call | solution.py:125
  7.2 0.0 copy-start
  7.2 0.0 copy-start.1
  7.2 0.0 copy-start.2
  7.2 0.0 collective-permute-done.recv_ref
  7.2 0.0 copy-done.3
  7.2 0.0 copy-done.4
  7.3 0.9 %pack_first.1 = (bf16[256,512]{1,0:T(8,128)(2,1)S(1)}, bf16[392,128]{1,0:T(8,128)(2,1)S(1)}, bf16[392,128]{1,0:T(8,128)(2,1)S(1)}) custom-call(s32[1]{0:T(128)} %bitcast.me_ref, f32[256,512]{1,0:T(8,128)S(1)} %project_keep.1.keep_ref, f32[256,640]{1,0:T(8,128)S(1)} %collective-permute-done.recv_ref, f32[256,640]{1,0:T(8,128)S(1)} %get-tuple-element.22.send_ref, ...), custom_call_target="tpu_custom_call" | custom-call | tf_op jit(solution)/shard_map/pack_first/pallas_call | solution.py:186
  8.1 5.6 %collective-permute-start.1 = (bf16[392,128]{1,0:T(8,128)(2,1)S(1)}, bf16[392,128]{1,0:T(8,128)(2,1)S(1)}, u32[]{:S(2)}, u32[]{:S(2)}) collective-permute-start(bf16[392,128]{1,0:T(8,128)(2,1)S(1)} %get-tuple-element.29), channel_id=1, source_target_pairs={{0,14},{2,12},{4,10},{6,8},{8,6},{10,4},{12,2},{14,0},{1,15},{3,13... | collective-permute-start | bytes 301064 | tf_op jit(solution)/shard_map/ppermute | solution.py:329
  13.8 0.2 collective-permute-start.3
  14.0 0.9 %pack_rest.1 = (bf16[392,128]{1,0:T(8,128)(2,1)S(1)}, bf16[392,128]{1,0:T(8,128)(2,1)S(1)}, bf16[392,128]{1,0:T(8,128)(2,1)S(1)}, bf16[392,128]{1,0:T(8,128)(2,1...) custom-call(s32[1]{0:T(128)} %bitcast.me_ref, bf16[256,512]{1,0:T(8,128)(2,1)S(1)} %get-tuple-element.23.kv_ref, ...), custom_call_target="tpu_custom_call" | custom-call | flops 16777216 | bytes 4194304 | tf_op jit(solution)/shard_map/pack_rest/pallas_call | solution.py:196
  14.9 0.1 collective-permute-start.2
  14.9 1.9 %collective-permute-start.4 = (bf16[392,128]{1,0:T(8,128)(2,1)S(1)}, bf16[392,128]{1,0:T(8,128)(2,1)S(1)}, u32[]{:S(2)}, u32[]{:S(2)}) collective-permute-start(bf16[392,128]{1,0:T(8,128)(2,1)S(1)} %get-tuple-element.32), channel_id=1, source_target_pairs={{0,4},{2,6},{4,0},{6,2},{8,12},{10,14},{12,8},{14,10},{1,5},{3,7},... | collective-permute-start | bytes 301064 | tf_op jit(solution)/shard_map/ppermute | solution.py:329
  16.8 3.2 %collective-permute-start.5 = (bf16[392,128]{1,0:T(8,128)(2,1)S(1)}, bf16[392,128]{1,0:T(8,128)(2,1)S(1)}, u32[]{:S(2)}, u32[]{:S(2)}) collective-permute-start(bf16[392,128]{1,0:T(8,128)(2,1)S(1)} %get-tuple-element.33), channel_id=1, source_target_pairs={{0,10},{2,8},{4,14},{6,12},{8,2},{10,0},{12,6},{14,4},{1,11},{3,9}... | collective-permute-start | bytes 301064 | tf_op jit(solution)/shard_map/ppermute | solution.py:329
  20.0 0.0 collective-permute-done.1.refs_0_
  20.0 0.6 %collective-permute-start.6 = (bf16[392,128]{1,0:T(8,128)(2,1)S(1)}, bf16[392,128]{1,0:T(8,128)(2,1)S(1)}, u32[]{:S(2)}, u32[]{:S(2)}) collective-permute-start(bf16[392,128]{1,0:T(8,128)(2,1)S(1)} %get-tuple-element.34), channel_id=1, source_target_pairs={{0,2},{2,0},{4,6},{6,4},{8,10},{10,8},{12,14},{14,12},{1,3},{3,1},... | collective-permute-start | bytes 301064 | tf_op jit(solution)/shard_map/ppermute | solution.py:329
  20.6 0.7 %collective-permute-done.3.refs_2_ = bf16[392,128]{1,0:T(8,128)(2,1)S(1)} collective-permute-done((bf16[392,128]{1,0:T(8,128)(2,1)S(1)}, bf16[392,128]{1,0:T(8,128)(2,1)S(1)}, u32[]{:S(2)}, u32[]{:S(2)}) %collective-permute-start.3) | collective-permute-done | bytes 100384 | tf_op jit(solution)/shard_map/ppermute | solution.py:329
  21.3 3.6 %collective-permute-start.7 = (bf16[392,128]{1,0:T(8,128)(2,1)S(1)}, bf16[392,128]{1,0:T(8,128)(2,1)S(1)}, u32[]{:S(2)}, u32[]{:S(2)}) collective-permute-start(bf16[392,128]{1,0:T(8,128)(2,1)S(1)} %get-tuple-element.35), channel_id=1, source_target_pairs={{0,8},{2,10},{4,12},{6,14},{8,0},{10,2},{12,4},{14,6},{1,9},{3,11}... | collective-permute-start | bytes 301064 | tf_op jit(solution)/shard_map/ppermute | solution.py:329
  24.9 0.0 copy-done
  24.9 0.0 copy-done.1
  24.9 0.0 copy-done.2
  24.9 1.4 %attend_first.1 = (f32[16,96,128]{2,1,0:T(8,128)S(1)}, f32[16,96,128]{2,1,0:T(8,128)S(1)}, f32[2,96,128]{2,1,0:T(8,128)S(1)}, f32[16,96,128]{2,1,0:T(8,128)S(1)}) custom-call(bf16[80,2048]{1,0:T(8,128)(2,1)S(1)} %copy-done, bf16[80,512]{1,0:T(8,128)(2,1)S(1)} %copy-done.1, s32[1,8]{1,0:T(1,128)S(1)} %copy-done.2, ...), custom_call_target="tpu_custom_call" | custom-call | flops 16777216 | bytes 4194304 | tf_op jit(solution)/shard_map/attend_first/pallas_call | solution.py:277
  26.3 0.0 collective-permute-done.2.refs_1_
  26.3 1.7 %attend_more.2.acc_in = f32[16,96,128]{2,1,0:T(8,128)S(1)} custom-call(s32[1,8]{1,0:T(1,128)S(1)} %copy-done.2, f32[16,96,128]{2,1,0:T(8,128)S(1)} %get-tuple-element.25.q_ref, f32[16,96,128]{2,1,0:T(8,128)S(1)} %get-tuple-element.26.score_ref, f32[2,96,128]{2,1,0:T(8,128)S(1)} %get-tuple-element.27.value_ref, ...), custom_call_target="tpu_custom_call", output_to_operand_aliasing={{}: (4, {})} | custom-call | flops 16777216 | bytes 4194304 | tf_op jit(solution)/shard_map/attend_more/pallas_call | solution.py:305
  27.9 0.0 collective-permute-done.4.refs_0_
  28.0 1.7 %collective-permute-done.5.refs_1_ = bf16[392,128]{1,0:T(8,128)(2,1)S(1)} collective-permute-done((bf16[392,128]{1,0:T(8,128)(2,1)S(1)}, bf16[392,128]{1,0:T(8,128)(2,1)S(1)}, u32[]{:S(2)}, u32[]{:S(2)}) %collective-permute-start.5) | collective-permute-done | bytes 100384 | tf_op jit(solution)/shard_map/ppermute | solution.py:329
  29.7 0.0 collective-permute-done.6.refs_2_
  29.7 1.7 %attend_more.3.acc_in = f32[16,96,128]{2,1,0:T(8,128)S(1)} custom-call(s32[1,8]{1,0:T(1,128)S(1)} %copy-done.2, f32[16,96,128]{2,1,0:T(8,128)S(1)} %get-tuple-element.25.q_ref, f32[16,96,128]{2,1,0:T(8,128)S(1)} %get-tuple-element.26.score_ref, f32[2,96,128]{2,1,0:T(8,128)S(1)} %get-tuple-element.27.value_ref, ...), custom_call_target="tpu_custom_call", output_to_operand_aliasing={{}: (4, {})} | custom-call | flops 16777216 | bytes 4194304 | tf_op jit(solution)/shard_map/attend_more/pallas_call | solution.py:305
  31.4 0.1 collective-permute-done.7.refs_0_
  31.5 2.0 %attend_last.1 = (f32[16,96,128]{2,1,0:T(8,128)S(1)}, bf16[80,2048]{1,0:T(8,128)(2,1)}) custom-call(s32[1,8]{1,0:T(1,128)S(1)} %copy-done.2, f32[16,96,128]{2,1,0:T(8,128)S(1)} %get-tuple-element.25.q_ref, f32[16,96,128]{2,1,0:T(8,128)S(1)} %get-tuple-element.26.score_ref, ...), custom_call_target="tpu_custom_call", output_to_operand_aliasing={{0}: (4, {})} | custom-call | flops 16777216 | bytes 4194304 | tf_op jit(solution)/shard_map/attend_last/pallas_call | solution.py:305
  (2 shorter events, 0.0 us)
Async XLA Ops:
  4.0 3.3 %collective-permute-start = (f32[256,640]{1,0:T(8,128)S(1)}, f32[256,640]{1,0:T(8,128)S(1)}, u32[]{:S(2)}, u32[]{:S(2)}) collective-permute-start(f32[256,640]{1,0:T(8,128)S(1)} %get-tuple-element.22.send_ref), channel_id=1, source_target_pairs={{0,1},{1,0},{2,3},{3,2},{4,5},{5,4},{6,7},{7,6},{8,9},{9,8},{10,11... | collective-permute-start | bytes 1966088 | tf_op jit(solution)/shard_map/ppermute | solution.py:323
  4.5 2.7 %copy-start.3 = (s32[1,8]{1,0:T(1,128)S(1)}, s32[1,8]{1,0:T(1,128)}, u32[]{:S(2)}) copy-start(s32[1,8]{1,0:T(1,128)} %len_ref.3) | copy-start | bytes 100
  4.5 2.8 %copy-start.4 = (s32[1,8]{1,0:T(1,128)S(1)}, s32[1,8]{1,0:T(1,128)}, u32[]{:S(2)}) copy-start(s32[1,8]{1,0:T(1,128)} %host_ref.3) | copy-start | bytes 100
  7.2 17.7 %copy-start = (bf16[80,2048]{1,0:T(8,128)(2,1)S(1)}, bf16[80,2048]{1,0:T(8,128)(2,1)}, u32[]{:S(2)}) copy-start(bf16[80,2048]{1,0:T(8,128)(2,1)} %query_ref.1) | copy-start | bytes 983044
  7.2 17.7 %copy-start.1 = (bf16[80,512]{1,0:T(8,128)(2,1)S(1)}, bf16[80,512]{1,0:T(8,128)(2,1)}, u32[]{:S(2)}) copy-start(bf16[80,512]{1,0:T(8,128)(2,1)} %own_ref.1) | copy-start | bytes 245764
  7.2 17.7 %copy-start.2 = (s32[1,8]{1,0:T(1,128)S(1)}, s32[1,8]{1,0:T(1,128)}, u32[]{:S(2)}) copy-start(s32[1,8]{1,0:T(1,128)} %count_ref.7) | copy-start | bytes 100
  8.1 11.9 %collective-permute-start.1 = (bf16[392,128]{1,0:T(8,128)(2,1)S(1)}, bf16[392,128]{1,0:T(8,128)(2,1)S(1)}, u32[]{:S(2)}, u32[]{:S(2)}) collective-permute-start(bf16[392,128]{1,0:T(8,128)(2,1)S(1)} %get-tuple-element.29), channel_id=1, source_target_pairs={{0,14},{2,12},{4,10},{6,8},{8,6},{10,4},{12,2},{14,0},{1,15},{3,13... | collective-permute-start | bytes 301064 | tf_op jit(solution)/shard_map/ppermute | solution.py:329
  13.8 7.5 %collective-permute-start.3 = (bf16[392,128]{1,0:T(8,128)(2,1)S(1)}, bf16[392,128]{1,0:T(8,128)(2,1)S(1)}, u32[]{:S(2)}, u32[]{:S(2)}) collective-permute-start(bf16[392,128]{1,0:T(8,128)(2,1)S(1)} %get-tuple-element.31), channel_id=1, source_target_pairs={{0,12},{2,14},{4,8},{6,10},{8,4},{10,6},{12,0},{14,2},{1,13},{3,15... | collective-permute-start | bytes 301064 | tf_op jit(solution)/shard_map/ppermute | solution.py:329
  14.9 11.4 %collective-permute-start.2 = (bf16[392,128]{1,0:T(8,128)(2,1)S(1)}, bf16[392,128]{1,0:T(8,128)(2,1)S(1)}, u32[]{:S(2)}, u32[]{:S(2)}) collective-permute-start(bf16[392,128]{1,0:T(8,128)(2,1)S(1)} %get-tuple-element.30), channel_id=1, source_target_pairs={{0,6},{2,4},{4,2},{6,0},{8,14},{10,12},{12,10},{14,8},{1,7},{3,5},... | collective-permute-start | bytes 301064 | tf_op jit(solution)/shard_map/ppermute | solution.py:329
  14.9 13.0 %collective-permute-start.4 = (bf16[392,128]{1,0:T(8,128)(2,1)S(1)}, bf16[392,128]{1,0:T(8,128)(2,1)S(1)}, u32[]{:S(2)}, u32[]{:S(2)}) collective-permute-start(bf16[392,128]{1,0:T(8,128)(2,1)S(1)} %get-tuple-element.32), channel_id=1, source_target_pairs={{0,4},{2,6},{4,0},{6,2},{8,12},{10,14},{12,8},{14,10},{1,5},{3,7},... | collective-permute-start | bytes 301064 | tf_op jit(solution)/shard_map/ppermute | solution.py:329
  16.8 12.9 %collective-permute-start.5 = (bf16[392,128]{1,0:T(8,128)(2,1)S(1)}, bf16[392,128]{1,0:T(8,128)(2,1)S(1)}, u32[]{:S(2)}, u32[]{:S(2)}) collective-permute-start(bf16[392,128]{1,0:T(8,128)(2,1)S(1)} %get-tuple-element.33), channel_id=1, source_target_pairs={{0,10},{2,8},{4,14},{6,12},{8,2},{10,0},{12,6},{14,4},{1,11},{3,9}... | collective-permute-start | bytes 301064 | tf_op jit(solution)/shard_map/ppermute | solution.py:329
  20.0 9.7 %collective-permute-start.6 = (bf16[392,128]{1,0:T(8,128)(2,1)S(1)}, bf16[392,128]{1,0:T(8,128)(2,1)S(1)}, u32[]{:S(2)}, u32[]{:S(2)}) collective-permute-start(bf16[392,128]{1,0:T(8,128)(2,1)S(1)} %get-tuple-element.34), channel_id=1, source_target_pairs={{0,2},{2,0},{4,6},{6,4},{8,10},{10,8},{12,14},{14,12},{1,3},{3,1},... | collective-permute-start | bytes 301064 | tf_op jit(solution)/shard_map/ppermute | solution.py:329
  21.3 10.2 %collective-permute-start.7 = (bf16[392,128]{1,0:T(8,128)(2,1)S(1)}, bf16[392,128]{1,0:T(8,128)(2,1)S(1)}, u32[]{:S(2)}, u32[]{:S(2)}) collective-permute-start(bf16[392,128]{1,0:T(8,128)(2,1)S(1)} %get-tuple-element.35), channel_id=1, source_target_pairs={{0,8},{2,10},{4,12},{6,14},{8,0},{10,2},{12,4},{14,6},{1,9},{3,11}... | collective-permute-start | bytes 301064 | tf_op jit(solution)/shard_map/ppermute | solution.py:329

commit v6 on v5

v6 whole, which is shorter than its diff:
```python
import functools

import jax
import jax.numpy as jnp
from jax import lax
from jax.experimental import pallas as pl
from jax.experimental.pallas import tpu as pltpu
from jax.sharding import PartitionSpec as P

D = 8192
QPK = 8
HD = 128
BMAX = 16
MAXLEN = 96
META = 8
STEP = 1024
GROUP = 8
FRONT = 2
ORDER = (7, 3, 6, 2, 5, 1, 4)
VMEM_LIMIT = 44 * 1024 * 1024
PROJECT_LIMIT = VMEM_LIMIT

VMEM = pl.BlockSpec(memory_space=pltpu.VMEM)
SMEM = pl.BlockSpec(memory_space=pltpu.SMEM)
HBM = pl.BlockSpec(memory_space=pltpu.HBM)


def weight_copy(w_ref, w_buf, sem, half, c):
    width = w_buf.shape[2]
    columns = pl.ds(pl.multiple_of(half * width, width), width)
    rows = pl.ds(pl.multiple_of(c * STEP, STEP), STEP)
    return pltpu.make_async_copy(w_ref.at[rows, columns], w_buf.at[c], sem.at[c])


def project_send_kernel(tok_ref, gain_hbm, w_ref, out_ref, scaled_ref, gain_buf, gain_ref, tok_buf, w_buf, gain_sem, tok_sem, w_sem):
    half = 1 - lax.axis_index("tensor")
    steps = w_buf.shape[0]
    width = w_buf.shape[2]
    blocks = STEP // HD

    def token_copy(c):
        columns = pl.ds(pl.multiple_of(c * STEP, STEP), STEP)
        return pltpu.make_async_copy(tok_ref.at[:, columns], tok_buf.at[c], tok_sem.at[c])

    def begin(c, _):
        token_copy(c).start()
        weight_copy(w_ref, w_buf, w_sem, half, c).start()
        return _

    def step(c, _):
        token_copy(c).wait()
        squares = out_ref[:, width:]
        for b in range(blocks):
            tok = tok_buf[c, :, b * HD : (b + 1) * HD].astype(jnp.float32)
            scale = gain_ref[pl.ds(c * blocks + b, 1), :]
            scaled_ref[c, :, b * HD : (b + 1) * HD] = (tok * scale).astype(jnp.bfloat16)
            squares = squares + tok * tok
        out_ref[:, width:] = squares
        weight_copy(w_ref, w_buf, w_sem, half, c).wait()
        out_ref[:, :width] += jnp.dot(scaled_ref[c], w_buf[c], preferred_element_type=jnp.float32)
        return _

    gain_copy = pltpu.make_async_copy(gain_hbm, gain_buf, gain_sem.at[0])
    gain_copy.start()
    out_ref[...] = jnp.zeros_like(out_ref)
    lax.fori_loop(0, steps, begin, 0)
    gain_copy.wait()
    gain_ref[...] = gain_buf[...].astype(jnp.float32)
    lax.fori_loop(0, steps, step, 0)


def make_picks(order, me, rows, len_ref, host_ref, pick_ref, meta_ref, slot_ref, start_ref):
    start = 0
    for i in range(len_ref.shape[1]):
        turn = host_ref[0, i] ^ me
        slot_ref[turn] = i
        start_ref[turn] = start
        start = start + len_ref[0, i]
    lane = lax.broadcasted_iota(jnp.int32, (META, HD), 1)
    row_at = lax.broadcasted_iota(jnp.int32, (MAXLEN, rows), 1)
    row_at = row_at - lax.broadcasted_iota(jnp.int32, (MAXLEN, rows), 0)
    for i, k in enumerate(order):
        hit = (row_at == start_ref[k]).astype(jnp.float32).astype(jnp.bfloat16)
        pick_ref[i * MAXLEN : (i + 1) * MAXLEN, :] = hit
        slot = slot_ref[k]
        meta = jnp.where(lane == 0, slot, jnp.where(lane == 1, len_ref[0, slot], 0))
        meta_ref[i] = meta.astype(jnp.float32)


def project_keep_kernel(len_hbm, host_hbm, scaled_ref, w_ref, out_ref, pick_ref, meta_ref, w_buf, w_sem, len_ref, host_ref, small_sem, slot_ref, start_ref, *, order):
    half = lax.axis_index("tensor")
    steps = w_buf.shape[0]
    len_copy = pltpu.make_async_copy(len_hbm, len_ref, small_sem.at[0])
    host_copy = pltpu.make_async_copy(host_hbm, host_ref, small_sem.at[1])
    len_copy.start()
    host_copy.start()
    for c in range(steps):
        weight_copy(w_ref, w_buf, w_sem, half, c).start()
    len_copy.wait()
    host_copy.wait()
    make_picks(order, lax.axis_index("section"), out_ref.shape[0], len_ref, host_ref, pick_ref, meta_ref, slot_ref, start_ref)
    for c in range(steps):
        weight_copy(w_ref, w_buf, w_sem, half, c).wait()
        part = jnp.dot(scaled_ref[c], w_buf[c], preferred_element_type=jnp.float32)
        if c == 0:
            out_ref[...] = part
        else:
            out_ref[...] += part


def project_cost(rows, depth, width):
    return pl.CostEstimate(
        flops=2 * rows * depth * width,
        bytes_accessed=2 * depth * (rows + width) + 4 * rows * width,
        transcendentals=0,
    )


def project_send(tokens, gain, weight):
    rows, depth = tokens.shape
    width = weight.shape[1] // 2
    steps = depth // STEP
    return pl.pallas_call(
        project_send_kernel,
        out_shape=(
            jax.ShapeDtypeStruct((rows, width + HD), jnp.float32),
            jax.ShapeDtypeStruct((steps, rows, STEP), jnp.bfloat16),
        ),
        in_specs=[HBM, HBM, HBM],
        out_specs=(VMEM, VMEM),
        scratch_shapes=[
            pltpu.VMEM(gain.shape, jnp.bfloat16),
            pltpu.VMEM(gain.shape, jnp.float32),
            pltpu.VMEM((steps, rows, STEP), jnp.bfloat16),
            pltpu.VMEM((steps, STEP, width), jnp.bfloat16),
            pltpu.SemaphoreType.DMA((1,)),
            pltpu.SemaphoreType.DMA((steps,)),
            pltpu.SemaphoreType.DMA((steps,)),
        ],
        compiler_params=pltpu.CompilerParams(vmem_limit_bytes=PROJECT_LIMIT),
        cost_estimate=project_cost(rows, depth, width),
        name="project_send",
    )(tokens, gain, weight)


def project_keep(lengths, decode_host, scaled, weight, order):
    steps, rows, _ = scaled.shape
    depth = steps * STEP
    width = weight.shape[1] // 2
    sections = len(order)
    return pl.pallas_call(
        functools.partial(project_keep_kernel, order=order),
        out_shape=(
            jax.ShapeDtypeStruct((rows, width), jnp.float32),
            jax.ShapeDtypeStruct((sections * MAXLEN, rows), jnp.bfloat16),
            jax.ShapeDtypeStruct((sections, META, HD), jnp.float32),
        ),
        in_specs=[HBM, HBM, VMEM, HBM],
        out_specs=(VMEM, VMEM, VMEM),
        scratch_shapes=[
            pltpu.VMEM((steps, STEP, width), jnp.bfloat16),
            pltpu.SemaphoreType.DMA((steps,)),
            pltpu.SMEM((1, sections), jnp.int32),
            pltpu.SMEM((1, sections), jnp.int32),
            pltpu.SemaphoreType.DMA((2,)),
            pltpu.SMEM((sections,), jnp.int32),
            pltpu.SMEM((sections,), jnp.int32),
        ],
        compiler_params=pltpu.CompilerParams(vmem_limit_bytes=VMEM_LIMIT),
        cost_estimate=project_cost(rows, depth, width),
        name="project_keep",
    )(lengths, decode_host, scaled, weight)


def pack_blocks(first, kv, pick_ref, meta_ref, outs):
    width = kv.shape[1]
    for base in range(0, len(outs), GROUP):
        part = outs[base : base + GROUP]
        top = (first + base) * MAXLEN
        picks = pick_ref[top : top + len(part) * MAXLEN, :]
        blocks = jnp.dot(picks, kv, preferred_element_type=jnp.float32).astype(jnp.bfloat16)
        for i, out in enumerate(part):
            for g in range(width // HD):
                out[g * MAXLEN : (g + 1) * MAXLEN, :] = blocks[
                    i * MAXLEN : (i + 1) * MAXLEN, g * HD : (g + 1) * HD
                ]
            out[width // HD * MAXLEN :, :] = meta_ref[first + base + i].astype(jnp.bfloat16)


def pack_kernel(keep_ref, recv_ref, send_ref, pick_ref, meta_ref, *outs):
    width = keep_ref.shape[1]
    squares = jnp.sum(recv_ref[:, width:] + send_ref[:, width:], axis=1, keepdims=True)
    inverse = lax.rsqrt(squares / D + 1e-05)
    kv = ((keep_ref[...] + recv_ref[:, :width]) * inverse).astype(jnp.bfloat16)
    pack_blocks(0, kv, pick_ref, meta_ref, outs)


def pack(keep, recv, send, picks, metas, order):
    rows, width = keep.shape
    block = jax.ShapeDtypeStruct((width // HD * MAXLEN + META, HD), jnp.bfloat16)
    blocks = pl.pallas_call(
        pack_kernel,
        out_shape=[block] * len(order),
        in_specs=[VMEM] * 5,
        out_specs=[VMEM] * len(order),
        compiler_params=pltpu.CompilerParams(vmem_limit_bytes=VMEM_LIMIT),
        name="pack",
    )(keep, recv, send, picks, metas)
    return dict(zip(order, blocks))


def attend_blocks(blocks, table_ref, q_ref, score_ref, value_ref, acc_ref):
    groups = q_ref.shape[0] // QPK
    scale = HD ** (-0.5)
    flat = QPK * BMAX
    lane = lax.broadcasted_iota(jnp.int32, (flat, MAXLEN), 1)
    beam = lax.broadcasted_iota(jnp.int32, (QPK, BMAX, HD), 1)
    place = lax.broadcasted_iota(jnp.int32, table_ref.shape, 0).astype(jnp.float32)
    work = []
    for block in blocks:
        meta = block[2 * groups * MAXLEN :, :].astype(jnp.float32)
        length = meta[:1, 1:2].astype(jnp.int32)
        entry = jnp.sum(jnp.where(place == meta[:1, :1], table_ref[...], 0.0), axis=0, keepdims=True)
        start = entry[0, 0].astype(jnp.int32)
        count = entry[:1, 1:2].astype(jnp.int32)
        for g in range(groups):
            work.append((block, g, length, pl.ds(start, BMAX), count))
    scores = []
    for block, g, length, at, count in work:
        q = q_ref[g * QPK : (g + 1) * QPK, at, :].reshape(flat, HD).astype(jnp.bfloat16)
        keys = block[2 * g * MAXLEN : (2 * g + 1) * MAXLEN, :]
        raw = lax.dot_general(q, keys, (((1,), (1,)), ((), ())), preferred_element_type=jnp.float32)
        scores.append(jnp.where(lane < length, raw * scale, -jnp.inf))
    tops, owns = [], []
    for (block, g, length, at, count), score in zip(work, scores):
        own = score_ref[g * QPK : (g + 1) * QPK, at, :].reshape(flat, HD)[:, :1]
        owns.append(own)
        tops.append(jnp.maximum(jnp.max(score, axis=1, keepdims=True), own))
    expos = [jnp.exp(score - top) for score, top in zip(scores, tops)]
    own_expos = [jnp.exp(own - top) for own, top in zip(owns, tops)]
    totals = [jnp.sum(e, axis=1, keepdims=True) + o for e, o in zip(expos, own_expos)]
    weights = [(e / t).astype(jnp.bfloat16) for e, t in zip(expos, totals)]
    own_weights = [(o / t).astype(jnp.bfloat16).astype(jnp.float32) for o, t in zip(own_expos, totals)]
    mixes = []
    for (block, g, length, at, count), weight in zip(work, weights):
        values = block[(2 * g + 1) * MAXLEN : (2 * g + 2) * MAXLEN, :]
        mixes.append(jnp.dot(weight, values, preferred_element_type=jnp.float32))
    for (block, g, length, at, count), mix, own in zip(work, mixes, own_weights):
        own = own.reshape(QPK, BMAX, 1) * value_ref[g, at, :][None]
        heads = slice(g * QPK, (g + 1) * QPK)
        acc_ref[heads, at, :] = jnp.where(
            beam < count, mix.reshape(QPK, BMAX, HD) + own, acc_ref[heads, at, :]
        )


def first_kernel(query_ref, own_ref, count_ref, block_ref, q_ref, score_ref, value_ref, table_ref, acc_ref):
    beams = query_ref.shape[0]
    heads = query_ref.shape[1] // HD
    scale = HD ** (-0.5)
    tail = jnp.zeros((BMAX, HD), jnp.float32)
    for g in range(heads // QPK):
        key = own_ref[:, 2 * g * HD : (2 * g + 1) * HD].astype(jnp.float32)
        value_ref[g, :beams, :] = own_ref[:, (2 * g + 1) * HD : (2 * g + 2) * HD].astype(jnp.float32)
        value_ref[g, beams:, :] = tail
        for h in range(g * QPK, (g + 1) * QPK):
            q = query_ref[:, h * HD : (h + 1) * HD].astype(jnp.float32)
            q_ref[h, :beams, :] = q
            q_ref[h, beams:, :] = tail
            score = jnp.sum(q * key, axis=1, keepdims=True) * scale
            score_ref[h, :beams, :] = jnp.broadcast_to(score, (beams, HD))
            score_ref[h, beams:, :] = tail
    lane = lax.broadcasted_iota(jnp.int32, (1, HD), 1)
    start = 0
    for i in range(count_ref.shape[1]):
        count = count_ref[0, i]
        row = jnp.where(lane == 0, start, jnp.where(lane == 1, count, 0))
        table_ref[i : i + 1, :] = row.astype(jnp.float32)
        start = start + count
    acc_ref[...] = jnp.zeros_like(acc_ref)
    attend_blocks([block_ref], table_ref, q_ref, score_ref, value_ref, acc_ref)


def attend_first(query, own, counts, block):
    beams, width = query.shape
    heads = width // HD
    tall = jax.ShapeDtypeStruct((heads, beams + BMAX, HD), jnp.float32)
    return pl.pallas_call(
        first_kernel,
        out_shape=(
            tall,
            tall,
            jax.ShapeDtypeStruct((heads // QPK, beams + BMAX, HD), jnp.float32),
            jax.ShapeDtypeStruct((counts.shape[1], HD), jnp.float32),
            tall,
        ),
        in_specs=[VMEM, VMEM, SMEM, VMEM],
        out_specs=(VMEM,) * 5,
        compiler_params=pltpu.CompilerParams(vmem_limit_bytes=VMEM_LIMIT),
        cost_estimate=pl.CostEstimate(flops=1 << 24, bytes_accessed=4 << 20, transcendentals=0),
        name="attend_first",
    )(query, own, counts, block)


def later_kernel(table_ref, q_ref, score_ref, value_ref, acc_in, *refs, n_blocks, last):
    blocks, rest = refs[:n_blocks], refs[n_blocks:]
    acc_ref = rest[0]
    for base in range(0, n_blocks, GROUP // 2):
        attend_blocks(blocks[base : base + GROUP // 2], table_ref, q_ref, score_ref, value_ref, acc_ref)
    if last:
        out_ref = rest[1]
        beams = out_ref.shape[0]
        for h in range(acc_ref.shape[0]):
            out_ref[:, h * HD : (h + 1) * HD] = acc_ref[h, :beams, :].astype(jnp.bfloat16)


def attend_later(table, q, score, value, acc, blocks, out_shape):
    last = out_shape is not None
    shapes = [jax.ShapeDtypeStruct(acc.shape, acc.dtype)]
    if last:
        shapes.append(out_shape)
    return pl.pallas_call(
        functools.partial(later_kernel, n_blocks=len(blocks), last=last),
        out_shape=shapes,
        in_specs=[VMEM] * (5 + len(blocks)),
        out_specs=[VMEM] * len(shapes),
        input_output_aliases={4: 0},
        compiler_params=pltpu.CompilerParams(vmem_limit_bytes=VMEM_LIMIT),
        cost_estimate=pl.CostEstimate(flops=1 << 24, bytes_accessed=4 << 20, transcendentals=0),
        name="attend_last" if last else "attend_more",
    )(table, q, score, value, acc, *blocks)


def per_device(tokens, norm_gain, kv_weight, lengths, decode_host, beam_counts, beam_query, beam_newkv):
    sections = lax.axis_size("section")
    gain = pltpu.with_memory_space_constraint(norm_gain.reshape(-1, HD), pltpu.HBM)
    tokens = pltpu.with_memory_space_constraint(tokens, pltpu.HBM)
    send, scaled = project_send(tokens, gain, kv_weight)
    recv = lax.ppermute(send, "tensor", [(0, 1), (1, 0)])
    turns = tuple(range(sections - 1, -1, -1))
    keep, picks, metas = project_keep(lengths, decode_host, scaled, kv_weight, turns)
    blocks = pack(keep, recv, send, picks, metas, turns)
    got = {}
    for k in range(1, sections):
        got[k] = lax.ppermute(blocks[k], "section", [(s, s ^ k) for s in range(sections)])
    q, score, value, table, acc = attend_first(beam_query, beam_newkv, beam_counts, blocks[0])
    order = ORDER if sections == len(ORDER) + 1 else tuple(range(sections - 1, 0, -1))
    for part in (order[:3], order[3:-1]):
        (acc,) = attend_later(table, q, score, value, acc, [got[k] for k in part], None)
    late = [got[order[-1]]]
    out_shape = jax.ShapeDtypeStruct(beam_query.shape, jnp.bfloat16)
    return attend_later(table, q, score, value, acc, late, out_shape)[1]


def solution(mesh):
    rows = ("groups", "section")
    placed = (
        P(rows, "tensor"),
        P("tensor"),
        P("tensor", None),
        P(rows, None),
        P(rows, None),
        P(rows, None),
        P(rows, "tensor"),
        P(rows, "tensor"),
    )
    return jax.shard_map(
        per_device,
        mesh=mesh,
        in_specs=placed,
        out_specs=P(rows, "tensor"),
        check_vma=False,
    )
```

time: 33.7 us -> 32.7 us (0.970)
  waiting for transfers between devices: 2.51 us -> 8.13 us
  starting transfers between devices: 15.7 us -> 12 us
  Pallas kernels: 15.1 us -> 12.2 us
    ppermute x7, waiting for transfers between devices: 2.51 us -> 8.13 us  [per_device(): lax.ppermute(blocks[k], 'section', [(s, s ^ k) for s in range(sections)])]
    ppermute x7, starting transfers between devices: 15.2 us -> 11.5 us  [per_device(): lax.ppermute(blocks[k], 'section', [(s, s ^ k) for s in range(sections)])]
    pallas_call x3, Pallas kernels: 5.33 us -> 3.71 us  [attend_later(): pl.pallas_call(functools.partial(later_kernel, n_blocks=len(blocks), last...]
    pallas_call x3 -> x2, Pallas kernels: 4.41 us -> 3.14 us  [the longest x1 2.68 us: project_keep(): pl.pallas_call(functools.partial(project_keep_kernel, order=order), out_s...]
  transfers between devices with their start and end apart: 8 -> 8, of which waited for: 3 -> 3; matrix products, arithmetic and copies ran while one was open for 0% -> 0% of each run, Pallas kernels for 25% -> 19%
where the time goes in v6:
time: 32.7 us; the launch traced here: 32.5 us
  Pallas kernels  12.2 us (37%)
  starting transfers between devices  12 us (37%)
  waiting for transfers between devices  8.13 us (25%)
    ppermute x7, starting transfers between devices, per_device(): lax.ppermute(blocks[k], 'section', [(s, s ^ k) for s in range(sections)])  11.5 us
    ppermute x7, waiting for transfers between devices, per_device(): lax.ppermute(blocks[k], 'section', [(s, s ^ k) for s in range(sections)])  8.13 us
    pallas_call x1, Pallas kernels, project_send(): pl.pallas_call(project_send_kernel, out_shape=(jax.ShapeDtypeStruct((rows...  4 us
    pallas_call x3, Pallas kernels, attend_later(): pl.pallas_call(functools.partial(later_kernel, n_blocks=len(blocks), last...  3.71 us
    pallas_call x1, Pallas kernels, project_keep(): pl.pallas_call(functools.partial(project_keep_kernel, order=order), out_s...  2.68 us
    pallas_call x1, Pallas kernels, attend_first(): pl.pallas_call(first_kernel, out_shape=(tall, tall, jax.ShapeDtypeStruct(...  1.38 us
  transfers between devices with their start and end apart: 8, of which 3 were waited for; matrix products, arithmetic and copies ran while one was open for 0% of the time, Pallas kernels for 19%

profile of v6, /device:TPU:0, one launch (start us, length us, event | category | flops | bytes accessed | tf_op | source)
XLA Modules:
  0.0 32.5 jit_solution(11046333973334553279)
XLA Ops:
  0.0 0.0 copy-start.2
  0.0 4.0 %project_send.1 = (f32[256,640]{1,0:T(8,128)S(1)}, bf16[4,256,1024]{2,1,0:T(8,128)(2,1)S(1)}) custom-call(bf16[256,4096]{1,0:T(8,128)(2,1)} %tok_ref.1, bf16[32,128]{1,0:T(8,128)(2,1)} %bitcast.1, bf16[4096,1024]{1,0:T(8,128)(2,1)} %w_ref.3), custom_call_target="tpu_custom_call" | custom-call | flops 1073741824 | bytes 6815744 | tf_op jit(solution)/shard_map/project_send/pallas_call | solution.py:123
  4.0 0.5 %collective-permute-start = (f32[256,640]{1,0:T(8,128)S(1)}, f32[256,640]{1,0:T(8,128)S(1)}, u32[]{:S(2)}, u32[]{:S(2)}) collective-permute-start(f32[256,640]{1,0:T(8,128)S(1)} %get-tuple-element.26.send_ref), channel_id=1, source_target_pairs={{0,1},{1,0},{2,3},{3,2},{4,5},{5,4},{6,7},{7,6},{8,9},{9,8},{10,11... | collective-permute-start | bytes 1966088 | tf_op jit(solution)/shard_map/ppermute | solution.py:338
  4.5 0.0 copy-done.2
  4.5 0.0 copy-done.3
  4.5 2.7 %project_keep.1 = (f32[256,512]{1,0:T(8,128)S(1)}, bf16[768,256]{1,0:T(8,128)(2,1)S(1)}, f32[8,8,128]{2,1,0:T(8,128)S(1)}) custom-call(s32[1,8]{1,0:T(1,128)S(1)} %copy-done.2, s32[1,8]{1,0:T(1,128)S(1)} %copy-done.3, bf16[4,256,1024]{2,1,0:T(8,128)(2,1)S(1)} %get-tuple-element.24.scaled_ref, bf16[4096,1024]{1,0:T(8,128)(2,1)} %w_ref.3), custom_call_target="tpu_custom_call" | custom-call | flops 1073741824 | bytes 6815744 | tf_op jit(solution)/shard_map/project_keep/pallas_call | solution.py:151
  7.2 0.0 copy-start
  7.2 0.0 copy-start.1
  7.2 0.0 copy-start.4
  7.3 0.0 collective-permute-done.recv_ref
  7.3 0.5 %pack.1 = (bf16[392,128]{1,0:T(8,128)(2,1)S(1)}, bf16[392,128]{1,0:T(8,128)(2,1)S(1)}, bf16[392,128]{1,0:T(8,128)(2,1)S(1)}, bf16[392,128]{1,0:T(8,128)(2,1)S(1)...) custom-call(f32[256,512]{1,0:T(8,128)S(1)} %get-tuple-element.25.kee, ...), custom_call_target="tpu_custom_call" | custom-call | tf_op jit(solution)/shard_map/pack/pallas_call | solution.py:201
  7.7 5.7 %collective-permute-start.1 = (bf16[392,128]{1,0:T(8,128)(2,1)S(1)}, bf16[392,128]{1,0:T(8,128)(2,1)S(1)}, u32[]{:S(2)}, u32[]{:S(2)}) collective-permute-start(bf16[392,128]{1,0:T(8,128)(2,1)S(1)} %get-tuple-element.35), channel_id=1, source_target_pairs={{0,14},{2,12},{4,10},{6,8},{8,6},{10,4},{12,2},{14,0},{1,15},{3,13... | collective-permute-start | bytes 301064 | tf_op jit(solution)/shard_map/ppermute | solution.py:344
  13.4 0.0 collective-permute-start.2
  13.4 0.8 %collective-permute-start.3 = (bf16[392,128]{1,0:T(8,128)(2,1)S(1)}, bf16[392,128]{1,0:T(8,128)(2,1)S(1)}, u32[]{:S(2)}, u32[]{:S(2)}) collective-permute-start(bf16[392,128]{1,0:T(8,128)(2,1)S(1)} %get-tuple-element.37), channel_id=1, source_target_pairs={{0,12},{2,14},{4,8},{6,10},{8,4},{10,6},{12,0},{14,2},{1,13},{3,15... | collective-permute-start | bytes 301064 | tf_op jit(solution)/shard_map/ppermute | solution.py:344
  14.2 1.1 %collective-permute-start.4 = (bf16[392,128]{1,0:T(8,128)(2,1)S(1)}, bf16[392,128]{1,0:T(8,128)(2,1)S(1)}, u32[]{:S(2)}, u32[]{:S(2)}) collective-permute-start(bf16[392,128]{1,0:T(8,128)(2,1)S(1)} %get-tuple-element.38), channel_id=1, source_target_pairs={{0,4},{2,6},{4,0},{6,2},{8,12},{10,14},{12,8},{14,10},{1,5},{3,7},... | collective-permute-start | bytes 301064 | tf_op jit(solution)/shard_map/ppermute | solution.py:344
  15.4 2.9 %collective-permute-start.5 = (bf16[392,128]{1,0:T(8,128)(2,1)S(1)}, bf16[392,128]{1,0:T(8,128)(2,1)S(1)}, u32[]{:S(2)}, u32[]{:S(2)}) collective-permute-start(bf16[392,128]{1,0:T(8,128)(2,1)S(1)} %get-tuple-element.39), channel_id=1, source_target_pairs={{0,10},{2,8},{4,14},{6,12},{8,2},{10,0},{12,6},{14,4},{1,11},{3,9}... | collective-permute-start | bytes 301064 | tf_op jit(solution)/shard_map/ppermute | solution.py:344
  18.2 0.0 collective-permute-done.1.refs_0_
  18.2 1.0 %collective-permute-start.6 = (bf16[392,128]{1,0:T(8,128)(2,1)S(1)}, bf16[392,128]{1,0:T(8,128)(2,1)S(1)}, u32[]{:S(2)}, u32[]{:S(2)}) collective-permute-start(bf16[392,128]{1,0:T(8,128)(2,1)S(1)} %get-tuple-element.40), channel_id=1, source_target_pairs={{0,2},{2,0},{4,6},{6,4},{8,10},{10,8},{12,14},{14,12},{1,3},{3,1},... | collective-permute-start | bytes 301064 | tf_op jit(solution)/shard_map/ppermute | solution.py:344
  19.3 3.3 %collective-permute-done.2.refs_1_ = bf16[392,128]{1,0:T(8,128)(2,1)S(1)} collective-permute-done((bf16[392,128]{1,0:T(8,128)(2,1)S(1)}, bf16[392,128]{1,0:T(8,128)(2,1)S(1)}, u32[]{:S(2)}, u32[]{:S(2)}) %collective-permute-start.2) | collective-permute-done | bytes 100384 | tf_op jit(solution)/shard_map/ppermute | solution.py:344
  22.5 0.0 collective-permute-start.7
  22.5 0.0 copy-done
  22.5 0.0 copy-done.1
  22.5 0.0 copy-done.4
  22.5 1.4 %attend_first.1 = (f32[16,96,128]{2,1,0:T(8,128)S(1)}, f32[16,96,128]{2,1,0:T(8,128)S(1)}, f32[2,96,128]{2,1,0:T(8,128)S(1)}, f32[8,128]{1,0:T(8,128)S(1)}, f32[16,96,128]{2,1,0:T(8,128)S(1)}) custom-call(bf16[80,2048]{1,0:T(8,128)(2,1)S(1)} %copy-done, bf16[80,512]{1,0:T(8,128)(2,1)S(1)} %copy-done.1, s32[1,8]{1,0:T(1,128)S(1)} %copy-done.4, ...), custom_call_target="tpu_custom_call" | custom-call | flops 16777216 | bytes 4194304 | tf_op jit(solution)/shard_map/attend_first/pallas_call | solution.py:287
  23.9 0.0 collective-permute-done.3.refs_2_
  23.9 1.1 %attend_more.2.acc_in = f32[16,96,128]{2,1,0:T(8,128)S(1)} custom-call(f32[8,128]{1,0:T(8,128)S(1)} %get-tuple-element.30.table_ref, f32[16,96,128]{2,1,0:T(8,128)S(1)} %get-tuple-element.31.q_ref, f32[16,96,128]{2,1,0:T(8,128)S(1)} %get-tuple-element.32.score_ref, f32[2,96,128]{2,1,0:T(8,128)S(1)} %get-tuple-element.33.value_ref, ...), custom_call_target="tpu_custom_call", output_to_operand_aliasing={{}: (4, {})} | custom-call | flops 16777216 | bytes 4194304 | tf_op jit(solution)/shard_map/attend_more/pallas_call | solution.py:321
  25.1 0.0 collective-permute-done.4.refs_0_
  25.1 4.8 %collective-permute-done.5.refs_1_ = bf16[392,128]{1,0:T(8,128)(2,1)S(1)} collective-permute-done((bf16[392,128]{1,0:T(8,128)(2,1)S(1)}, bf16[392,128]{1,0:T(8,128)(2,1)S(1)}, u32[]{:S(2)}, u32[]{:S(2)}) %collective-permute-start.5) | collective-permute-done | bytes 100384 | tf_op jit(solution)/shard_map/ppermute | solution.py:344
  29.8 0.0 collective-permute-done.6.refs_2_
  29.8 1.1 %attend_more.3.acc_in = f32[16,96,128]{2,1,0:T(8,128)S(1)} custom-call(f32[8,128]{1,0:T(8,128)S(1)} %get-tuple-element.30.table_ref, f32[16,96,128]{2,1,0:T(8,128)S(1)} %get-tuple-element.31.q_ref, f32[16,96,128]{2,1,0:T(8,128)S(1)} %get-tuple-element.32.score_ref, f32[2,96,128]{2,1,0:T(8,128)S(1)} %get-tuple-element.33.value_ref, ...), custom_call_target="tpu_custom_call", output_to_operand_aliasing={{}: (4, {})} | custom-call | flops 16777216 | bytes 4194304 | tf_op jit(solution)/shard_map/attend_more/pallas_call | solution.py:321
  31.0 0.1 collective-permute-done.7.refs_0_
  31.1 1.5 %attend_last.1 = (f32[16,96,128]{2,1,0:T(8,128)S(1)}, bf16[80,2048]{1,0:T(8,128)(2,1)}) custom-call(f32[8,128]{1,0:T(8,128)S(1)} %get-tuple-element.30.table_ref, f32[16,96,128]{2,1,0:T(8,128)S(1)} %get-tuple-element.31.q_ref, f32[16,96,128]{2,1,0:T(8,128)S(1)} %get-tuple-element.32.score_ref, ...), custom_call_target="tpu_custom_call", output_to_operand_aliasing={{0}: (4, {})} | custom-call | flops 16777216 | bytes 4194304 | tf_op jit(solution)/shard_map/attend_last/pallas_call | solution.py:321
  (1 shorter events, 0.0 us)
Async XLA Ops:
  0.0 4.5 %copy-start.2 = (s32[1,8]{1,0:T(1,128)S(1)}, s32[1,8]{1,0:T(1,128)}, u32[]{:S(2)}) copy-start(s32[1,8]{1,0:T(1,128)} %len_hbm.1) | copy-start | bytes 100
  0.0 4.5 %copy-start.3 = (s32[1,8]{1,0:T(1,128)S(1)}, s32[1,8]{1,0:T(1,128)}, u32[]{:S(2)}) copy-start(s32[1,8]{1,0:T(1,128)} %host_hbm.1) | copy-start | bytes 100
  4.0 3.3 %collective-permute-start = (f32[256,640]{1,0:T(8,128)S(1)}, f32[256,640]{1,0:T(8,128)S(1)}, u32[]{:S(2)}, u32[]{:S(2)}) collective-permute-start(f32[256,640]{1,0:T(8,128)S(1)} %get-tuple-element.26.send_ref), channel_id=1, source_target_pairs={{0,1},{1,0},{2,3},{3,2},{4,5},{5,4},{6,7},{7,6},{8,9},{9,8},{10,11... | collective-permute-start | bytes 1966088 | tf_op jit(solution)/shard_map/ppermute | solution.py:338
  7.2 15.3 %copy-start = (bf16[80,2048]{1,0:T(8,128)(2,1)S(1)}, bf16[80,2048]{1,0:T(8,128)(2,1)}, u32[]{:S(2)}) copy-start(bf16[80,2048]{1,0:T(8,128)(2,1)} %query_ref.1) | copy-start | bytes 983044
  7.2 15.3 %copy-start.1 = (bf16[80,512]{1,0:T(8,128)(2,1)S(1)}, bf16[80,512]{1,0:T(8,128)(2,1)}, u32[]{:S(2)}) copy-start(bf16[80,512]{1,0:T(8,128)(2,1)} %own_ref.1) | copy-start | bytes 245764
  7.2 15.3 %copy-start.4 = (s32[1,8]{1,0:T(1,128)S(1)}, s32[1,8]{1,0:T(1,128)}, u32[]{:S(2)}) copy-start(s32[1,8]{1,0:T(1,128)} %count_ref.1) | copy-start | bytes 100
  7.7 10.5 %collective-permute-start.1 = (bf16[392,128]{1,0:T(8,128)(2,1)S(1)}, bf16[392,128]{1,0:T(8,128)(2,1)S(1)}, u32[]{:S(2)}, u32[]{:S(2)}) collective-permute-start(bf16[392,128]{1,0:T(8,128)(2,1)S(1)} %get-tuple-element.35), channel_id=1, source_target_pairs={{0,14},{2,12},{4,10},{6,8},{8,6},{10,4},{12,2},{14,0},{1,15},{3,13... | collective-permute-start | bytes 301064 | tf_op jit(solution)/shard_map/ppermute | solution.py:344
  13.4 9.1 %collective-permute-start.2 = (bf16[392,128]{1,0:T(8,128)(2,1)S(1)}, bf16[392,128]{1,0:T(8,128)(2,1)S(1)}, u32[]{:S(2)}, u32[]{:S(2)}) collective-permute-start(bf16[392,128]{1,0:T(8,128)(2,1)S(1)} %get-tuple-element.36), channel_id=1, source_target_pairs={{0,6},{2,4},{4,2},{6,0},{8,14},{10,12},{12,10},{14,8},{1,7},{3,5},... | collective-permute-start | bytes 301064 | tf_op jit(solution)/shard_map/ppermute | solution.py:344
  13.4 10.5 %collective-permute-start.3 = (bf16[392,128]{1,0:T(8,128)(2,1)S(1)}, bf16[392,128]{1,0:T(8,128)(2,1)S(1)}, u32[]{:S(2)}, u32[]{:S(2)}) collective-permute-start(bf16[392,128]{1,0:T(8,128)(2,1)S(1)} %get-tuple-element.37), channel_id=1, source_target_pairs={{0,12},{2,14},{4,8},{6,10},{8,4},{10,6},{12,0},{14,2},{1,13},{3,15... | collective-permute-start | bytes 301064 | tf_op jit(solution)/shard_map/ppermute | solution.py:344
  14.2 10.8 %collective-permute-start.4 = (bf16[392,128]{1,0:T(8,128)(2,1)S(1)}, bf16[392,128]{1,0:T(8,128)(2,1)S(1)}, u32[]{:S(2)}, u32[]{:S(2)}) collective-permute-start(bf16[392,128]{1,0:T(8,128)(2,1)S(1)} %get-tuple-element.38), channel_id=1, source_target_pairs={{0,4},{2,6},{4,0},{6,2},{8,12},{10,14},{12,8},{14,10},{1,5},{3,7},... | collective-permute-start | bytes 301064 | tf_op jit(solution)/shard_map/ppermute | solution.py:344
  15.4 14.5 %collective-permute-start.5 = (bf16[392,128]{1,0:T(8,128)(2,1)S(1)}, bf16[392,128]{1,0:T(8,128)(2,1)S(1)}, u32[]{:S(2)}, u32[]{:S(2)}) collective-permute-start(bf16[392,128]{1,0:T(8,128)(2,1)S(1)} %get-tuple-element.39), channel_id=1, source_target_pairs={{0,10},{2,8},{4,14},{6,12},{8,2},{10,0},{12,6},{14,4},{1,11},{3,9}... | collective-permute-start | bytes 301064 | tf_op jit(solution)/shard_map/ppermute | solution.py:344
  18.2 11.6 %collective-permute-start.6 = (bf16[392,128]{1,0:T(8,128)(2,1)S(1)}, bf16[392,128]{1,0:T(8,128)(2,1)S(1)}, u32[]{:S(2)}, u32[]{:S(2)}) collective-permute-start(bf16[392,128]{1,0:T(8,128)(2,1)S(1)} %get-tuple-element.40), channel_id=1, source_target_pairs={{0,2},{2,0},{4,6},{6,4},{8,10},{10,8},{12,14},{14,12},{1,3},{3,1},... | collective-permute-start | bytes 301064 | tf_op jit(solution)/shard_map/ppermute | solution.py:344
  22.5 8.5 %collective-permute-start.7 = (bf16[392,128]{1,0:T(8,128)(2,1)S(1)}, bf16[392,128]{1,0:T(8,128)(2,1)S(1)}, u32[]{:S(2)}, u32[]{:S(2)}) collective-permute-start(bf16[392,128]{1,0:T(8,128)(2,1)S(1)} %get-tuple-element.41), channel_id=1, source_target_pairs={{0,8},{2,10},{4,12},{6,14},{8,0},{10,2},{12,4},{14,6},{1,9},{3,11}... | collective-permute-start | bytes 301064 | tf_op jit(solution)/shard_map/ppermute | solution.py:344

commit v7 on v6

--- a/solution.py
+++ b/solution.py
@@ -16,7 +16,7 @@
 STEP = 1024
 GROUP = 8
 FRONT = 2
-ORDER = (7, 3, 6, 2, 5, 1, 4)
+ORDER = (4, 2, 5, 3, 7, 1, 6)
 VMEM_LIMIT = 44 * 1024 * 1024
 PROJECT_LIMIT = VMEM_LIMIT
 

time: 32.7 us -> 30.4 us (0.930)
  the two profiles are of different devices: /device:TPU:0 before, /device:TPU:23 now
where the time goes in v7:
time: 30.4 us; the launch traced here: 30.3 us
  Pallas kernels  12.2 us (40%)
  waiting for transfers between devices  10.2 us (34%)
  starting transfers between devices  7.69 us (25%)
    ppermute x7, waiting for transfers between devices, per_device(): lax.ppermute(blocks[k], 'section', [(s, s ^ k) for s in range(sections)])  10.2 us
    ppermute x7, starting transfers between devices, per_device(): lax.ppermute(blocks[k], 'section', [(s, s ^ k) for s in range(sections)])  6.95 us
    pallas_call x1, Pallas kernels, project_send(): pl.pallas_call(project_send_kernel, out_shape=(jax.ShapeDtypeStruct((rows...  4 us
    pallas_call x3, Pallas kernels, attend_later(): pl.pallas_call(functools.partial(later_kernel, n_blocks=len(blocks), last...  3.72 us
    pallas_call x1, Pallas kernels, project_keep(): pl.pallas_call(functools.partial(project_keep_kernel, order=order), out_s...  2.68 us
    pallas_call x1, Pallas kernels, attend_first(): pl.pallas_call(first_kernel, out_shape=(tall, tall, jax.ShapeDtypeStruct(...  1.38 us
    ppermute x1, starting transfers between devices, per_device(): recv = lax.ppermute(send, 'tensor', [(0, 1), (1, 0)])  0.74 us
  transfers between devices with their start and end apart: 8, of which 6 were waited for; matrix products, arithmetic and copies ran while one was open for 0% of the time, Pallas kernels for 21%

profile of v7, /device:TPU:23, one launch (start us, length us, event | category | flops | bytes accessed | tf_op | source)
XLA Modules:
  0.0 30.3 jit_solution(6112051279236547826)
XLA Ops:
  0.0 0.0 copy-start.2
  0.0 4.0 %project_send.1 = (f32[256,640]{1,0:T(8,128)S(1)}, bf16[4,256,1024]{2,1,0:T(8,128)(2,1)S(1)}) custom-call(bf16[256,4096]{1,0:T(8,128)(2,1)} %tok_ref.1, bf16[32,128]{1,0:T(8,128)(2,1)} %bitcast.1, bf16[4096,1024]{1,0:T(8,128)(2,1)} %w_ref.3), custom_call_target="tpu_custom_call" | custom-call | flops 1073741824 | bytes 6815744 | tf_op jit(solution)/shard_map/project_send/pallas_call | solution.py:123
  4.0 0.7 %collective-permute-start = (f32[256,640]{1,0:T(8,128)S(1)}, f32[256,640]{1,0:T(8,128)S(1)}, u32[]{:S(2)}, u32[]{:S(2)}) collective-permute-start(f32[256,640]{1,0:T(8,128)S(1)} %get-tuple-element.26.send_ref), channel_id=1, source_target_pairs={{0,1},{1,0},{2,3},{3,2},{4,5},{5,4},{6,7},{7,6},{8,9},{9,8},{10,11... | collective-permute-start | bytes 1966088 | tf_op jit(solution)/shard_map/ppermute | solution.py:338
  4.8 0.0 copy-done.2
  4.8 0.0 copy-done.3
  4.8 2.7 %project_keep.1 = (f32[256,512]{1,0:T(8,128)S(1)}, bf16[768,256]{1,0:T(8,128)(2,1)S(1)}, f32[8,8,128]{2,1,0:T(8,128)S(1)}) custom-call(s32[1,8]{1,0:T(1,128)S(1)} %copy-done.2, s32[1,8]{1,0:T(1,128)S(1)} %copy-done.3, bf16[4,256,1024]{2,1,0:T(8,128)(2,1)S(1)} %get-tuple-element.24.scaled_ref, bf16[4096,1024]{1,0:T(8,128)(2,1)} %w_ref.3), custom_call_target="tpu_custom_call" | custom-call | flops 1073741824 | bytes 6815744 | tf_op jit(solution)/shard_map/project_keep/pallas_call | solution.py:151
  7.4 0.0 copy-start
  7.5 0.0 copy-start.1
  7.5 0.0 copy-start.4
  7.5 0.0 collective-permute-done.recv_ref
  7.5 0.5 %pack.1 = (bf16[392,128]{1,0:T(8,128)(2,1)S(1)}, bf16[392,128]{1,0:T(8,128)(2,1)S(1)}, bf16[392,128]{1,0:T(8,128)(2,1)S(1)}, bf16[392,128]{1,0:T(8,128)(2,1)S(1)...) custom-call(f32[256,512]{1,0:T(8,128)S(1)} %get-tuple-element.25.kee, ...), custom_call_target="tpu_custom_call" | custom-call | tf_op jit(solution)/shard_map/pack/pallas_call | solution.py:201
  8.0 0.1 collective-permute-start.1
  8.1 1.3 %collective-permute-start.2 = (bf16[392,128]{1,0:T(8,128)(2,1)S(1)}, bf16[392,128]{1,0:T(8,128)(2,1)S(1)}, u32[]{:S(2)}, u32[]{:S(2)}) collective-permute-start(bf16[392,128]{1,0:T(8,128)(2,1)S(1)} %get-tuple-element.36), channel_id=1, source_target_pairs={{0,4},{2,6},{4,0},{6,2},{8,12},{10,14},{12,8},{14,10},{1,5},{3,7},... | collective-permute-start | bytes 301064 | tf_op jit(solution)/shard_map/ppermute | solution.py:344
  9.4 2.2 %collective-permute-start.3 = (bf16[392,128]{1,0:T(8,128)(2,1)S(1)}, bf16[392,128]{1,0:T(8,128)(2,1)S(1)}, u32[]{:S(2)}, u32[]{:S(2)}) collective-permute-start(bf16[392,128]{1,0:T(8,128)(2,1)S(1)} %get-tuple-element.37), channel_id=1, source_target_pairs={{0,10},{2,8},{4,14},{6,12},{8,2},{10,0},{12,6},{14,4},{1,11},{3,9}... | collective-permute-start | bytes 301064 | tf_op jit(solution)/shard_map/ppermute | solution.py:344
  11.6 1.1 %collective-permute-start.4 = (bf16[392,128]{1,0:T(8,128)(2,1)S(1)}, bf16[392,128]{1,0:T(8,128)(2,1)S(1)}, u32[]{:S(2)}, u32[]{:S(2)}) collective-permute-start(bf16[392,128]{1,0:T(8,128)(2,1)S(1)} %get-tuple-element.38), channel_id=1, source_target_pairs={{0,6},{2,4},{4,2},{6,0},{8,14},{10,12},{12,10},{14,8},{1,7},{3,5},... | collective-permute-start | bytes 301064 | tf_op jit(solution)/shard_map/ppermute | solution.py:344
  12.8 0.1 collective-permute-start.5
  12.9 0.5 %collective-permute-done.1.refs_0_ = bf16[392,128]{1,0:T(8,128)(2,1)S(1)} collective-permute-done((bf16[392,128]{1,0:T(8,128)(2,1)S(1)}, bf16[392,128]{1,0:T(8,128)(2,1)S(1)}, u32[]{:S(2)}, u32[]{:S(2)}) %collective-permute-start.1) | collective-permute-done | bytes 100384 | tf_op jit(solution)/shard_map/ppermute | solution.py:344
  13.4 0.8 %collective-permute-start.6 = (bf16[392,128]{1,0:T(8,128)(2,1)S(1)}, bf16[392,128]{1,0:T(8,128)(2,1)S(1)}, u32[]{:S(2)}, u32[]{:S(2)}) collective-permute-start(bf16[392,128]{1,0:T(8,128)(2,1)S(1)} %get-tuple-element.40), channel_id=1, source_target_pairs={{0,2},{2,0},{4,6},{6,4},{8,10},{10,8},{12,14},{14,12},{1,3},{3,1},... | collective-permute-start | bytes 301064 | tf_op jit(solution)/shard_map/ppermute | solution.py:344
  14.1 0.4 %collective-permute-done.2.refs_1_ = bf16[392,128]{1,0:T(8,128)(2,1)S(1)} collective-permute-done((bf16[392,128]{1,0:T(8,128)(2,1)S(1)}, bf16[392,128]{1,0:T(8,128)(2,1)S(1)}, u32[]{:S(2)}, u32[]{:S(2)}) %collective-permute-start.2) | collective-permute-done | bytes 100384 | tf_op jit(solution)/shard_map/ppermute | solution.py:344
  14.5 1.3 %collective-permute-start.7 = (bf16[392,128]{1,0:T(8,128)(2,1)S(1)}, bf16[392,128]{1,0:T(8,128)(2,1)S(1)}, u32[]{:S(2)}, u32[]{:S(2)}) collective-permute-start(bf16[392,128]{1,0:T(8,128)(2,1)S(1)} %get-tuple-element.41), channel_id=1, source_target_pairs={{0,12},{2,14},{4,8},{6,10},{8,4},{10,6},{12,0},{14,2},{1,13},{3,15... | collective-permute-start | bytes 301064 | tf_op jit(solution)/shard_map/ppermute | solution.py:344
  15.8 0.0 copy-done
  15.8 0.0 copy-done.1
  15.8 0.0 copy-done.4
  15.8 1.4 %attend_first.1 = (f32[16,96,128]{2,1,0:T(8,128)S(1)}, f32[16,96,128]{2,1,0:T(8,128)S(1)}, f32[2,96,128]{2,1,0:T(8,128)S(1)}, f32[8,128]{1,0:T(8,128)S(1)}, f32[16,96,128]{2,1,0:T(8,128)S(1)}) custom-call(bf16[80,2048]{1,0:T(8,128)(2,1)S(1)} %copy-done, bf16[80,512]{1,0:T(8,128)(2,1)S(1)} %copy-done.1, s32[1,8]{1,0:T(1,128)S(1)} %copy-done.4, ...), custom_call_target="tpu_custom_call" | custom-call | flops 16777216 | bytes 4194304 | tf_op jit(solution)/shard_map/attend_first/pallas_call | solution.py:287
  17.2 0.8 %collective-permute-done.3.refs_2_ = bf16[392,128]{1,0:T(8,128)(2,1)S(1)} collective-permute-done((bf16[392,128]{1,0:T(8,128)(2,1)S(1)}, bf16[392,128]{1,0:T(8,128)(2,1)S(1)}, u32[]{:S(2)}, u32[]{:S(2)}) %collective-permute-start.3) | collective-permute-done | bytes 100384 | tf_op jit(solution)/shard_map/ppermute | solution.py:344
  18.0 1.1 %attend_more.2.acc_in = f32[16,96,128]{2,1,0:T(8,128)S(1)} custom-call(f32[8,128]{1,0:T(8,128)S(1)} %get-tuple-element.30.table_ref, f32[16,96,128]{2,1,0:T(8,128)S(1)} %get-tuple-element.31.q_ref, f32[16,96,128]{2,1,0:T(8,128)S(1)} %get-tuple-element.32.score_ref, f32[2,96,128]{2,1,0:T(8,128)S(1)} %get-tuple-element.33.value_ref, ...), custom_call_target="tpu_custom_call", output_to_operand_aliasing={{}: (4, {})} | custom-call | flops 16777216 | bytes 4194304 | tf_op jit(solution)/shard_map/attend_more/pallas_call | solution.py:321
  19.2 0.4 %collective-permute-done.4.refs_0_ = bf16[392,128]{1,0:T(8,128)(2,1)S(1)} collective-permute-done((bf16[392,128]{1,0:T(8,128)(2,1)S(1)}, bf16[392,128]{1,0:T(8,128)(2,1)S(1)}, u32[]{:S(2)}, u32[]{:S(2)}) %collective-permute-start.4) | collective-permute-done | bytes 100384 | tf_op jit(solution)/shard_map/ppermute | solution.py:344
  19.6 7.0 %collective-permute-done.5.refs_1_ = bf16[392,128]{1,0:T(8,128)(2,1)S(1)} collective-permute-done((bf16[392,128]{1,0:T(8,128)(2,1)S(1)}, bf16[392,128]{1,0:T(8,128)(2,1)S(1)}, u32[]{:S(2)}, u32[]{:S(2)}) %collective-permute-start.5) | collective-permute-done | bytes 100384 | tf_op jit(solution)/shard_map/ppermute | solution.py:344
  26.6 0.0 collective-permute-done.6.refs_2_
  26.6 1.1 %attend_more.3.acc_in = f32[16,96,128]{2,1,0:T(8,128)S(1)} custom-call(f32[8,128]{1,0:T(8,128)S(1)} %get-tuple-element.30.table_ref, f32[16,96,128]{2,1,0:T(8,128)S(1)} %get-tuple-element.31.q_ref, f32[16,96,128]{2,1,0:T(8,128)S(1)} %get-tuple-element.32.score_ref, f32[2,96,128]{2,1,0:T(8,128)S(1)} %get-tuple-element.33.value_ref, ...), custom_call_target="tpu_custom_call", output_to_operand_aliasing={{}: (4, {})} | custom-call | flops 16777216 | bytes 4194304 | tf_op jit(solution)/shard_map/attend_more/pallas_call | solution.py:321
  27.7 1.1 %collective-permute-done.7.refs_0_ = bf16[392,128]{1,0:T(8,128)(2,1)S(1)} collective-permute-done((bf16[392,128]{1,0:T(8,128)(2,1)S(1)}, bf16[392,128]{1,0:T(8,128)(2,1)S(1)}, u32[]{:S(2)}, u32[]{:S(2)}) %collective-permute-start.7) | collective-permute-done | bytes 100384 | tf_op jit(solution)/shard_map/ppermute | solution.py:344
  28.8 1.5 %attend_last.1 = (f32[16,96,128]{2,1,0:T(8,128)S(1)}, bf16[80,2048]{1,0:T(8,128)(2,1)}) custom-call(f32[8,128]{1,0:T(8,128)S(1)} %get-tuple-element.30.table_ref, f32[16,96,128]{2,1,0:T(8,128)S(1)} %get-tuple-element.31.q_ref, f32[16,96,128]{2,1,0:T(8,128)S(1)} %get-tuple-element.32.score_ref, ...), custom_call_target="tpu_custom_call", output_to_operand_aliasing={{0}: (4, {})} | custom-call | flops 16777216 | bytes 4194304 | tf_op jit(solution)/shard_map/attend_last/pallas_call | solution.py:321
  (1 shorter events, 0.0 us)
Async XLA Ops:
  0.0 4.8 %copy-start.2 = (s32[1,8]{1,0:T(1,128)S(1)}, s32[1,8]{1,0:T(1,128)}, u32[]{:S(2)}) copy-start(s32[1,8]{1,0:T(1,128)} %len_hbm.1) | copy-start | bytes 100
  0.0 4.8 %copy-start.3 = (s32[1,8]{1,0:T(1,128)S(1)}, s32[1,8]{1,0:T(1,128)}, u32[]{:S(2)}) copy-start(s32[1,8]{1,0:T(1,128)} %host_hbm.1) | copy-start | bytes 100
  4.0 3.5 %collective-permute-start = (f32[256,640]{1,0:T(8,128)S(1)}, f32[256,640]{1,0:T(8,128)S(1)}, u32[]{:S(2)}, u32[]{:S(2)}) collective-permute-start(f32[256,640]{1,0:T(8,128)S(1)} %get-tuple-element.26.send_ref), channel_id=1, source_target_pairs={{0,1},{1,0},{2,3},{3,2},{4,5},{5,4},{6,7},{7,6},{8,9},{9,8},{10,11... | collective-permute-start | bytes 1966088 | tf_op jit(solution)/shard_map/ppermute | solution.py:338
  7.4 8.4 %copy-start = (bf16[80,2048]{1,0:T(8,128)(2,1)S(1)}, bf16[80,2048]{1,0:T(8,128)(2,1)}, u32[]{:S(2)}) copy-start(bf16[80,2048]{1,0:T(8,128)(2,1)} %query_ref.1) | copy-start | bytes 983044
  7.5 8.4 %copy-start.1 = (bf16[80,512]{1,0:T(8,128)(2,1)S(1)}, bf16[80,512]{1,0:T(8,128)(2,1)}, u32[]{:S(2)}) copy-start(bf16[80,512]{1,0:T(8,128)(2,1)} %own_ref.1) | copy-start | bytes 245764
  7.5 8.3 %copy-start.4 = (s32[1,8]{1,0:T(1,128)S(1)}, s32[1,8]{1,0:T(1,128)}, u32[]{:S(2)}) copy-start(s32[1,8]{1,0:T(1,128)} %count_ref.1) | copy-start | bytes 100
  8.0 5.4 %collective-permute-start.1 = (bf16[392,128]{1,0:T(8,128)(2,1)S(1)}, bf16[392,128]{1,0:T(8,128)(2,1)S(1)}, u32[]{:S(2)}, u32[]{:S(2)}) collective-permute-start(bf16[392,128]{1,0:T(8,128)(2,1)S(1)} %get-tuple-element.35), channel_id=1, source_target_pairs={{0,8},{2,10},{4,12},{6,14},{8,0},{10,2},{12,4},{14,6},{1,9},{3,11}... | collective-permute-start | bytes 301064 | tf_op jit(solution)/shard_map/ppermute | solution.py:344
  8.1 6.5 %collective-permute-start.2 = (bf16[392,128]{1,0:T(8,128)(2,1)S(1)}, bf16[392,128]{1,0:T(8,128)(2,1)S(1)}, u32[]{:S(2)}, u32[]{:S(2)}) collective-permute-start(bf16[392,128]{1,0:T(8,128)(2,1)S(1)} %get-tuple-element.36), channel_id=1, source_target_pairs={{0,4},{2,6},{4,0},{6,2},{8,12},{10,14},{12,8},{14,10},{1,5},{3,7},... | collective-permute-start | bytes 301064 | tf_op jit(solution)/shard_map/ppermute | solution.py:344
  9.4 8.6 %collective-permute-start.3 = (bf16[392,128]{1,0:T(8,128)(2,1)S(1)}, bf16[392,128]{1,0:T(8,128)(2,1)S(1)}, u32[]{:S(2)}, u32[]{:S(2)}) collective-permute-start(bf16[392,128]{1,0:T(8,128)(2,1)S(1)} %get-tuple-element.37), channel_id=1, source_target_pairs={{0,10},{2,8},{4,14},{6,12},{8,2},{10,0},{12,6},{14,4},{1,11},{3,9}... | collective-permute-start | bytes 301064 | tf_op jit(solution)/shard_map/ppermute | solution.py:344
  11.6 8.0 %collective-permute-start.4 = (bf16[392,128]{1,0:T(8,128)(2,1)S(1)}, bf16[392,128]{1,0:T(8,128)(2,1)S(1)}, u32[]{:S(2)}, u32[]{:S(2)}) collective-permute-start(bf16[392,128]{1,0:T(8,128)(2,1)S(1)} %get-tuple-element.38), channel_id=1, source_target_pairs={{0,6},{2,4},{4,2},{6,0},{8,14},{10,12},{12,10},{14,8},{1,7},{3,5},... | collective-permute-start | bytes 301064 | tf_op jit(solution)/shard_map/ppermute | solution.py:344
  12.8 13.8 %collective-permute-start.5 = (bf16[392,128]{1,0:T(8,128)(2,1)S(1)}, bf16[392,128]{1,0:T(8,128)(2,1)S(1)}, u32[]{:S(2)}, u32[]{:S(2)}) collective-permute-start(bf16[392,128]{1,0:T(8,128)(2,1)S(1)} %get-tuple-element.39), channel_id=1, source_target_pairs={{0,14},{2,12},{4,10},{6,8},{8,6},{10,4},{12,2},{14,0},{1,15},{3,13... | collective-permute-start | bytes 301064 | tf_op jit(solution)/shard_map/ppermute | solution.py:344
  13.4 13.2 %collective-permute-start.6 = (bf16[392,128]{1,0:T(8,128)(2,1)S(1)}, bf16[392,128]{1,0:T(8,128)(2,1)S(1)}, u32[]{:S(2)}, u32[]{:S(2)}) collective-permute-start(bf16[392,128]{1,0:T(8,128)(2,1)S(1)} %get-tuple-element.40), channel_id=1, source_target_pairs={{0,2},{2,0},{4,6},{6,4},{8,10},{10,8},{12,14},{14,12},{1,3},{3,1},... | collective-permute-start | bytes 301064 | tf_op jit(solution)/shard_map/ppermute | solution.py:344
  14.5 14.2 %collective-permute-start.7 = (bf16[392,128]{1,0:T(8,128)(2,1)S(1)}, bf16[392,128]{1,0:T(8,128)(2,1)S(1)}, u32[]{:S(2)}, u32[]{:S(2)}) collective-permute-start(bf16[392,128]{1,0:T(8,128)(2,1)S(1)} %get-tuple-element.41), channel_id=1, source_target_pairs={{0,12},{2,14},{4,8},{6,10},{8,4},{10,6},{12,0},{14,2},{1,13},{3,15... | collective-permute-start | bytes 301064 | tf_op jit(solution)/shard_map/ppermute | solution.py:344

commit v8 on v7

--- a/solution.py
+++ b/solution.py
@@ -13,7 +13,7 @@
 BMAX = 16
 MAXLEN = 96
 META = 8
-STEP = 1024
+STEP = 512
 GROUP = 8
 FRONT = 2
 ORDER = (4, 2, 5, 3, 7, 1, 6)
@@ -66,7 +66,7 @@
     lax.fori_loop(0, steps, begin, 0)
     gain_copy.wait()
     gain_ref[...] = gain_buf[...].astype(jnp.float32)
-    lax.fori_loop(0, steps, step, 0)
+    lax.fori_loop(0, steps, step, 0, unroll=2)
 
 
 def make_picks(order, me, rows, len_ref, host_ref, pick_ref, meta_ref, slot_ref, start_ref):
@@ -344,7 +344,7 @@
         got[k] = lax.ppermute(blocks[k], "section", [(s, s ^ k) for s in range(sections)])
     q, score, value, table, acc = attend_first(beam_query, beam_newkv, beam_counts, blocks[0])
     order = ORDER if sections == len(ORDER) + 1 else tuple(range(sections - 1, 0, -1))
-    for part in (order[:3], order[3:-1]):
+    for part in (order[:4], order[4:-1]):
         (acc,) = attend_later(table, q, score, value, acc, [got[k] for k in part], None)
     late = [got[order[-1]]]
     out_shape = jax.ShapeDtypeStruct(beam_query.shape, jnp.bfloat16)

time: 30.4 us -> 30.4 us (level)
  the two profiles are of different devices: /device:TPU:23 before, /device:TPU:21 now
where the time goes in v8:
time: 30.4 us; the launch traced here: 30.3 us
  Pallas kernels  12.2 us (40%)
  waiting for transfers between devices  10.2 us (34%)
  starting transfers between devices  7.72 us (25%)
    ppermute x7, waiting for transfers between devices, per_device(): lax.ppermute(blocks[k], 'section', [(s, s ^ k) for s in range(sections)])  10.2 us
    ppermute x7, starting transfers between devices, per_device(): lax.ppermute(blocks[k], 'section', [(s, s ^ k) for s in range(sections)])  6.97 us
    pallas_call x1, Pallas kernels, project_send(): pl.pallas_call(project_send_kernel, out_shape=(jax.ShapeDtypeStruct((rows...  3.98 us
    pallas_call x3, Pallas kernels, attend_later(): pl.pallas_call(functools.partial(later_kernel, n_blocks=len(blocks), last...  3.66 us
    pallas_call x1, Pallas kernels, project_keep(): pl.pallas_call(functools.partial(project_keep_kernel, order=order), out_s...  2.74 us
    pallas_call x1, Pallas kernels, attend_first(): pl.pallas_call(first_kernel, out_shape=(tall, tall, jax.ShapeDtypeStruct(...  1.38 us
    ppermute x1, starting transfers between devices, per_device(): recv = lax.ppermute(send, 'tensor', [(0, 1), (1, 0)])  0.74 us
  transfers between devices with their start and end apart: 8, of which 6 were waited for; matrix products, arithmetic and copies ran while one was open for 0% of the time, Pallas kernels for 21%

profile of v8, /device:TPU:21, one launch (start us, length us, event | category | flops | bytes accessed | tf_op | source)
XLA Modules:
  0.0 30.3 jit_solution(15800121492265724155)
XLA Ops:
  0.0 0.0 copy-start.2
  0.0 4.0 %project_send.1 = (f32[256,640]{1,0:T(8,128)S(1)}, bf16[8,256,512]{2,1,0:T(8,128)(2,1)S(1)}) custom-call(bf16[256,4096]{1,0:T(8,128)(2,1)} %tok_ref.1, bf16[32,128]{1,0:T(8,128)(2,1)} %bitcast.1, bf16[4096,1024]{1,0:T(8,128)(2,1)} %w_ref.3), custom_call_target="tpu_custom_call" | custom-call | flops 1073741824 | bytes 6815744 | tf_op jit(solution)/shard_map/project_send/pallas_call | solution.py:123
  4.0 0.7 %collective-permute-start = (f32[256,640]{1,0:T(8,128)S(1)}, f32[256,640]{1,0:T(8,128)S(1)}, u32[]{:S(2)}, u32[]{:S(2)}) collective-permute-start(f32[256,640]{1,0:T(8,128)S(1)} %get-tuple-element.26.send_ref), channel_id=1, source_target_pairs={{0,1},{1,0},{2,3},{3,2},{4,5},{5,4},{6,7},{7,6},{8,9},{9,8},{10,11... | collective-permute-start | bytes 1966088 | tf_op jit(solution)/shard_map/ppermute | solution.py:338
  4.7 0.0 copy-done.2
  4.7 0.0 copy-done.3
  4.7 2.7 %project_keep.1 = (f32[256,512]{1,0:T(8,128)S(1)}, bf16[768,256]{1,0:T(8,128)(2,1)S(1)}, f32[8,8,128]{2,1,0:T(8,128)S(1)}) custom-call(s32[1,8]{1,0:T(1,128)S(1)} %copy-done.2, s32[1,8]{1,0:T(1,128)S(1)} %copy-done.3, bf16[8,256,512]{2,1,0:T(8,128)(2,1)S(1)} %get-tuple-element.24.scaled_ref, bf16[4096,1024]{1,0:T(8,128)(2,1)} %w_ref.3), custom_call_target="tpu_custom_call" | custom-call | flops 1073741824 | bytes 6815744 | tf_op jit(solution)/shard_map/project_keep/pallas_call | solution.py:151
  7.5 0.0 copy-start
  7.5 0.0 copy-start.1
  7.5 0.0 copy-start.4
  7.5 0.0 collective-permute-done.recv_ref
  7.5 0.5 %pack.1 = (bf16[392,128]{1,0:T(8,128)(2,1)S(1)}, bf16[392,128]{1,0:T(8,128)(2,1)S(1)}, bf16[392,128]{1,0:T(8,128)(2,1)S(1)}, bf16[392,128]{1,0:T(8,128)(2,1)S(1)...) custom-call(f32[256,512]{1,0:T(8,128)S(1)} %get-tuple-element.25.kee, ...), custom_call_target="tpu_custom_call" | custom-call | tf_op jit(solution)/shard_map/pack/pallas_call | solution.py:201
  8.0 0.1 collective-permute-start.1
  8.1 1.3 %collective-permute-start.2 = (bf16[392,128]{1,0:T(8,128)(2,1)S(1)}, bf16[392,128]{1,0:T(8,128)(2,1)S(1)}, u32[]{:S(2)}, u32[]{:S(2)}) collective-permute-start(bf16[392,128]{1,0:T(8,128)(2,1)S(1)} %get-tuple-element.36), channel_id=1, source_target_pairs={{0,4},{2,6},{4,0},{6,2},{8,12},{10,14},{12,8},{14,10},{1,5},{3,7},... | collective-permute-start | bytes 301064 | tf_op jit(solution)/shard_map/ppermute | solution.py:344
  9.4 2.2 %collective-permute-start.3 = (bf16[392,128]{1,0:T(8,128)(2,1)S(1)}, bf16[392,128]{1,0:T(8,128)(2,1)S(1)}, u32[]{:S(2)}, u32[]{:S(2)}) collective-permute-start(bf16[392,128]{1,0:T(8,128)(2,1)S(1)} %get-tuple-element.37), channel_id=1, source_target_pairs={{0,10},{2,8},{4,14},{6,12},{8,2},{10,0},{12,6},{14,4},{1,11},{3,9}... | collective-permute-start | bytes 301064 | tf_op jit(solution)/shard_map/ppermute | solution.py:344
  11.7 1.1 %collective-permute-start.4 = (bf16[392,128]{1,0:T(8,128)(2,1)S(1)}, bf16[392,128]{1,0:T(8,128)(2,1)S(1)}, u32[]{:S(2)}, u32[]{:S(2)}) collective-permute-start(bf16[392,128]{1,0:T(8,128)(2,1)S(1)} %get-tuple-element.38), channel_id=1, source_target_pairs={{0,6},{2,4},{4,2},{6,0},{8,14},{10,12},{12,10},{14,8},{1,7},{3,5},... | collective-permute-start | bytes 301064 | tf_op jit(solution)/shard_map/ppermute | solution.py:344
  12.8 0.1 collective-permute-start.5
  12.9 0.5 %collective-permute-done.1.refs_0_ = bf16[392,128]{1,0:T(8,128)(2,1)S(1)} collective-permute-done((bf16[392,128]{1,0:T(8,128)(2,1)S(1)}, bf16[392,128]{1,0:T(8,128)(2,1)S(1)}, u32[]{:S(2)}, u32[]{:S(2)}) %collective-permute-start.1) | collective-permute-done | bytes 100384 | tf_op jit(solution)/shard_map/ppermute | solution.py:344
  13.4 0.8 %collective-permute-start.6 = (bf16[392,128]{1,0:T(8,128)(2,1)S(1)}, bf16[392,128]{1,0:T(8,128)(2,1)S(1)}, u32[]{:S(2)}, u32[]{:S(2)}) collective-permute-start(bf16[392,128]{1,0:T(8,128)(2,1)S(1)} %get-tuple-element.40), channel_id=1, source_target_pairs={{0,2},{2,0},{4,6},{6,4},{8,10},{10,8},{12,14},{14,12},{1,3},{3,1},... | collective-permute-start | bytes 301064 | tf_op jit(solution)/shard_map/ppermute | solution.py:344
  14.2 0.4 %collective-permute-done.2.refs_1_ = bf16[392,128]{1,0:T(8,128)(2,1)S(1)} collective-permute-done((bf16[392,128]{1,0:T(8,128)(2,1)S(1)}, bf16[392,128]{1,0:T(8,128)(2,1)S(1)}, u32[]{:S(2)}, u32[]{:S(2)}) %collective-permute-start.2) | collective-permute-done | bytes 100384 | tf_op jit(solution)/shard_map/ppermute | solution.py:344
  14.6 1.3 %collective-permute-start.7 = (bf16[392,128]{1,0:T(8,128)(2,1)S(1)}, bf16[392,128]{1,0:T(8,128)(2,1)S(1)}, u32[]{:S(2)}, u32[]{:S(2)}) collective-permute-start(bf16[392,128]{1,0:T(8,128)(2,1)S(1)} %get-tuple-element.41), channel_id=1, source_target_pairs={{0,12},{2,14},{4,8},{6,10},{8,4},{10,6},{12,0},{14,2},{1,13},{3,15... | collective-permute-start | bytes 301064 | tf_op jit(solution)/shard_map/ppermute | solution.py:344
  15.8 0.0 copy-done
  15.8 0.0 copy-done.1
  15.8 0.0 copy-done.4
  15.8 1.4 %attend_first.1 = (f32[16,96,128]{2,1,0:T(8,128)S(1)}, f32[16,96,128]{2,1,0:T(8,128)S(1)}, f32[2,96,128]{2,1,0:T(8,128)S(1)}, f32[8,128]{1,0:T(8,128)S(1)}, f32[16,96,128]{2,1,0:T(8,128)S(1)}) custom-call(bf16[80,2048]{1,0:T(8,128)(2,1)S(1)} %copy-done, bf16[80,512]{1,0:T(8,128)(2,1)S(1)} %copy-done.1, s32[1,8]{1,0:T(1,128)S(1)} %copy-done.4, ...), custom_call_target="tpu_custom_call" | custom-call | flops 16777216 | bytes 4194304 | tf_op jit(solution)/shard_map/attend_first/pallas_call | solution.py:287
  17.2 0.8 %collective-permute-done.3.refs_2_ = bf16[392,128]{1,0:T(8,128)(2,1)S(1)} collective-permute-done((bf16[392,128]{1,0:T(8,128)(2,1)S(1)}, bf16[392,128]{1,0:T(8,128)(2,1)S(1)}, u32[]{:S(2)}, u32[]{:S(2)}) %collective-permute-start.3) | collective-permute-done | bytes 100384 | tf_op jit(solution)/shard_map/ppermute | solution.py:344
  18.1 1.6 %collective-permute-done.4.refs_3_ = bf16[392,128]{1,0:T(8,128)(2,1)S(1)} collective-permute-done((bf16[392,128]{1,0:T(8,128)(2,1)S(1)}, bf16[392,128]{1,0:T(8,128)(2,1)S(1)}, u32[]{:S(2)}, u32[]{:S(2)}) %collective-permute-start.4) | collective-permute-done | bytes 100384 | tf_op jit(solution)/shard_map/ppermute | solution.py:344
  19.6 1.5 %attend_more.2.acc_in = f32[16,96,128]{2,1,0:T(8,128)S(1)} custom-call(f32[8,128]{1,0:T(8,128)S(1)} %get-tuple-element.30.table_ref, f32[16,96,128]{2,1,0:T(8,128)S(1)} %get-tuple-element.31.q_ref, f32[16,96,128]{2,1,0:T(8,128)S(1)} %get-tuple-element.32.score_ref, f32[2,96,128]{2,1,0:T(8,128)S(1)} %get-tuple-element.33.value_ref, ...), custom_call_target="tpu_custom_call", output_to_operand_aliasing={{}: (4, {})} | custom-call | flops 16777216 | bytes 4194304 | tf_op jit(solution)/shard_map/attend_more/pallas_call | solution.py:321
  21.1 5.5 %collective-permute-done.5.refs_0_ = bf16[392,128]{1,0:T(8,128)(2,1)S(1)} collective-permute-done((bf16[392,128]{1,0:T(8,128)(2,1)S(1)}, bf16[392,128]{1,0:T(8,128)(2,1)S(1)}, u32[]{:S(2)}, u32[]{:S(2)}) %collective-permute-start.5) | collective-permute-done | bytes 100384 | tf_op jit(solution)/shard_map/ppermute | solution.py:344
  26.6 0.0 collective-permute-done.6.refs_1_
  26.6 0.7 %attend_more.3.acc_in = f32[16,96,128]{2,1,0:T(8,128)S(1)} custom-call(f32[8,128]{1,0:T(8,128)S(1)} %get-tuple-element.30.table_ref, f32[16,96,128]{2,1,0:T(8,128)S(1)} %get-tuple-element.31.q_ref, f32[16,96,128]{2,1,0:T(8,128)S(1)} %get-tuple-element.32.score_ref, f32[2,96,128]{2,1,0:T(8,128)S(1)} %get-tuple-element.33.value_ref, ...), custom_call_target="tpu_custom_call", output_to_operand_aliasing={{}: (4, {})} | custom-call | flops 16777216 | bytes 4194304 | tf_op jit(solution)/shard_map/attend_more/pallas_call | solution.py:321
  27.4 1.5 %collective-permute-done.7.refs_0_ = bf16[392,128]{1,0:T(8,128)(2,1)S(1)} collective-permute-done((bf16[392,128]{1,0:T(8,128)(2,1)S(1)}, bf16[392,128]{1,0:T(8,128)(2,1)S(1)}, u32[]{:S(2)}, u32[]{:S(2)}) %collective-permute-start.7) | collective-permute-done | bytes 100384 | tf_op jit(solution)/shard_map/ppermute | solution.py:344
  28.8 1.5 %attend_last.1 = (f32[16,96,128]{2,1,0:T(8,128)S(1)}, bf16[80,2048]{1,0:T(8,128)(2,1)}) custom-call(f32[8,128]{1,0:T(8,128)S(1)} %get-tuple-element.30.table_ref, f32[16,96,128]{2,1,0:T(8,128)S(1)} %get-tuple-element.31.q_ref, f32[16,96,128]{2,1,0:T(8,128)S(1)} %get-tuple-element.32.score_ref, ...), custom_call_target="tpu_custom_call", output_to_operand_aliasing={{0}: (4, {})} | custom-call | flops 16777216 | bytes 4194304 | tf_op jit(solution)/shard_map/attend_last/pallas_call | solution.py:321
  (1 shorter events, 0.0 us)
Async XLA Ops:
  0.0 4.7 %copy-start.2 = (s32[1,8]{1,0:T(1,128)S(1)}, s32[1,8]{1,0:T(1,128)}, u32[]{:S(2)}) copy-start(s32[1,8]{1,0:T(1,128)} %len_hbm.1) | copy-start | bytes 100
  0.0 4.7 %copy-start.3 = (s32[1,8]{1,0:T(1,128)S(1)}, s32[1,8]{1,0:T(1,128)}, u32[]{:S(2)}) copy-start(s32[1,8]{1,0:T(1,128)} %host_hbm.1) | copy-start | bytes 100
  4.0 3.5 %collective-permute-start = (f32[256,640]{1,0:T(8,128)S(1)}, f32[256,640]{1,0:T(8,128)S(1)}, u32[]{:S(2)}, u32[]{:S(2)}) collective-permute-start(f32[256,640]{1,0:T(8,128)S(1)} %get-tuple-element.26.send_ref), channel_id=1, source_target_pairs={{0,1},{1,0},{2,3},{3,2},{4,5},{5,4},{6,7},{7,6},{8,9},{9,8},{10,11... | collective-permute-start | bytes 1966088 | tf_op jit(solution)/shard_map/ppermute | solution.py:338
  7.5 8.4 %copy-start = (bf16[80,2048]{1,0:T(8,128)(2,1)S(1)}, bf16[80,2048]{1,0:T(8,128)(2,1)}, u32[]{:S(2)}) copy-start(bf16[80,2048]{1,0:T(8,128)(2,1)} %query_ref.1) | copy-start | bytes 983044
  7.5 8.3 %copy-start.1 = (bf16[80,512]{1,0:T(8,128)(2,1)S(1)}, bf16[80,512]{1,0:T(8,128)(2,1)}, u32[]{:S(2)}) copy-start(bf16[80,512]{1,0:T(8,128)(2,1)} %own_ref.1) | copy-start | bytes 245764
  7.5 8.3 %copy-start.4 = (s32[1,8]{1,0:T(1,128)S(1)}, s32[1,8]{1,0:T(1,128)}, u32[]{:S(2)}) copy-start(s32[1,8]{1,0:T(1,128)} %count_ref.1) | copy-start | bytes 100
  8.0 5.4 %collective-permute-start.1 = (bf16[392,128]{1,0:T(8,128)(2,1)S(1)}, bf16[392,128]{1,0:T(8,128)(2,1)S(1)}, u32[]{:S(2)}, u32[]{:S(2)}) collective-permute-start(bf16[392,128]{1,0:T(8,128)(2,1)S(1)} %get-tuple-element.35), channel_id=1, source_target_pairs={{0,8},{2,10},{4,12},{6,14},{8,0},{10,2},{12,4},{14,6},{1,9},{3,11}... | collective-permute-start | bytes 301064 | tf_op jit(solution)/shard_map/ppermute | solution.py:344
  8.1 6.4 %collective-permute-start.2 = (bf16[392,128]{1,0:T(8,128)(2,1)S(1)}, bf16[392,128]{1,0:T(8,128)(2,1)S(1)}, u32[]{:S(2)}, u32[]{:S(2)}) collective-permute-start(bf16[392,128]{1,0:T(8,128)(2,1)S(1)} %get-tuple-element.36), channel_id=1, source_target_pairs={{0,4},{2,6},{4,0},{6,2},{8,12},{10,14},{12,8},{14,10},{1,5},{3,7},... | collective-permute-start | bytes 301064 | tf_op jit(solution)/shard_map/ppermute | solution.py:344
  9.4 8.6 %collective-permute-start.3 = (bf16[392,128]{1,0:T(8,128)(2,1)S(1)}, bf16[392,128]{1,0:T(8,128)(2,1)S(1)}, u32[]{:S(2)}, u32[]{:S(2)}) collective-permute-start(bf16[392,128]{1,0:T(8,128)(2,1)S(1)} %get-tuple-element.37), channel_id=1, source_target_pairs={{0,10},{2,8},{4,14},{6,12},{8,2},{10,0},{12,6},{14,4},{1,11},{3,9}... | collective-permute-start | bytes 301064 | tf_op jit(solution)/shard_map/ppermute | solution.py:344
  11.7 8.0 %collective-permute-start.4 = (bf16[392,128]{1,0:T(8,128)(2,1)S(1)}, bf16[392,128]{1,0:T(8,128)(2,1)S(1)}, u32[]{:S(2)}, u32[]{:S(2)}) collective-permute-start(bf16[392,128]{1,0:T(8,128)(2,1)S(1)} %get-tuple-element.38), channel_id=1, source_target_pairs={{0,6},{2,4},{4,2},{6,0},{8,14},{10,12},{12,10},{14,8},{1,7},{3,5},... | collective-permute-start | bytes 301064 | tf_op jit(solution)/shard_map/ppermute | solution.py:344
  12.8 13.8 %collective-permute-start.5 = (bf16[392,128]{1,0:T(8,128)(2,1)S(1)}, bf16[392,128]{1,0:T(8,128)(2,1)S(1)}, u32[]{:S(2)}, u32[]{:S(2)}) collective-permute-start(bf16[392,128]{1,0:T(8,128)(2,1)S(1)} %get-tuple-element.39), channel_id=1, source_target_pairs={{0,14},{2,12},{4,10},{6,8},{8,6},{10,4},{12,2},{14,0},{1,15},{3,13... | collective-permute-start | bytes 301064 | tf_op jit(solution)/shard_map/ppermute | solution.py:344
  13.4 13.2 %collective-permute-start.6 = (bf16[392,128]{1,0:T(8,128)(2,1)S(1)}, bf16[392,128]{1,0:T(8,128)(2,1)S(1)}, u32[]{:S(2)}, u32[]{:S(2)}) collective-permute-start(bf16[392,128]{1,0:T(8,128)(2,1)S(1)} %get-tuple-element.40), channel_id=1, source_target_pairs={{0,2},{2,0},{4,6},{6,4},{8,10},{10,8},{12,14},{14,12},{1,3},{3,1},... | collective-permute-start | bytes 301064 | tf_op jit(solution)/shard_map/ppermute | solution.py:344
  14.6 14.3 %collective-permute-start.7 = (bf16[392,128]{1,0:T(8,128)(2,1)S(1)}, bf16[392,128]{1,0:T(8,128)(2,1)S(1)}, u32[]{:S(2)}, u32[]{:S(2)}) collective-permute-start(bf16[392,128]{1,0:T(8,128)(2,1)S(1)} %get-tuple-element.41), channel_id=1, source_target_pairs={{0,12},{2,14},{4,8},{6,10},{8,4},{10,6},{12,0},{14,2},{1,13},{3,15... | collective-permute-start | bytes 301064 | tf_op jit(solution)/shard_map/ppermute | solution.py:344

commit v9 on v8

--- a/solution.py
+++ b/solution.py
@@ -66,7 +66,7 @@
     lax.fori_loop(0, steps, begin, 0)
     gain_copy.wait()
     gain_ref[...] = gain_buf[...].astype(jnp.float32)
-    lax.fori_loop(0, steps, step, 0, unroll=2)
+    lax.fori_loop(0, steps, step, 0, unroll=4)
 
 
 def make_picks(order, me, rows, len_ref, host_ref, pick_ref, meta_ref, slot_ref, start_ref):

time: 30.4 us -> 30.2 us (level)
  the two profiles are of different devices: /device:TPU:21 before, /device:TPU:19 now
where the time goes in v9:
time: 30.2 us; the launch traced here: 30.1 us
  Pallas kernels  12 us (40%)
  starting transfers between devices  9.04 us (30%)
  waiting for transfers between devices  8.92 us (30%)
    ppermute x7, waiting for transfers between devices, per_device(): lax.ppermute(blocks[k], 'section', [(s, s ^ k) for s in range(sections)])  8.92 us
    ppermute x7, starting transfers between devices, per_device(): lax.ppermute(blocks[k], 'section', [(s, s ^ k) for s in range(sections)])  8.3 us
    pallas_call x1, Pallas kernels, project_send(): pl.pallas_call(project_send_kernel, out_shape=(jax.ShapeDtypeStruct((rows...  3.75 us
    pallas_call x3, Pallas kernels, attend_later(): pl.pallas_call(functools.partial(later_kernel, n_blocks=len(blocks), last...  3.66 us
    pallas_call x1, Pallas kernels, project_keep(): pl.pallas_call(functools.partial(project_keep_kernel, order=order), out_s...  2.74 us
    pallas_call x1, Pallas kernels, attend_first(): pl.pallas_call(first_kernel, out_shape=(tall, tall, jax.ShapeDtypeStruct(...  1.38 us
    ppermute x1, starting transfers between devices, per_device(): recv = lax.ppermute(send, 'tensor', [(0, 1), (1, 0)])  0.74 us
  transfers between devices with their start and end apart: 8, of which 4 were waited for; matrix products, arithmetic and copies ran while one was open for 0% of the time, Pallas kernels for 21%

profile of v9, /device:TPU:19, one launch (start us, length us, event | category | flops | bytes accessed | tf_op | source)
XLA Modules:
  0.0 30.1 jit_solution(14584921238127719079)
XLA Ops:
  0.0 0.0 copy-start.3
  0.0 3.7 %project_send.1 = (f32[256,640]{1,0:T(8,128)S(1)}, bf16[8,256,512]{2,1,0:T(8,128)(2,1)S(1)}) custom-call(bf16[256,4096]{1,0:T(8,128)(2,1)} %tok_ref.1, bf16[32,128]{1,0:T(8,128)(2,1)} %bitcast.1, bf16[4096,1024]{1,0:T(8,128)(2,1)} %w_ref.3), custom_call_target="tpu_custom_call" | custom-call | flops 1073741824 | bytes 6815744 | tf_op jit(solution)/shard_map/project_send/pallas_call | solution.py:123
  3.8 0.7 %collective-permute-start = (f32[256,640]{1,0:T(8,128)S(1)}, f32[256,640]{1,0:T(8,128)S(1)}, u32[]{:S(2)}, u32[]{:S(2)}) collective-permute-start(f32[256,640]{1,0:T(8,128)S(1)} %get-tuple-element.26.send_ref), channel_id=1, source_target_pairs={{0,1},{1,0},{2,3},{3,2},{4,5},{5,4},{6,7},{7,6},{8,9},{9,8},{10,11... | collective-permute-start | bytes 1966088 | tf_op jit(solution)/shard_map/ppermute | solution.py:338
  4.5 0.0 copy-done.2
  4.5 0.0 copy-done.3
  4.5 2.7 %project_keep.1 = (f32[256,512]{1,0:T(8,128)S(1)}, bf16[768,256]{1,0:T(8,128)(2,1)S(1)}, f32[8,8,128]{2,1,0:T(8,128)S(1)}) custom-call(s32[1,8]{1,0:T(1,128)S(1)} %copy-done.2, s32[1,8]{1,0:T(1,128)S(1)} %copy-done.3, bf16[8,256,512]{2,1,0:T(8,128)(2,1)S(1)} %get-tuple-element.24.scaled_ref, bf16[4096,1024]{1,0:T(8,128)(2,1)} %w_ref.3), custom_call_target="tpu_custom_call" | custom-call | flops 1073741824 | bytes 6815744 | tf_op jit(solution)/shard_map/project_keep/pallas_call | solution.py:151
  7.3 0.0 copy-start
  7.3 0.0 copy-start.1
  7.3 0.0 copy-start.4
  7.3 0.0 collective-permute-done.recv_ref
  7.3 0.5 %pack.1 = (bf16[392,128]{1,0:T(8,128)(2,1)S(1)}, bf16[392,128]{1,0:T(8,128)(2,1)S(1)}, bf16[392,128]{1,0:T(8,128)(2,1)S(1)}, bf16[392,128]{1,0:T(8,128)(2,1)S(1)...) custom-call(f32[256,512]{1,0:T(8,128)S(1)} %get-tuple-element.25.kee, ...), custom_call_target="tpu_custom_call" | custom-call | tf_op jit(solution)/shard_map/pack/pallas_call | solution.py:201
  7.8 0.1 collective-permute-start.1
  7.9 1.3 %collective-permute-start.2 = (bf16[392,128]{1,0:T(8,128)(2,1)S(1)}, bf16[392,128]{1,0:T(8,128)(2,1)S(1)}, u32[]{:S(2)}, u32[]{:S(2)}) collective-permute-start(bf16[392,128]{1,0:T(8,128)(2,1)S(1)} %get-tuple-element.36), channel_id=1, source_target_pairs={{0,4},{2,6},{4,0},{6,2},{8,12},{10,14},{12,8},{14,10},{1,5},{3,7},... | collective-permute-start | bytes 301064 | tf_op jit(solution)/shard_map/ppermute | solution.py:344
  9.2 3.2 %collective-permute-start.3 = (bf16[392,128]{1,0:T(8,128)(2,1)S(1)}, bf16[392,128]{1,0:T(8,128)(2,1)S(1)}, u32[]{:S(2)}, u32[]{:S(2)}) collective-permute-start(bf16[392,128]{1,0:T(8,128)(2,1)S(1)} %get-tuple-element.37), channel_id=1, source_target_pairs={{0,10},{2,8},{4,14},{6,12},{8,2},{10,0},{12,6},{14,4},{1,11},{3,9}... | collective-permute-start | bytes 301064 | tf_op jit(solution)/shard_map/ppermute | solution.py:344
  12.5 0.1 collective-permute-start.4
  12.6 1.1 %collective-permute-start.5 = (bf16[392,128]{1,0:T(8,128)(2,1)S(1)}, bf16[392,128]{1,0:T(8,128)(2,1)S(1)}, u32[]{:S(2)}, u32[]{:S(2)}) collective-permute-start(bf16[392,128]{1,0:T(8,128)(2,1)S(1)} %get-tuple-element.39), channel_id=1, source_target_pairs={{0,14},{2,12},{4,10},{6,8},{8,6},{10,4},{12,2},{14,0},{1,15},{3,13... | collective-permute-start | bytes 301064 | tf_op jit(solution)/shard_map/ppermute | solution.py:344
  13.7 0.0 collective-permute-done.1.refs_0_
  13.7 0.7 %collective-permute-start.6 = (bf16[392,128]{1,0:T(8,128)(2,1)S(1)}, bf16[392,128]{1,0:T(8,128)(2,1)S(1)}, u32[]{:S(2)}, u32[]{:S(2)}) collective-permute-start(bf16[392,128]{1,0:T(8,128)(2,1)S(1)} %get-tuple-element.40), channel_id=1, source_target_pairs={{0,2},{2,0},{4,6},{6,4},{8,10},{10,8},{12,14},{14,12},{1,3},{3,1},... | collective-permute-start | bytes 301064 | tf_op jit(solution)/shard_map/ppermute | solution.py:344
  14.4 0.0 collective-permute-done.2.refs_1_
  14.4 1.7 %collective-permute-start.7 = (bf16[392,128]{1,0:T(8,128)(2,1)S(1)}, bf16[392,128]{1,0:T(8,128)(2,1)S(1)}, u32[]{:S(2)}, u32[]{:S(2)}) collective-permute-start(bf16[392,128]{1,0:T(8,128)(2,1)S(1)} %get-tuple-element.41), channel_id=1, source_target_pairs={{0,12},{2,14},{4,8},{6,10},{8,4},{10,6},{12,0},{14,2},{1,13},{3,15... | collective-permute-start | bytes 301064 | tf_op jit(solution)/shard_map/ppermute | solution.py:344
  16.1 0.0 copy-done
  16.1 0.0 copy-done.1
  16.1 0.0 copy-done.4
  16.1 1.4 %attend_first.1 = (f32[16,96,128]{2,1,0:T(8,128)S(1)}, f32[16,96,128]{2,1,0:T(8,128)S(1)}, f32[2,96,128]{2,1,0:T(8,128)S(1)}, f32[8,128]{1,0:T(8,128)S(1)}, f32[16,96,128]{2,1,0:T(8,128)S(1)}) custom-call(bf16[80,2048]{1,0:T(8,128)(2,1)S(1)} %copy-done, bf16[80,512]{1,0:T(8,128)(2,1)S(1)} %copy-done.1, s32[1,8]{1,0:T(1,128)S(1)} %copy-done.4, ...), custom_call_target="tpu_custom_call" | custom-call | flops 16777216 | bytes 4194304 | tf_op jit(solution)/shard_map/attend_first/pallas_call | solution.py:287
  17.5 1.4 %collective-permute-done.3.refs_2_ = bf16[392,128]{1,0:T(8,128)(2,1)S(1)} collective-permute-done((bf16[392,128]{1,0:T(8,128)(2,1)S(1)}, bf16[392,128]{1,0:T(8,128)(2,1)S(1)}, u32[]{:S(2)}, u32[]{:S(2)}) %collective-permute-start.3) | collective-permute-done | bytes 100384 | tf_op jit(solution)/shard_map/ppermute | solution.py:344
  18.8 1.6 %collective-permute-done.4.refs_3_ = bf16[392,128]{1,0:T(8,128)(2,1)S(1)} collective-permute-done((bf16[392,128]{1,0:T(8,128)(2,1)S(1)}, bf16[392,128]{1,0:T(8,128)(2,1)S(1)}, u32[]{:S(2)}, u32[]{:S(2)}) %collective-permute-start.4) | collective-permute-done | bytes 100384 | tf_op jit(solution)/shard_map/ppermute | solution.py:344
  20.4 1.5 %attend_more.2.acc_in = f32[16,96,128]{2,1,0:T(8,128)S(1)} custom-call(f32[8,128]{1,0:T(8,128)S(1)} %get-tuple-element.30.table_ref, f32[16,96,128]{2,1,0:T(8,128)S(1)} %get-tuple-element.31.q_ref, f32[16,96,128]{2,1,0:T(8,128)S(1)} %get-tuple-element.32.score_ref, f32[2,96,128]{2,1,0:T(8,128)S(1)} %get-tuple-element.33.value_ref, ...), custom_call_target="tpu_custom_call", output_to_operand_aliasing={{}: (4, {})} | custom-call | flops 16777216 | bytes 4194304 | tf_op jit(solution)/shard_map/attend_more/pallas_call | solution.py:321
  21.9 5.5 %collective-permute-done.5.refs_0_ = bf16[392,128]{1,0:T(8,128)(2,1)S(1)} collective-permute-done((bf16[392,128]{1,0:T(8,128)(2,1)S(1)}, bf16[392,128]{1,0:T(8,128)(2,1)S(1)}, u32[]{:S(2)}, u32[]{:S(2)}) %collective-permute-start.5) | collective-permute-done | bytes 100384 | tf_op jit(solution)/shard_map/ppermute | solution.py:344
  27.4 0.0 collective-permute-done.6.refs_1_
  27.4 0.7 %attend_more.3.acc_in = f32[16,96,128]{2,1,0:T(8,128)S(1)} custom-call(f32[8,128]{1,0:T(8,128)S(1)} %get-tuple-element.30.table_ref, f32[16,96,128]{2,1,0:T(8,128)S(1)} %get-tuple-element.31.q_ref, f32[16,96,128]{2,1,0:T(8,128)S(1)} %get-tuple-element.32.score_ref, f32[2,96,128]{2,1,0:T(8,128)S(1)} %get-tuple-element.33.value_ref, ...), custom_call_target="tpu_custom_call", output_to_operand_aliasing={{}: (4, {})} | custom-call | flops 16777216 | bytes 4194304 | tf_op jit(solution)/shard_map/attend_more/pallas_call | solution.py:321
  28.2 0.4 %collective-permute-done.7.refs_0_ = bf16[392,128]{1,0:T(8,128)(2,1)S(1)} collective-permute-done((bf16[392,128]{1,0:T(8,128)(2,1)S(1)}, bf16[392,128]{1,0:T(8,128)(2,1)S(1)}, u32[]{:S(2)}, u32[]{:S(2)}) %collective-permute-start.7) | collective-permute-done | bytes 100384 | tf_op jit(solution)/shard_map/ppermute | solution.py:344
  28.6 1.5 %attend_last.1 = (f32[16,96,128]{2,1,0:T(8,128)S(1)}, bf16[80,2048]{1,0:T(8,128)(2,1)}) custom-call(f32[8,128]{1,0:T(8,128)S(1)} %get-tuple-element.30.table_ref, f32[16,96,128]{2,1,0:T(8,128)S(1)} %get-tuple-element.31.q_ref, f32[16,96,128]{2,1,0:T(8,128)S(1)} %get-tuple-element.32.score_ref, ...), custom_call_target="tpu_custom_call", output_to_operand_aliasing={{0}: (4, {})} | custom-call | flops 16777216 | bytes 4194304 | tf_op jit(solution)/shard_map/attend_last/pallas_call | solution.py:321
  (1 shorter events, 0.0 us)
Async XLA Ops:
  0.0 4.5 %copy-start.2 = (s32[1,8]{1,0:T(1,128)S(1)}, s32[1,8]{1,0:T(1,128)}, u32[]{:S(2)}) copy-start(s32[1,8]{1,0:T(1,128)} %len_hbm.1) | copy-start | bytes 100
  0.0 4.5 %copy-start.3 = (s32[1,8]{1,0:T(1,128)S(1)}, s32[1,8]{1,0:T(1,128)}, u32[]{:S(2)}) copy-start(s32[1,8]{1,0:T(1,128)} %host_hbm.1) | copy-start | bytes 100
  3.8 3.5 %collective-permute-start = (f32[256,640]{1,0:T(8,128)S(1)}, f32[256,640]{1,0:T(8,128)S(1)}, u32[]{:S(2)}, u32[]{:S(2)}) collective-permute-start(f32[256,640]{1,0:T(8,128)S(1)} %get-tuple-element.26.send_ref), channel_id=1, source_target_pairs={{0,1},{1,0},{2,3},{3,2},{4,5},{5,4},{6,7},{7,6},{8,9},{9,8},{10,11... | collective-permute-start | bytes 1966088 | tf_op jit(solution)/shard_map/ppermute | solution.py:338
  7.3 8.8 %copy-start = (bf16[80,2048]{1,0:T(8,128)(2,1)S(1)}, bf16[80,2048]{1,0:T(8,128)(2,1)}, u32[]{:S(2)}) copy-start(bf16[80,2048]{1,0:T(8,128)(2,1)} %query_ref.1) | copy-start | bytes 983044
  7.3 8.8 %copy-start.1 = (bf16[80,512]{1,0:T(8,128)(2,1)S(1)}, bf16[80,512]{1,0:T(8,128)(2,1)}, u32[]{:S(2)}) copy-start(bf16[80,512]{1,0:T(8,128)(2,1)} %own_ref.1) | copy-start | bytes 245764
  7.3 8.8 %copy-start.4 = (s32[1,8]{1,0:T(1,128)S(1)}, s32[1,8]{1,0:T(1,128)}, u32[]{:S(2)}) copy-start(s32[1,8]{1,0:T(1,128)} %count_ref.1) | copy-start | bytes 100
  7.8 5.9 %collective-permute-start.1 = (bf16[392,128]{1,0:T(8,128)(2,1)S(1)}, bf16[392,128]{1,0:T(8,128)(2,1)S(1)}, u32[]{:S(2)}, u32[]{:S(2)}) collective-permute-start(bf16[392,128]{1,0:T(8,128)(2,1)S(1)} %get-tuple-element.35), channel_id=1, source_target_pairs={{0,8},{2,10},{4,12},{6,14},{8,0},{10,2},{12,4},{14,6},{1,9},{3,11}... | collective-permute-start | bytes 301064 | tf_op jit(solution)/shard_map/ppermute | solution.py:344
  7.9 6.5 %collective-permute-start.2 = (bf16[392,128]{1,0:T(8,128)(2,1)S(1)}, bf16[392,128]{1,0:T(8,128)(2,1)S(1)}, u32[]{:S(2)}, u32[]{:S(2)}) collective-permute-start(bf16[392,128]{1,0:T(8,128)(2,1)S(1)} %get-tuple-element.36), channel_id=1, source_target_pairs={{0,4},{2,6},{4,0},{6,2},{8,12},{10,14},{12,8},{14,10},{1,5},{3,7},... | collective-permute-start | bytes 301064 | tf_op jit(solution)/shard_map/ppermute | solution.py:344
  9.2 9.6 %collective-permute-start.3 = (bf16[392,128]{1,0:T(8,128)(2,1)S(1)}, bf16[392,128]{1,0:T(8,128)(2,1)S(1)}, u32[]{:S(2)}, u32[]{:S(2)}) collective-permute-start(bf16[392,128]{1,0:T(8,128)(2,1)S(1)} %get-tuple-element.37), channel_id=1, source_target_pairs={{0,10},{2,8},{4,14},{6,12},{8,2},{10,0},{12,6},{14,4},{1,11},{3,9}... | collective-permute-start | bytes 301064 | tf_op jit(solution)/shard_map/ppermute | solution.py:344
  12.5 8.0 %collective-permute-start.4 = (bf16[392,128]{1,0:T(8,128)(2,1)S(1)}, bf16[392,128]{1,0:T(8,128)(2,1)S(1)}, u32[]{:S(2)}, u32[]{:S(2)}) collective-permute-start(bf16[392,128]{1,0:T(8,128)(2,1)S(1)} %get-tuple-element.38), channel_id=1, source_target_pairs={{0,6},{2,4},{4,2},{6,0},{8,14},{10,12},{12,10},{14,8},{1,7},{3,5},... | collective-permute-start | bytes 301064 | tf_op jit(solution)/shard_map/ppermute | solution.py:344
  12.6 14.8 %collective-permute-start.5 = (bf16[392,128]{1,0:T(8,128)(2,1)S(1)}, bf16[392,128]{1,0:T(8,128)(2,1)S(1)}, u32[]{:S(2)}, u32[]{:S(2)}) collective-permute-start(bf16[392,128]{1,0:T(8,128)(2,1)S(1)} %get-tuple-element.39), channel_id=1, source_target_pairs={{0,14},{2,12},{4,10},{6,8},{8,6},{10,4},{12,2},{14,0},{1,15},{3,13... | collective-permute-start | bytes 301064 | tf_op jit(solution)/shard_map/ppermute | solution.py:344
  13.7 13.7 %collective-permute-start.6 = (bf16[392,128]{1,0:T(8,128)(2,1)S(1)}, bf16[392,128]{1,0:T(8,128)(2,1)S(1)}, u32[]{:S(2)}, u32[]{:S(2)}) collective-permute-start(bf16[392,128]{1,0:T(8,128)(2,1)S(1)} %get-tuple-element.40), channel_id=1, source_target_pairs={{0,2},{2,0},{4,6},{6,4},{8,10},{10,8},{12,14},{14,12},{1,3},{3,1},... | collective-permute-start | bytes 301064 | tf_op jit(solution)/shard_map/ppermute | solution.py:344
  14.4 14.2 %collective-permute-start.7 = (bf16[392,128]{1,0:T(8,128)(2,1)S(1)}, bf16[392,128]{1,0:T(8,128)(2,1)S(1)}, u32[]{:S(2)}, u32[]{:S(2)}) collective-permute-start(bf16[392,128]{1,0:T(8,128)(2,1)S(1)} %get-tuple-element.41), channel_id=1, source_target_pairs={{0,12},{2,14},{4,8},{6,10},{8,4},{10,6},{12,0},{14,2},{1,13},{3,15... | collective-permute-start | bytes 301064 | tf_op jit(solution)/shard_map/ppermute | solution.py:344

commit v10 on v8

--- a/solution.py
+++ b/solution.py
@@ -13,7 +13,7 @@
 BMAX = 16
 MAXLEN = 96
 META = 8
-STEP = 512
+STEP = 1024
 GROUP = 8
 FRONT = 2
 ORDER = (4, 2, 5, 3, 7, 1, 6)

time: 30.4 us -> 30.2 us (level)
  the two profiles are of different devices: /device:TPU:21 before, /device:TPU:17 now
where the time goes in v10:
time: 30.2 us; the launch traced here: 30 us
  Pallas kernels  11.9 us (39%)
  starting transfers between devices  9.03 us (30%)
  waiting for transfers between devices  8.93 us (30%)
    ppermute x7, waiting for transfers between devices, per_device(): lax.ppermute(blocks[k], 'section', [(s, s ^ k) for s in range(sections)])  8.93 us
    ppermute x7, starting transfers between devices, per_device(): lax.ppermute(blocks[k], 'section', [(s, s ^ k) for s in range(sections)])  8.29 us
    pallas_call x1, Pallas kernels, project_send(): pl.pallas_call(project_send_kernel, out_shape=(jax.ShapeDtypeStruct((rows...  3.76 us
    pallas_call x3, Pallas kernels, attend_later(): pl.pallas_call(functools.partial(later_kernel, n_blocks=len(blocks), last...  3.66 us
    pallas_call x1, Pallas kernels, project_keep(): pl.pallas_call(functools.partial(project_keep_kernel, order=order), out_s...  2.68 us
    pallas_call x1, Pallas kernels, attend_first(): pl.pallas_call(first_kernel, out_shape=(tall, tall, jax.ShapeDtypeStruct(...  1.38 us
    ppermute x1, starting transfers between devices, per_device(): recv = lax.ppermute(send, 'tensor', [(0, 1), (1, 0)])  0.74 us
  transfers between devices with their start and end apart: 8, of which 4 were waited for; matrix products, arithmetic and copies ran while one was open for 0% of the time, Pallas kernels for 21%

profile of v10, /device:TPU:17, one launch (start us, length us, event | category | flops | bytes accessed | tf_op | source)
XLA Modules:
  0.0 30.0 jit_solution(11696250939425451392)
XLA Ops:
  0.0 0.0 copy-start.2
  0.0 3.8 %project_send.1 = (f32[256,640]{1,0:T(8,128)S(1)}, bf16[4,256,1024]{2,1,0:T(8,128)(2,1)S(1)}) custom-call(bf16[256,4096]{1,0:T(8,128)(2,1)} %tok_ref.1, bf16[32,128]{1,0:T(8,128)(2,1)} %bitcast.1, bf16[4096,1024]{1,0:T(8,128)(2,1)} %w_ref.3), custom_call_target="tpu_custom_call" | custom-call | flops 1073741824 | bytes 6815744 | tf_op jit(solution)/shard_map/project_send/pallas_call | solution.py:123
  3.8 0.7 %collective-permute-start = (f32[256,640]{1,0:T(8,128)S(1)}, f32[256,640]{1,0:T(8,128)S(1)}, u32[]{:S(2)}, u32[]{:S(2)}) collective-permute-start(f32[256,640]{1,0:T(8,128)S(1)} %get-tuple-element.26.send_ref), channel_id=1, source_target_pairs={{0,1},{1,0},{2,3},{3,2},{4,5},{5,4},{6,7},{7,6},{8,9},{9,8},{10,11... | collective-permute-start | bytes 1966088 | tf_op jit(solution)/shard_map/ppermute | solution.py:338
  4.5 0.0 copy-done.2
  4.5 0.0 copy-done.3
  4.5 2.7 %project_keep.1 = (f32[256,512]{1,0:T(8,128)S(1)}, bf16[768,256]{1,0:T(8,128)(2,1)S(1)}, f32[8,8,128]{2,1,0:T(8,128)S(1)}) custom-call(s32[1,8]{1,0:T(1,128)S(1)} %copy-done.2, s32[1,8]{1,0:T(1,128)S(1)} %copy-done.3, bf16[4,256,1024]{2,1,0:T(8,128)(2,1)S(1)} %get-tuple-element.24.scaled_ref, bf16[4096,1024]{1,0:T(8,128)(2,1)} %w_ref.3), custom_call_target="tpu_custom_call" | custom-call | flops 1073741824 | bytes 6815744 | tf_op jit(solution)/shard_map/project_keep/pallas_call | solution.py:151
  7.2 0.0 copy-start
  7.2 0.0 copy-start.1
  7.2 0.0 copy-start.4
  7.2 0.0 collective-permute-done.recv_ref
  7.3 0.5 %pack.1 = (bf16[392,128]{1,0:T(8,128)(2,1)S(1)}, bf16[392,128]{1,0:T(8,128)(2,1)S(1)}, bf16[392,128]{1,0:T(8,128)(2,1)S(1)}, bf16[392,128]{1,0:T(8,128)(2,1)S(1)...) custom-call(f32[256,512]{1,0:T(8,128)S(1)} %get-tuple-element.25.kee, ...), custom_call_target="tpu_custom_call" | custom-call | tf_op jit(solution)/shard_map/pack/pallas_call | solution.py:201
  7.7 0.1 collective-permute-start.1
  7.8 1.4 %collective-permute-start.2 = (bf16[392,128]{1,0:T(8,128)(2,1)S(1)}, bf16[392,128]{1,0:T(8,128)(2,1)S(1)}, u32[]{:S(2)}, u32[]{:S(2)}) collective-permute-start(bf16[392,128]{1,0:T(8,128)(2,1)S(1)} %get-tuple-element.36), channel_id=1, source_target_pairs={{0,4},{2,6},{4,0},{6,2},{8,12},{10,14},{12,8},{14,10},{1,5},{3,7},... | collective-permute-start | bytes 301064 | tf_op jit(solution)/shard_map/ppermute | solution.py:344
  9.2 3.2 %collective-permute-start.3 = (bf16[392,128]{1,0:T(8,128)(2,1)S(1)}, bf16[392,128]{1,0:T(8,128)(2,1)S(1)}, u32[]{:S(2)}, u32[]{:S(2)}) collective-permute-start(bf16[392,128]{1,0:T(8,128)(2,1)S(1)} %get-tuple-element.37), channel_id=1, source_target_pairs={{0,10},{2,8},{4,14},{6,12},{8,2},{10,0},{12,6},{14,4},{1,11},{3,9}... | collective-permute-start | bytes 301064 | tf_op jit(solution)/shard_map/ppermute | solution.py:344
  12.4 0.1 collective-permute-start.4
  12.5 1.1 %collective-permute-start.5 = (bf16[392,128]{1,0:T(8,128)(2,1)S(1)}, bf16[392,128]{1,0:T(8,128)(2,1)S(1)}, u32[]{:S(2)}, u32[]{:S(2)}) collective-permute-start(bf16[392,128]{1,0:T(8,128)(2,1)S(1)} %get-tuple-element.39), channel_id=1, source_target_pairs={{0,14},{2,12},{4,10},{6,8},{8,6},{10,4},{12,2},{14,0},{1,15},{3,13... | collective-permute-start | bytes 301064 | tf_op jit(solution)/shard_map/ppermute | solution.py:344
  13.7 0.0 collective-permute-done.1.refs_0_
  13.7 0.7 %collective-permute-start.6 = (bf16[392,128]{1,0:T(8,128)(2,1)S(1)}, bf16[392,128]{1,0:T(8,128)(2,1)S(1)}, u32[]{:S(2)}, u32[]{:S(2)}) collective-permute-start(bf16[392,128]{1,0:T(8,128)(2,1)S(1)} %get-tuple-element.40), channel_id=1, source_target_pairs={{0,2},{2,0},{4,6},{6,4},{8,10},{10,8},{12,14},{14,12},{1,3},{3,1},... | collective-permute-start | bytes 301064 | tf_op jit(solution)/shard_map/ppermute | solution.py:344
  14.4 0.0 collective-permute-done.2.refs_1_
  14.4 1.6 %collective-permute-start.7 = (bf16[392,128]{1,0:T(8,128)(2,1)S(1)}, bf16[392,128]{1,0:T(8,128)(2,1)S(1)}, u32[]{:S(2)}, u32[]{:S(2)}) collective-permute-start(bf16[392,128]{1,0:T(8,128)(2,1)S(1)} %get-tuple-element.41), channel_id=1, source_target_pairs={{0,12},{2,14},{4,8},{6,10},{8,4},{10,6},{12,0},{14,2},{1,13},{3,15... | collective-permute-start | bytes 301064 | tf_op jit(solution)/shard_map/ppermute | solution.py:344
  16.0 0.0 copy-done
  16.0 0.0 copy-done.1
  16.0 0.0 copy-done.4
  16.0 1.4 %attend_first.1 = (f32[16,96,128]{2,1,0:T(8,128)S(1)}, f32[16,96,128]{2,1,0:T(8,128)S(1)}, f32[2,96,128]{2,1,0:T(8,128)S(1)}, f32[8,128]{1,0:T(8,128)S(1)}, f32[16,96,128]{2,1,0:T(8,128)S(1)}) custom-call(bf16[80,2048]{1,0:T(8,128)(2,1)S(1)} %copy-done, bf16[80,512]{1,0:T(8,128)(2,1)S(1)} %copy-done.1, s32[1,8]{1,0:T(1,128)S(1)} %copy-done.4, ...), custom_call_target="tpu_custom_call" | custom-call | flops 16777216 | bytes 4194304 | tf_op jit(solution)/shard_map/attend_first/pallas_call | solution.py:287
  17.4 1.4 %collective-permute-done.3.refs_2_ = bf16[392,128]{1,0:T(8,128)(2,1)S(1)} collective-permute-done((bf16[392,128]{1,0:T(8,128)(2,1)S(1)}, bf16[392,128]{1,0:T(8,128)(2,1)S(1)}, u32[]{:S(2)}, u32[]{:S(2)}) %collective-permute-start.3) | collective-permute-done | bytes 100384 | tf_op jit(solution)/shard_map/ppermute | solution.py:344
  18.8 1.6 %collective-permute-done.4.refs_3_ = bf16[392,128]{1,0:T(8,128)(2,1)S(1)} collective-permute-done((bf16[392,128]{1,0:T(8,128)(2,1)S(1)}, bf16[392,128]{1,0:T(8,128)(2,1)S(1)}, u32[]{:S(2)}, u32[]{:S(2)}) %collective-permute-start.4) | collective-permute-done | bytes 100384 | tf_op jit(solution)/shard_map/ppermute | solution.py:344
  20.4 1.5 %attend_more.2.acc_in = f32[16,96,128]{2,1,0:T(8,128)S(1)} custom-call(f32[8,128]{1,0:T(8,128)S(1)} %get-tuple-element.30.table_ref, f32[16,96,128]{2,1,0:T(8,128)S(1)} %get-tuple-element.31.q_ref, f32[16,96,128]{2,1,0:T(8,128)S(1)} %get-tuple-element.32.score_ref, f32[2,96,128]{2,1,0:T(8,128)S(1)} %get-tuple-element.33.value_ref, ...), custom_call_target="tpu_custom_call", output_to_operand_aliasing={{}: (4, {})} | custom-call | flops 16777216 | bytes 4194304 | tf_op jit(solution)/shard_map/attend_more/pallas_call | solution.py:321
  21.8 5.5 %collective-permute-done.5.refs_0_ = bf16[392,128]{1,0:T(8,128)(2,1)S(1)} collective-permute-done((bf16[392,128]{1,0:T(8,128)(2,1)S(1)}, bf16[392,128]{1,0:T(8,128)(2,1)S(1)}, u32[]{:S(2)}, u32[]{:S(2)}) %collective-permute-start.5) | collective-permute-done | bytes 100384 | tf_op jit(solution)/shard_map/ppermute | solution.py:344
  27.4 0.0 collective-permute-done.6.refs_1_
  27.4 0.7 %attend_more.3.acc_in = f32[16,96,128]{2,1,0:T(8,128)S(1)} custom-call(f32[8,128]{1,0:T(8,128)S(1)} %get-tuple-element.30.table_ref, f32[16,96,128]{2,1,0:T(8,128)S(1)} %get-tuple-element.31.q_ref, f32[16,96,128]{2,1,0:T(8,128)S(1)} %get-tuple-element.32.score_ref, f32[2,96,128]{2,1,0:T(8,128)S(1)} %get-tuple-element.33.value_ref, ...), custom_call_target="tpu_custom_call", output_to_operand_aliasing={{}: (4, {})} | custom-call | flops 16777216 | bytes 4194304 | tf_op jit(solution)/shard_map/attend_more/pallas_call | solution.py:321
  28.1 0.4 %collective-permute-done.7.refs_0_ = bf16[392,128]{1,0:T(8,128)(2,1)S(1)} collective-permute-done((bf16[392,128]{1,0:T(8,128)(2,1)S(1)}, bf16[392,128]{1,0:T(8,128)(2,1)S(1)}, u32[]{:S(2)}, u32[]{:S(2)}) %collective-permute-start.7) | collective-permute-done | bytes 100384 | tf_op jit(solution)/shard_map/ppermute | solution.py:344
  28.6 1.5 %attend_last.1 = (f32[16,96,128]{2,1,0:T(8,128)S(1)}, bf16[80,2048]{1,0:T(8,128)(2,1)}) custom-call(f32[8,128]{1,0:T(8,128)S(1)} %get-tuple-element.30.table_ref, f32[16,96,128]{2,1,0:T(8,128)S(1)} %get-tuple-element.31.q_ref, f32[16,96,128]{2,1,0:T(8,128)S(1)} %get-tuple-element.32.score_ref, ...), custom_call_target="tpu_custom_call", output_to_operand_aliasing={{0}: (4, {})} | custom-call | flops 16777216 | bytes 4194304 | tf_op jit(solution)/shard_map/attend_last/pallas_call | solution.py:321
  (1 shorter events, 0.0 us)
Async XLA Ops:
  0.0 4.5 %copy-start.2 = (s32[1,8]{1,0:T(1,128)S(1)}, s32[1,8]{1,0:T(1,128)}, u32[]{:S(2)}) copy-start(s32[1,8]{1,0:T(1,128)} %len_hbm.1) | copy-start | bytes 100
  0.0 4.5 %copy-start.3 = (s32[1,8]{1,0:T(1,128)S(1)}, s32[1,8]{1,0:T(1,128)}, u32[]{:S(2)}) copy-start(s32[1,8]{1,0:T(1,128)} %host_hbm.1) | copy-start | bytes 100
  3.8 3.5 %collective-permute-start = (f32[256,640]{1,0:T(8,128)S(1)}, f32[256,640]{1,0:T(8,128)S(1)}, u32[]{:S(2)}, u32[]{:S(2)}) collective-permute-start(f32[256,640]{1,0:T(8,128)S(1)} %get-tuple-element.26.send_ref), channel_id=1, source_target_pairs={{0,1},{1,0},{2,3},{3,2},{4,5},{5,4},{6,7},{7,6},{8,9},{9,8},{10,11... | collective-permute-start | bytes 1966088 | tf_op jit(solution)/shard_map/ppermute | solution.py:338
  7.2 8.8 %copy-start = (bf16[80,2048]{1,0:T(8,128)(2,1)S(1)}, bf16[80,2048]{1,0:T(8,128)(2,1)}, u32[]{:S(2)}) copy-start(bf16[80,2048]{1,0:T(8,128)(2,1)} %query_ref.1) | copy-start | bytes 983044
  7.2 8.8 %copy-start.1 = (bf16[80,512]{1,0:T(8,128)(2,1)S(1)}, bf16[80,512]{1,0:T(8,128)(2,1)}, u32[]{:S(2)}) copy-start(bf16[80,512]{1,0:T(8,128)(2,1)} %own_ref.1) | copy-start | bytes 245764
  7.2 8.8 %copy-start.4 = (s32[1,8]{1,0:T(1,128)S(1)}, s32[1,8]{1,0:T(1,128)}, u32[]{:S(2)}) copy-start(s32[1,8]{1,0:T(1,128)} %count_ref.1) | copy-start | bytes 100
  7.7 5.9 %collective-permute-start.1 = (bf16[392,128]{1,0:T(8,128)(2,1)S(1)}, bf16[392,128]{1,0:T(8,128)(2,1)S(1)}, u32[]{:S(2)}, u32[]{:S(2)}) collective-permute-start(bf16[392,128]{1,0:T(8,128)(2,1)S(1)} %get-tuple-element.35), channel_id=1, source_target_pairs={{0,8},{2,10},{4,12},{6,14},{8,0},{10,2},{12,4},{14,6},{1,9},{3,11}... | collective-permute-start | bytes 301064 | tf_op jit(solution)/shard_map/ppermute | solution.py:344
  7.8 6.6 %collective-permute-start.2 = (bf16[392,128]{1,0:T(8,128)(2,1)S(1)}, bf16[392,128]{1,0:T(8,128)(2,1)S(1)}, u32[]{:S(2)}, u32[]{:S(2)}) collective-permute-start(bf16[392,128]{1,0:T(8,128)(2,1)S(1)} %get-tuple-element.36), channel_id=1, source_target_pairs={{0,4},{2,6},{4,0},{6,2},{8,12},{10,14},{12,8},{14,10},{1,5},{3,7},... | collective-permute-start | bytes 301064 | tf_op jit(solution)/shard_map/ppermute | solution.py:344
  9.2 9.7 %collective-permute-start.3 = (bf16[392,128]{1,0:T(8,128)(2,1)S(1)}, bf16[392,128]{1,0:T(8,128)(2,1)S(1)}, u32[]{:S(2)}, u32[]{:S(2)}) collective-permute-start(bf16[392,128]{1,0:T(8,128)(2,1)S(1)} %get-tuple-element.37), channel_id=1, source_target_pairs={{0,10},{2,8},{4,14},{6,12},{8,2},{10,0},{12,6},{14,4},{1,11},{3,9}... | collective-permute-start | bytes 301064 | tf_op jit(solution)/shard_map/ppermute | solution.py:344
  12.4 8.0 %collective-permute-start.4 = (bf16[392,128]{1,0:T(8,128)(2,1)S(1)}, bf16[392,128]{1,0:T(8,128)(2,1)S(1)}, u32[]{:S(2)}, u32[]{:S(2)}) collective-permute-start(bf16[392,128]{1,0:T(8,128)(2,1)S(1)} %get-tuple-element.38), channel_id=1, source_target_pairs={{0,6},{2,4},{4,2},{6,0},{8,14},{10,12},{12,10},{14,8},{1,7},{3,5},... | collective-permute-start | bytes 301064 | tf_op jit(solution)/shard_map/ppermute | solution.py:344
  12.5 14.8 %collective-permute-start.5 = (bf16[392,128]{1,0:T(8,128)(2,1)S(1)}, bf16[392,128]{1,0:T(8,128)(2,1)S(1)}, u32[]{:S(2)}, u32[]{:S(2)}) collective-permute-start(bf16[392,128]{1,0:T(8,128)(2,1)S(1)} %get-tuple-element.39), channel_id=1, source_target_pairs={{0,14},{2,12},{4,10},{6,8},{8,6},{10,4},{12,2},{14,0},{1,15},{3,13... | collective-permute-start | bytes 301064 | tf_op jit(solution)/shard_map/ppermute | solution.py:344
  13.7 13.7 %collective-permute-start.6 = (bf16[392,128]{1,0:T(8,128)(2,1)S(1)}, bf16[392,128]{1,0:T(8,128)(2,1)S(1)}, u32[]{:S(2)}, u32[]{:S(2)}) collective-permute-start(bf16[392,128]{1,0:T(8,128)(2,1)S(1)} %get-tuple-element.40), channel_id=1, source_target_pairs={{0,2},{2,0},{4,6},{6,4},{8,10},{10,8},{12,14},{14,12},{1,3},{3,1},... | collective-permute-start | bytes 301064 | tf_op jit(solution)/shard_map/ppermute | solution.py:344
  14.4 14.2 %collective-permute-start.7 = (bf16[392,128]{1,0:T(8,128)(2,1)S(1)}, bf16[392,128]{1,0:T(8,128)(2,1)S(1)}, u32[]{:S(2)}, u32[]{:S(2)}) collective-permute-start(bf16[392,128]{1,0:T(8,128)(2,1)S(1)} %get-tuple-element.41), channel_id=1, source_target_pairs={{0,12},{2,14},{4,8},{6,10},{8,4},{10,6},{12,0},{14,2},{1,13},{3,15... | collective-permute-start | bytes 301064 | tf_op jit(solution)/shard_map/ppermute | solution.py:344
